TPU v7x, 32 devices: a whole 2x2x4 slice. The times are simulated.
32 devices in a mesh: fsdp: 8 (over y, x, core), rep: 4 (over z).
Axes of the slice: x: 2, y: 2, z: 4, core: 2. Of those that a mesh axis runs over, the one named last changes fastest.
Arguments:
- student_hidden: bfloat16 [6144, 3072], P(('fsdp', 'rep')), may hold values from -6 to 6
- out_cotangent: bfloat16 [6144, 768], P(('fsdp', 'rep')), may hold values from -0.078125 to 0.078125
- student_branch: bfloat16 [6144, 768], P(('fsdp', 'rep')), may hold values from -6 to 6
- layer_scale: float32 [768], replicated, may hold values from 0.1 to 1
- scale_first: float32 [768], replicated, may hold values from -1.75 to 1.75
- scale_second: float32 [768], replicated, may hold values from 0.05 to 1
- student_weight: bfloat16 [3072, 768], P(('fsdp', 'rep')), may hold values from -0.109375 to 0.109375
- first_moment: bfloat16 [3072, 768], P(('fsdp', 'rep')), may hold values from -0.1875 to 0.1875
- second_moment: bfloat16 [3072, 768], P(('fsdp', 'rep')), may hold values from 0.0019989014 to 0.049804688
- teacher_weight: bfloat16 [3072, 768], P('fsdp'), may hold values from -0.109375 to 0.109375
- teacher_scale: float32 [768], replicated, may hold values from 0.1 to 1
- teacher_hidden: bfloat16 [8192, 3072], P(('fsdp', 'rep')), may hold values from -6 to 6
- teacher_input: bfloat16 [8192, 768], P(('fsdp', 'rep')), may hold values from -6 to 6
Outputs:
- new_weight: bfloat16 [3072, 768], P(('fsdp', 'rep'))
- new_first: bfloat16 [3072, 768], P(('fsdp', 'rep'))
- new_second: bfloat16 [3072, 768], P(('fsdp', 'rep'))
- new_teacher: bfloat16 [3072, 768], P('fsdp')
- new_scale: float32 [768], replicated
- new_scale_first: float32 [768], replicated
- new_scale_second: float32 [768], replicated
- new_teacher_scale: float32 [768], replicated
- teacher_out: bfloat16 [8192, 768], P(('fsdp', 'rep'))
All inputs are finite; a program needn't handle non-finite values.
Results may differ from a plain program's by a relative error of at most 0.0048.
Values may be sent and summed in bfloat16 or wider, within the bound.
No kernel may reach another device: no remote copies, remote signals or barrier semaphores. Data moves between devices by JAX's collectives and lax.ppermute only.
A program may use at most 64 MiB of HBM per device.

v0:
```python
import jax
import jax.numpy as jnp
from jax import lax
from jax.sharding import PartitionSpec as P

beta_one = 0.9
beta_two = 0.95
learn_rate = 0.02
epsilon = 1e-08
teacher_keep = 0.75


def adam_step(values, moment_one, moment_two, gradient):
    first_new = beta_one * moment_one.astype(jnp.float32) + (1.0 - beta_one) * gradient
    second_new = beta_two * moment_two.astype(jnp.float32) + (1.0 - beta_two) * gradient * gradient
    values_new = values.astype(jnp.float32) - learn_rate * first_new / (
        jnp.sqrt(second_new) + epsilon
    )
    return (values_new, first_new, second_new)


def token_fold(arrived, portion):
    return lax.dot_general(
        arrived, portion, (((0,), (0,)), ((), ())), preferred_element_type=jnp.float32
    )


def shards(
    student_hidden,
    out_cotangent,
    student_branch,
    layer_scale,
    scale_first,
    scale_second,
    student_weight,
    first_moment,
    second_moment,
    teacher_weight,
    teacher_scale,
    teacher_hidden,
    teacher_input,
):
    fsdp_count = lax.axis_size("fsdp")
    rep_count = lax.axis_size("rep")
    tok_rows = student_hidden.shape[0]
    model_width = out_cotangent.shape[1]
    own_rows = student_weight.shape[0]
    cotangent = out_cotangent.astype(jnp.float32)
    scaled = (cotangent * layer_scale).astype(jnp.bfloat16)
    scale_grad = lax.psum(
        jnp.sum(cotangent * student_branch.astype(jnp.float32), axis=0), ("fsdp", "rep")
    )
    blocks = student_hidden.reshape(tok_rows, fsdp_count, rep_count * own_rows)
    blocks = blocks.transpose(1, 0, 2)
    arrived = lax.all_to_all(blocks, "fsdp", split_axis=0, concat_axis=0, tiled=True)
    arrived = arrived.reshape(fsdp_count * tok_rows, rep_count * own_rows)
    partial_term = token_fold(arrived, lax.all_gather(scaled, "fsdp", axis=0, tiled=True))
    gradient = lax.psum_scatter(
        partial_term.reshape(rep_count, own_rows, model_width),
        "rep",
        scatter_dimension=0,
        tiled=True,
    )
    gradient = gradient.reshape(own_rows, model_width)
    weight_new, first_new, second_new = adam_step(
        student_weight, first_moment, second_moment, gradient
    )
    scale_new, scale_first_new, scale_second_new = adam_step(
        layer_scale, scale_first, scale_second, scale_grad
    )
    rep_index = lax.axis_index("rep")
    teacher_own = lax.dynamic_slice_in_dim(teacher_weight, rep_index * own_rows, own_rows, 0)
    teacher_rows = (
        teacher_keep * teacher_own.astype(jnp.float32) + (1.0 - teacher_keep) * weight_new
    ).astype(jnp.bfloat16)
    teacher_scale_new = teacher_keep * teacher_scale + (1.0 - teacher_keep) * scale_new
    teacher_shard = lax.all_gather(teacher_rows, "rep", axis=0, tiled=True)
    projected = jnp.dot(
        teacher_hidden,
        lax.all_gather(teacher_shard, "fsdp", axis=0, tiled=True),
        preferred_element_type=jnp.float32,
    )
    teacher_out = (teacher_input.astype(jnp.float32) + teacher_scale_new * projected).astype(
        jnp.bfloat16
    )
    return (
        weight_new.astype(jnp.bfloat16),
        first_new.astype(jnp.bfloat16),
        second_new.astype(jnp.bfloat16),
        teacher_shard,
        scale_new,
        scale_first_new,
        scale_second_new,
        teacher_scale_new,
        teacher_out,
    )


def solution(mesh):
    in_specs = (
        P(("fsdp", "rep"), None),
        P(("fsdp", "rep"), None),
        P(("fsdp", "rep"), None),
        P(),
        P(),
        P(),
        P(("fsdp", "rep"), None),
        P(("fsdp", "rep"), None),
        P(("fsdp", "rep"), None),
        P("fsdp", None),
        P(),
        P(("fsdp", "rep"), None),
        P(("fsdp", "rep"), None),
    )
    out_specs = (
        P(("fsdp", "rep"), None),
        P(("fsdp", "rep"), None),
        P(("fsdp", "rep"), None),
        P("fsdp", None),
        P(),
        P(),
        P(),
        P(),
        P(("fsdp", "rep"), None),
    )
    return jax.shard_map(shards, mesh=mesh, in_specs=in_specs, out_specs=out_specs, check_vma=False)
```

profile of v0, /device:TPU:0, one launch (start us, length us, event | category | flops | bytes accessed | tf_op | source)
XLA Modules:
  0.0 152.8 jit_solution(17210031080352242552)
XLA Ops:
  7.2 0.0 copy-start
  7.2 0.0 copy-start.2
  7.2 0.0 all-gather.3.cloned.1.call-start
  7.2 2.0 %fusion.4 = (f32[768]{0:T(1024)S(1)}, bf16[192,768]{1,0:T(8,128)(2,1)}) fusion(bf16[192,768]{1,0:T(8,128)(2,1)} %param.14, bf16[192,768]{1,0:T(8,128)(2,1)} %param.15, f32[768]{0:T(1024)} %param.16), kind=kLoop, calls=%fused_computation.7 | loop fusion | flops 883968 | bytes 890880 | tf_op jit(solution)/shard_map/reduce_sum | solution.py:51
  9.3 0.0 all-gather.3.cloned.1.call-update
  9.3 0.0 reduce-scatter.2.cloned.1.call-start
  9.3 0.0 copy-done.2
  9.4 0.2 copy.32
  9.6 0.2 copy.29
  9.7 24.9 %all_to_all.5 = bf16[8,192,384]{2,1,0:T(8,128)(2,1)S(1)} all-to-all(bf16[8,192,384]{2,1,0:T(8,128)(2,1)S(1)} %copy.29), channel_id=1, replica_groups=mesh['fsdp'=8,'rep'=4] {'fsdp'}, dimensions={0} | all-to-all | bytes 2359296 | tf_op jit(solution)/shard_map/all_to_all | solution.py:55
  34.6 14.2 %all-gather.3.cloned.1.call-done = bf16[1536,768]{1,0:T(8,128)(2,1)} async-done(((bf16[192,768]{1,0:T(8,128)(2,1)}), bf16[1536,768]{1,0:T(8,128)(2,1)}) %all-gather.3.cloned.1.call-update) | async-done | bytes 2359312 | tf_op jit(solution)/shard_map/all_gather | solution.py:57
  48.8 0.0 copy-start.4
  48.8 0.0 copy-start.5
  48.8 0.0 copy-start.6
  48.8 3.9 %fusion.11 = f32[768,384]{0,1:T(8,128)} fusion(bf16[1536,768]{1,0:T(8,128)(2,1)} %all-gather.3.cloned.1.call-done, bf16[1536,384]{1,0:T(8,128)(2,1)S(1)} %bitcast.35), kind=kOutput, calls=%fused_computation.21 | convolution fusion | flops 905969664 | bytes 4718592 | tf_op jit(solution)/shard_map/dot_general | solution.py:23
  52.7 0.0 reduce-scatter.2.cloned.1.call-update
  52.7 0.0 copy-start.3
  52.7 0.0 all-gather.5.cloned.1.call-start
  52.8 0.0 copy-start.7
  52.8 0.0 copy-start.8
  52.8 0.0 copy-start.9
  52.8 0.0 copy-start.10
  52.8 29.2 %reduce-scatter.2.cloned.1.call-done = f32[1,96,768]{2,1,0:T(8,128)} async-done(((f32[4,96,768]{2,1,0:T(8,128)}), f32[1,96,768]{2,1,0:T(8,128)}) %reduce-scatter.2.cloned.1.call-update) | async-done | bytes 294928 | tf_op jit(solution)/shard_map/reduce_scatter | solution.py:58
  82.0 0.0 copy-done.4
  82.0 0.0 copy-done.5
  82.0 0.0 copy-done.6
  82.0 2.0 %add_convert_fusion = (bf16[96,768]{1,0:T(8,128)(2,1)S(1)}, bf16[96,768]{1,0:T(8,128)(2,1)}, bf16[96,768]{1,0:T(8,128)(2,1)}, bf16[96,768]{1,0:T(8,128)(2,1)}) fusion(bf16[384,768]{1,0:T(8,128)(2,1)} %param.22, s32[]{:T(128)S(6)} %select_n.3, bf16[96,768]{1,0:T(8,128)(2,1)S(1)} %copy-done.4, f32[1,96,768]{2,1,0:T(8,128)} %reduce-scatter.2.cloned.1.call-done, ...), kind=kLoop, calls=%fused_computation.12 | loop fusion | flops 1622016 | bytes 1474564 | tf_op jit(solution)/shard_map/convert_element_type | solution.py:75
  84.0 17.1 %all_gather.10 = bf16[384,768]{1,0:T(8,128)(2,1)} all-gather(bf16[96,768]{1,0:T(8,128)(2,1)S(1)} %get-tuple-element.49), channel_id=1, replica_groups=mesh['fsdp'=8,'rep'=4] {'rep'}, dimensions={0}, use_global_device_ids=true | all-gather | bytes 737280 | tf_op jit(solution)/shard_map/all_gather | solution.py:77
  101.1 0.0 all-gather.5.cloned.1.call-update
  101.1 0.0 copy-done.3
  101.1 0.2 copy.30
  101.3 38.8 %psum.7 = f32[768]{0:T(1024)S(1)} all-reduce(f32[768]{0:T(1024)S(1)} %get-tuple-element.53), channel_id=1, replica_groups=mesh['fsdp'=8,'rep'=4] {'fsdp','rep'}, use_global_device_ids=true, to_apply=%region_2.0 | all-reduce | flops 768 | bytes 6144 | tf_op jit(solution)/shard_map/psum | solution.py:50
  140.1 0.0 copy-done.7
  140.1 0.0 copy-done.8
  140.1 0.0 copy-done.9
  140.1 0.0 copy-done.10
  140.1 0.6 multiply_add_fusion
  140.7 0.0 copy-start.11
  140.7 0.0 all-gather.5.cloned.1.call-done
  140.7 0.0 copy-done
  140.7 0.0 copy-start.1
  140.7 3.8 %fusion.2 = bf16[256,768]{0,1:T(8,128)(2,1)S(1)} fusion(bf16[3072,768]{1,0:T(8,128)(2,1)} %all-gather.5.cloned.1.call-done, bf16[256,3072]{1,0:T(8,128)(2,1)S(1)} %copy-done, bf16[256,768]{0,1:T(8,128)(2,1)S(1)} %copy.30, f32[768]{0:T(1024)S(1)} %get-tuple-element.75), kind=kOutput, calls=%fused_computation.3 | convolution fusion | flops 1208745984 | bytes 7080960 | tf_op jit(solution)/shard_map/dot_general | solution.py:78
  144.6 0.0 copy-done.11
  144.6 0.9 copy.31
  145.5 0.0 copy-done.1
  145.5 0.8 copy.34
Async XLA Ops:
  7.2 133.5 %copy-start = (bf16[256,3072]{1,0:T(8,128)(2,1)S(1)}, bf16[256,3072]{1,0:T(8,128)(2,1)}, u32[]{:S(2)}) copy-start(bf16[256,3072]{1,0:T(8,128)(2,1)} %param.24) | copy-start | bytes 4718596
  7.2 2.2 %copy-start.2 = (bf16[192,3072]{1,0:T(8,128)(2,1)S(1)}, bf16[192,3072]{1,0:T(8,128)(2,1)}, u32[]{:S(2)}) copy-start(bf16[192,3072]{1,0:T(8,128)(2,1)} %param.13) | copy-start | bytes 3538948
  7.2 41.6 %all-gather.3.cloned.1.call-start = ((), (), s32[]{:S(2)}) async-start(), calls=%async_computation.2 | async-start | bytes 2654208 | tf_op jit(solution)/shard_map/all_gather | solution.py:57
  9.3 72.7 %reduce-scatter.2.cloned.1.call-start = ((), (), s32[]{:S(2)}) async-start(), calls=%async_computation.3 | async-start | bytes 1474560 | tf_op jit(solution)/shard_map/reduce_scatter | solution.py:58
  48.8 33.2 %copy-start.4 = (bf16[96,768]{1,0:T(8,128)(2,1)S(1)}, bf16[96,768]{1,0:T(8,128)(2,1)}, u32[]{:S(2)}) copy-start(bf16[96,768]{1,0:T(8,128)(2,1)} %param.21) | copy-start | bytes 442372
  48.8 33.2 %copy-start.5 = (bf16[96,768]{1,0:T(8,128)(2,1)S(1)}, bf16[96,768]{1,0:T(8,128)(2,1)}, u32[]{:S(2)}) copy-start(bf16[96,768]{1,0:T(8,128)(2,1)} %param.20) | copy-start | bytes 442372
  48.8 33.2 %copy-start.6 = (bf16[96,768]{1,0:T(8,128)(2,1)S(1)}, bf16[96,768]{1,0:T(8,128)(2,1)}, u32[]{:S(2)}) copy-start(bf16[96,768]{1,0:T(8,128)(2,1)} %param.19) | copy-start | bytes 442372
  52.7 48.4 %copy-start.3 = (bf16[256,768]{1,0:T(8,128)(2,1)S(1)}, bf16[256,768]{1,0:T(8,128)(2,1)}, u32[]{:S(2)}) copy-start(bf16[256,768]{1,0:T(8,128)(2,1)} %param.25) | copy-start | bytes 1179652
  52.7 88.0 %all-gather.5.cloned.1.call-start = ((), (), s32[]{:S(2)}) async-start(), calls=%async_computation.4 | async-start | bytes 5308416 | tf_op jit(solution)/shard_map/all_gather | solution.py:80
  52.8 87.3 %copy-start.7 = (f32[768]{0:T(1024)S(1)}, f32[768]{0:T(1024)}, u32[]{:S(2)}) copy-start(f32[768]{0:T(1024)} %param.16) | copy-start | bytes 9220
  52.8 87.3 %copy-start.8 = (f32[768]{0:T(1024)S(1)}, f32[768]{0:T(1024)}, u32[]{:S(2)}) copy-start(f32[768]{0:T(1024)} %param.23) | copy-start | bytes 9220
  52.8 87.3 %copy-start.9 = (f32[768]{0:T(1024)S(1)}, f32[768]{0:T(1024)}, u32[]{:S(2)}) copy-start(f32[768]{0:T(1024)} %param.17) | copy-start | bytes 9220
  52.8 87.3 %copy-start.10 = (f32[768]{0:T(1024)S(1)}, f32[768]{0:T(1024)}, u32[]{:S(2)}) copy-start(f32[768]{0:T(1024)} %param.18) | copy-start | bytes 9220
  140.7 3.9 %copy-start.11 = (f32[768]{0:T(1024)}, f32[768]{0:T(1024)S(1)}, u32[]{:S(2)}) copy-start(f32[768]{0:T(1024)S(1)} %get-tuple-element.75) | copy-start | bytes 9220
  140.7 4.8 %copy-start.1 = (bf16[384,768]{1,0:T(8,128)(2,1)S(1)}, bf16[384,768]{1,0:T(8,128)(2,1)}, u32[]{:S(2)}) copy-start(bf16[384,768]{1,0:T(8,128)(2,1)} %all_gather.10) | copy-start | bytes 1769476
Sparse Core Ops, SparseCore 0:
  10.5 38.2 all-gather.2
  52.8 29.1 reduce-scatter.1
  101.3 37.6 all-gather.4
where the time goes:
time: 153 us
  blocking collectives  80.7 us (53%)
  waiting for transfers between devices  43.4 us (28%)
  between operations  13.9 us (9%)
  matrix products  7.7 us (5%)
  other arithmetic  4.65 us (3%)
  local copies, waits for them, and re-layouts  2.34 us (2%)
    psum x1, blocking collectives, shards(): lax.psum(jnp.sum(cotangent * student_branch.astype(jnp.float32), axis=0),...  38.8 us
    reduce_scatter x1, waiting for transfers between devices, shards(): lax.psum_scatter(partial_term.reshape(rep_count, own_rows, model_width),...  29.2 us
    all_to_all x1, blocking collectives, shards(): lax.all_to_all(blocks, 'fsdp', split_axis=0, concat_axis=0, tiled=True)  24.9 us
    all_gather x1, blocking collectives, shards(): teacher_shard = lax.all_gather(teacher_rows, 'rep', axis=0, tiled=True)  17.1 us
    all_gather x1, waiting for transfers between devices, shards(): lax.all_gather(scaled, 'fsdp', axis=0, tiled=True)  14.2 us
    dot_general x1, matrix products, token_fold(): lax.dot_general(arrived, portion, (((0,), (0,)), ((), ())), preferred_ele...  3.87 us
    dot_general x1, matrix products, shards(): jnp.dot(teacher_hidden, lax.all_gather(teacher_shard, 'fsdp', axis=0, til...  3.83 us
  transfers between devices with their start and end apart: 3, of which 2 were waited for; matrix products, arithmetic and copies ran while one was open for 1% of the time, Pallas kernels for 0%

commit v1 on v0

--- a/solution.py
+++ b/solution.py
@@ -8,6 +8,8 @@
 learn_rate = 0.02
 epsilon = 1e-08
 teacher_keep = 0.75
+
+BOTH = ("fsdp", "rep")
 
 
 def adam_step(values, moment_one, moment_two, gradient):
@@ -23,6 +25,39 @@
     return lax.dot_general(
         arrived, portion, (((0,), (0,)), ((), ())), preferred_element_type=jnp.float32
     )
+
+
+def swap_fsdp(value, flip):
+    count = lax.axis_size("fsdp")
+    return lax.ppermute(value, "fsdp", [(i, i ^ flip) for i in range(count)])
+
+
+def swap_rep(value, flip):
+    count = lax.axis_size("rep")
+    return lax.ppermute(value, "rep", [(i, i ^ flip) for i in range(count)])
+
+
+def gather_chips(value, chips):
+    rows = value.shape[0]
+    if chips == 4 and rows % 32 == 0:
+        along_x = swap_fsdp(value, 2)
+        along_y = swap_fsdp(value, 4)
+        half = rows // 2
+        corner = [swap_fsdp(along_x[:half], 4), swap_fsdp(along_y[half:], 2)]
+        return [[value], [along_x], [along_y], corner]
+    return [[value]] + [[swap_fsdp(value, 2 * j)] for j in range(1, chips)]
+
+
+def all_sum(value):
+    flip = 1
+    while flip < lax.axis_size("rep"):
+        value = value + swap_rep(value, flip)
+        flip *= 2
+    flip = 1
+    while flip < lax.axis_size("fsdp"):
+        value = value + swap_fsdp(value, flip)
+        flip *= 2
+    return value
 
 
 def shards(
@@ -42,44 +77,61 @@
 ):
     fsdp_count = lax.axis_size("fsdp")
     rep_count = lax.axis_size("rep")
-    tok_rows = student_hidden.shape[0]
-    model_width = out_cotangent.shape[1]
+    chips = fsdp_count // 2
     own_rows = student_weight.shape[0]
+    width = rep_count * own_rows
+    me = lax.axis_index("fsdp")
+    my_rep = lax.axis_index("rep")
+
+    def columns(array, flip):
+        return lax.dynamic_slice_in_dim(array, (me ^ flip) * width, width, 1)
+
     cotangent = out_cotangent.astype(jnp.float32)
+    scale_grad = all_sum(jnp.sum(cotangent * student_branch.astype(jnp.float32), axis=0))
+    scale_new, scale_first_new, scale_second_new = adam_step(
+        layer_scale, scale_first, scale_second, scale_grad
+    )
+    teacher_scale_new = teacher_keep * teacher_scale + (1.0 - teacher_keep) * scale_new
+
     scaled = (cotangent * layer_scale).astype(jnp.bfloat16)
-    scale_grad = lax.psum(
-        jnp.sum(cotangent * student_branch.astype(jnp.float32), axis=0), ("fsdp", "rep")
-    )
-    blocks = student_hidden.reshape(tok_rows, fsdp_count, rep_count * own_rows)
-    blocks = blocks.transpose(1, 0, 2)
-    arrived = lax.all_to_all(blocks, "fsdp", split_axis=0, concat_axis=0, tiled=True)
-    arrived = arrived.reshape(fsdp_count * tok_rows, rep_count * own_rows)
-    partial_term = token_fold(arrived, lax.all_gather(scaled, "fsdp", axis=0, tiled=True))
-    gradient = lax.psum_scatter(
-        partial_term.reshape(rep_count, own_rows, model_width),
-        "rep",
-        scatter_dimension=0,
-        tiled=True,
-    )
-    gradient = gradient.reshape(own_rows, model_width)
+    scaled_of = [jnp.concatenate(b, 0) if len(b) > 1 else b[0] for b in gather_chips(scaled, chips)]
+    partial_term = None
+    for j in range(chips):
+        sent = jnp.concatenate([columns(student_hidden, 2 * j), columns(student_hidden, 2 * j + 1)], 1)
+        arrived = swap_fsdp(sent, 2 * j) if j else sent
+        term = token_fold(arrived, scaled_of[j])
+        partial_term = term if partial_term is None else partial_term + term
+    pair = partial_term[:width] + swap_fsdp(partial_term[width:], 1)
+
+    def rows_of(array, flip):
+        return lax.dynamic_slice_in_dim(array, (my_rep ^ flip) * own_rows, own_rows, 0)
+
+    gradient = rows_of(pair, 0)
+    for j in range(1, rep_count):
+        gradient = gradient + swap_rep(rows_of(pair, j).astype(jnp.bfloat16), j).astype(jnp.float32)
     weight_new, first_new, second_new = adam_step(
         student_weight, first_moment, second_moment, gradient
     )
-    scale_new, scale_first_new, scale_second_new = adam_step(
-        layer_scale, scale_first, scale_second, scale_grad
-    )
-    rep_index = lax.axis_index("rep")
-    teacher_own = lax.dynamic_slice_in_dim(teacher_weight, rep_index * own_rows, own_rows, 0)
     teacher_rows = (
-        teacher_keep * teacher_own.astype(jnp.float32) + (1.0 - teacher_keep) * weight_new
+        teacher_keep * rows_of(teacher_weight, 0).astype(jnp.float32)
+        + (1.0 - teacher_keep) * weight_new
     ).astype(jnp.bfloat16)
-    teacher_scale_new = teacher_keep * teacher_scale + (1.0 - teacher_keep) * scale_new
-    teacher_shard = lax.all_gather(teacher_rows, "rep", axis=0, tiled=True)
-    projected = jnp.dot(
-        teacher_hidden,
-        lax.all_gather(teacher_shard, "fsdp", axis=0, tiled=True),
-        preferred_element_type=jnp.float32,
-    )
+    teacher_shard = jnp.zeros((width,) + teacher_rows.shape[1:], jnp.bfloat16)
+    for j in range(rep_count):
+        piece = swap_rep(teacher_rows, j) if j else teacher_rows
+        teacher_shard = lax.dynamic_update_slice_in_dim(
+            teacher_shard, piece, (my_rep ^ j) * own_rows, 0
+        )
+    projected = None
+    for j, blocks in enumerate(gather_chips(teacher_shard, chips)):
+        low, high = columns(teacher_hidden, 2 * j), columns(teacher_hidden, 2 * j + 1)
+        start = 0
+        for block in blocks:
+            stop = start + block.shape[0]
+            for hidden, weights in ((low, block), (high, swap_fsdp(block, 1))):
+                term = jnp.dot(hidden[:, start:stop], weights, preferred_element_type=jnp.float32)
+                projected = term if projected is None else projected + term
+            start = stop
     teacher_out = (teacher_input.astype(jnp.float32) + teacher_scale_new * projected).astype(
         jnp.bfloat16
     )

time: 153 us -> 105 us (0.69)
  blocking collectives: 80.7 us -> 0 us
  starting transfers between devices: 0.12 us -> 33.2 us
  between operations: 13.9 us -> 1 us
  waiting for transfers between devices: 43.4 us -> 50.7 us
  other arithmetic: 4.65 us -> 7.89 us
  local copies, waits for them, and re-layouts: 2.34 us -> 5.14 us
    ppermute x0 -> x28, waiting for transfers between devices: none -> 50.7 us  [the longest x20 26.3 us: swap_fsdp(): return lax.ppermute(value, 'fsdp', [(i, i ^ flip) for i in range(count)])]
    psum x1 -> x0, blocking collectives: 38.8 us -> none  [shards(): lax.psum(jnp.sum(cotangent * student_branch.astype(jnp.float32), axis=0),...]
    ppermute x0 -> x28, starting transfers between devices: none -> 33.2 us  [the longest x20 19.4 us: swap_fsdp(): return lax.ppermute(value, 'fsdp', [(i, i ^ flip) for i in range(count)])]
    reduce_scatter x1 -> x0, waiting for transfers between devices: 29.2 us -> none  [shards(): lax.psum_scatter(partial_term.reshape(rep_count, own_rows, model_width),...]
    all_to_all x1 -> x0, blocking collectives: 24.9 us -> none  [shards(): lax.all_to_all(blocks, 'fsdp', split_axis=0, concat_axis=0, tiled=True)]
    all_gather x1 -> x0, blocking collectives: 17.1 us -> none  [shards(): teacher_shard = lax.all_gather(teacher_rows, 'rep', axis=0, tiled=True)]
    all_gather x2 -> x0, waiting for transfers between devices: 14.2 us -> none  [the longest x1 14.2 us: shards(): lax.all_gather(scaled, 'fsdp', axis=0, tiled=True)]
    dynamic_update_slice x0 -> x1, other arithmetic: none -> 2.32 us  [shards(): lax.dynamic_update_slice_in_dim(teacher_shard, piece, (my_rep ^ j) * own_...]
  transfers between devices with their start and end apart: 3 -> 28, of which waited for: 2 -> 18; matrix products, arithmetic and copies ran while one was open for 1% -> 8% of each run, Pallas kernels for 0% -> 0%
where the time goes in v1:
time: 105 us; the launch traced here: 104 us
  waiting for transfers between devices  50.7 us (48%)
  starting transfers between devices  33.2 us (32%)
  other arithmetic  7.89 us (8%)
  matrix products  6.36 us (6%)
  local copies, waits for them, and re-layouts  5.14 us (5%)
    ppermute x20, waiting for transfers between devices, swap_fsdp(): return lax.ppermute(value, 'fsdp', [(i, i ^ flip) for i in range(count)])  26.3 us
    ppermute x8, waiting for transfers between devices, swap_rep(): return lax.ppermute(value, 'rep', [(i, i ^ flip) for i in range(count)])  24.4 us
    ppermute x20, starting transfers between devices, swap_fsdp(): return lax.ppermute(value, 'fsdp', [(i, i ^ flip) for i in range(count)])  19.4 us
    ppermute x8, starting transfers between devices, swap_rep(): return lax.ppermute(value, 'rep', [(i, i ^ flip) for i in range(count)])  13.8 us
    dot_general x10, matrix products, shards(): jnp.dot(hidden[:, start:stop], weights, preferred_element_type=jnp.float32)  4.26 us
    unnamed x24, local copies, waits for them, and re-layouts  2.73 us
    dynamic_update_slice x1, other arithmetic, shards(): lax.dynamic_update_slice_in_dim(teacher_shard, piece, (my_rep ^ j) * own_...  2.32 us
  transfers between devices with their start and end apart: 28, of which 18 were waited for; matrix products, arithmetic and copies ran while one was open for 8% of the time, Pallas kernels for 0%

profile of v1, /device:TPU:0, one launch (start us, length us, event | category | flops | bytes accessed | tf_op | source)
XLA Modules:
  0.0 104.3 jit_solution(13752242109081489123)
XLA Ops:
  0.7 1.3 %fusion.10 = (f32[768]{0:T(1024)S(1)}, bf16[192,768]{1,0:T(8,128)(2,1)S(1)}) fusion(bf16[192,768]{1,0:T(8,128)(2,1)} %param.14, bf16[192,768]{1,0:T(8,128)(2,1)} %param.15, f32[768]{0:T(1024)} %param.16), kind=kLoop, calls=%fused_computation.17 | loop fusion | flops 883968 | bytes 890880 | tf_op jit(solution)/shard_map/reduce_sum | solution.py:90
  1.9 3.0 %collective-permute-start.1 = (bf16[192,768]{1,0:T(8,128)(2,1)S(1)}, bf16[192,768]{1,0:T(8,128)(2,1)S(1)}, u32[]{:S(2)}, u32[]{:S(2)}) collective-permute-start(bf16[192,768]{1,0:T(8,128)(2,1)S(1)} %get-tuple-element.29), channel_id=1, source_target_pairs={{0,8},{4,12},{8,0},{12,4},{16,24},{20,28},{24,16},{28,20},{1,9},{5... | collective-permute-start | bytes 884744 | tf_op jit(solution)/shard_map/ppermute | solution.py:32
  5.0 1.5 %collective-permute-start.3 = (bf16[192,768]{1,0:T(8,128)(2,1)S(1)}, bf16[192,768]{1,0:T(8,128)(2,1)S(1)}, u32[]{:S(2)}, u32[]{:S(2)}) collective-permute-start(bf16[192,768]{1,0:T(8,128)(2,1)S(1)} %get-tuple-element.29), channel_id=1, source_target_pairs={{0,16},{4,20},{8,24},{12,28},{16,0},{20,4},{24,8},{28,12},{1,17},{... | collective-permute-start | bytes 884744 | tf_op jit(solution)/shard_map/ppermute | solution.py:32
  6.5 1.5 %constant_dynamic-slice_fusion.1 = (bf16[192,384]{1,0:T(8,128)(2,1)S(1)}, bf16[192,384]{1,0:T(8,128)(2,1)S(1)}, bf16[192,384]{1,0:T(8,128)(2,1)S(1)}, bf16[192,3...) fusion(bf16[192,3072]{1,0:T(8,128)(2,1)} %param.13, ...), kind=kLoop, calls=%fused_computation.72 | loop fusion | bytes 2359328 | tf_op jit(solution)/shard_map/dynamic_slice | solution.py:87
  8.0 0.6 collective-permute-start
  8.6 0.1 collective-permute-start.2
  8.8 3.0 %collective-permute-start.4 = (bf16[192,768]{1,0:T(8,128)(2,1)S(1)}, bf16[192,768]{1,0:T(8,128)(2,1)S(1)}, u32[]{:S(2)}, u32[]{:S(2)}) collective-permute-start(bf16[192,768]{1,0:T(8,128)(2,1)S(1)} %pad_maximum_fusion.2), channel_id=1, source_target_pairs={{0,24},{4,28},{8,16},{12,20},{16,8},{20,12},{24,0},{28,4},{1,25},{... | collective-permute-start | bytes 884744 | tf_op jit(solution)/shard_map/ppermute | solution.py:32
  11.7 0.5 fusion.12
  12.2 0.5 collective-permute-done.1
  12.8 2.2 %collective-permute-start.5 = (bf16[96,768]{1,0:T(8,128)(2,1)S(1)}, bf16[96,768]{1,0:T(8,128)(2,1)S(1)}, u32[]{:S(2)}, u32[]{:S(2)}) collective-permute-start(bf16[96,768]{1,0:T(8,128)(2,1)S(1)} %slice.40), channel_id=1, source_target_pairs={{0,16},{4,20},{8,24},{12,28},{16,0},{20,4},{24,8},{28,12},{1,17},{... | collective-permute-start | bytes 442376 | tf_op jit(solution)/shard_map/ppermute | solution.py:32
  15.0 1.6 %collective-permute-start.6 = (bf16[96,768]{1,0:T(8,128)(2,1)S(1)}, bf16[96,768]{1,0:T(8,128)(2,1)S(1)}, u32[]{:S(2)}, u32[]{:S(2)}) collective-permute-start(bf16[96,768]{1,0:T(8,128)(2,1)S(1)} %slice.41), channel_id=1, source_target_pairs={{0,8},{4,12},{8,0},{12,4},{16,24},{20,28},{24,16},{28,20},{1,9},{5... | collective-permute-start | bytes 442376 | tf_op jit(solution)/shard_map/ppermute | solution.py:32
  16.5 2.6 %collective-permute-done = bf16[192,768]{1,0:T(8,128)(2,1)S(1)} collective-permute-done((bf16[192,768]{1,0:T(8,128)(2,1)S(1)}, bf16[192,768]{1,0:T(8,128)(2,1)S(1)}, u32[]{:S(2)}, u32[]{:S(2)}) %collective-permute-start) | collective-permute-done | bytes 294944 | tf_op jit(solution)/shard_map/ppermute | solution.py:32
  19.1 0.5 fusion.55
  19.6 7.9 %collective-permute-done.2 = bf16[192,768]{1,0:T(8,128)(2,1)S(1)} collective-permute-done((bf16[192,768]{1,0:T(8,128)(2,1)S(1)}, bf16[192,768]{1,0:T(8,128)(2,1)S(1)}, u32[]{:S(2)}, u32[]{:S(2)}) %collective-permute-start.2) | collective-permute-done | bytes 294944 | tf_op jit(solution)/shard_map/ppermute | solution.py:32
  27.5 0.5 fusion.56
  28.1 1.2 %collective-permute-done.5 = bf16[96,768]{1,0:T(8,128)(2,1)S(1)} collective-permute-done((bf16[96,768]{1,0:T(8,128)(2,1)S(1)}, bf16[96,768]{1,0:T(8,128)(2,1)S(1)}, u32[]{:S(2)}, u32[]{:S(2)}) %collective-permute-start.5) | collective-permute-done | bytes 147488 | tf_op jit(solution)/shard_map/ppermute | solution.py:32
  29.2 0.5 add_add_fusion
  29.8 1.4 %copy-done.1 = f32[768,768]{1,0:T(8,128)} copy-done((f32[768,768]{1,0:T(8,128)}, f32[768,768]{1,0:T(8,128)S(1)}, u32[]{:S(2)}) %copy-start.1) | copy-done | bytes 2359320
  31.2 0.1 slice.43
  31.4 2.9 %collective-permute-done.7 = f32[384,768]{1,0:T(8,128)} collective-permute-done((f32[384,768]{1,0:T(8,128)S(1)}, f32[384,768]{1,0:T(8,128)}, u32[]{:S(2)}, u32[]{:S(2)}) %collective-permute-start.7) | collective-permute-done | bytes 1179680 | tf_op jit(solution)/shard_map/ppermute | solution.py:32
  34.3 1.8 %slice_add_fusion = f32[384,768]{1,0:T(8,128)S(1)} fusion(f32[384,768]{1,0:T(8,128)} %collective-permute-done.7, f32[768,768]{1,0:T(8,128)} %copy-done.1), kind=kLoop, calls=%fused_computation.13 | loop fusion | flops 294912 | bytes 3538944 | tf_op jit(solution)/shard_map/add | solution.py:104
  36.1 0.7 dynamic-slice_convert_fusion.2
  36.8 3.6 %collective-permute-start.10 = (bf16[96,768]{1,0:T(8,128)(2,1)}, bf16[96,768]{1,0:T(8,128)(2,1)S(1)}, u32[]{:S(2)}, u32[]{:S(2)}) collective-permute-start(bf16[96,768]{1,0:T(8,128)(2,1)} %get-tuple-element.18), channel_id=1, source_target_pairs={{0,3},{1,2},{2,1},{3,0},{4,7},{5,6},{6,5},{7,4},{8,11},{9,10},{10,... | collective-permute-start | bytes 442376 | tf_op jit(solution)/shard_map/ppermute | solution.py:37
  40.4 0.8 collective-permute-start.9
  41.2 4.4 %collective-permute-done.10 = bf16[96,768]{1,0:T(8,128)(2,1)S(1)} collective-permute-done((bf16[96,768]{1,0:T(8,128)(2,1)}, bf16[96,768]{1,0:T(8,128)(2,1)S(1)}, u32[]{:S(2)}, u32[]{:S(2)}) %collective-permute-start.10) | collective-permute-done | bytes 147488 | tf_op jit(solution)/shard_map/ppermute | solution.py:37
  45.6 3.5 %collective-permute-done.8 = bf16[96,768]{1,0:T(8,128)(2,1)S(1)} collective-permute-done((bf16[96,768]{1,0:T(8,128)(2,1)S(1)}, bf16[96,768]{1,0:T(8,128)(2,1)S(1)}, u32[]{:S(2)}, u32[]{:S(2)}) %collective-permute-start.8) | collective-permute-done | bytes 147488 | tf_op jit(solution)/shard_map/ppermute | solution.py:37
  49.1 0.7 copy-done.6
  49.7 3.8 %collective-permute-done.9 = bf16[96,768]{1,0:T(8,128)(2,1)} collective-permute-done((bf16[96,768]{1,0:T(8,128)(2,1)S(1)}, bf16[96,768]{1,0:T(8,128)(2,1)}, u32[]{:S(2)}, u32[]{:S(2)}) %collective-permute-start.9) | collective-permute-done | bytes 147488 | tf_op jit(solution)/shard_map/ppermute | solution.py:37
  53.6 2.3 %constant_dynamic-update-slice_fusion.3 = (bf16[384,768]{1,0:T(8,128)(2,1)S(1)}, bf16[96,768]{1,0:T(8,128)(2,1)S(1)}, bf16[96,768]{1,0:T(8,128)(2,1)}, f32[96,768]{1,0:T(8,128)}) fusion(bf16[384,768]{1,0:T(8,128)(2,1)S(1)} %broadcast_in_dim.2, s32[]{:T(128)S(6)} %select_n.57, bf16[384,768]{1,0:T(8,128)(2,1)} %param.22, bf16[96,768]{1,0:T(8,128)(2,1)S(1)} %copy-done.3, ...), kind=kLoop, calls=%fused_computation.70 | loop fusion | flops 1916928 | bytes 2064388 | tf_op jit(solution)/shard_map/dynamic_update_slice | solution.py:122
  56.0 3.0 %collective-permute-start.12 = (bf16[96,768]{1,0:T(8,128)(2,1)S(1)}, bf16[96,768]{1,0:T(8,128)(2,1)S(1)}, u32[]{:S(2)}, u32[]{:S(2)}) collective-permute-start(bf16[96,768]{1,0:T(8,128)(2,1)S(1)} %get-tuple-element.14), channel_id=1, source_target_pairs={{0,2},{1,3},{2,0},{3,1},{4,6},{5,7},{6,4},{7,5},{8,10},{9,11},{10,... | collective-permute-start | bytes 442376 | tf_op jit(solution)/shard_map/ppermute | solution.py:37
  59.0 1.3 %collective-permute-start.13 = (bf16[96,768]{1,0:T(8,128)(2,1)S(1)}, bf16[96,768]{1,0:T(8,128)(2,1)S(1)}, u32[]{:S(2)}, u32[]{:S(2)}) collective-permute-start(bf16[96,768]{1,0:T(8,128)(2,1)S(1)} %get-tuple-element.14), channel_id=1, source_target_pairs={{0,3},{1,2},{2,1},{3,0},{4,7},{5,6},{6,5},{7,4},{8,11},{9,10},{10,... | collective-permute-start | bytes 442376 | tf_op jit(solution)/shard_map/ppermute | solution.py:37
  60.3 2.9 %collective-permute-done.11 = bf16[96,768]{1,0:T(8,128)(2,1)S(1)} collective-permute-done((bf16[96,768]{1,0:T(8,128)(2,1)S(1)}, bf16[96,768]{1,0:T(8,128)(2,1)S(1)}, u32[]{:S(2)}, u32[]{:S(2)}) %collective-permute-start.11) | collective-permute-done | bytes 147488 | tf_op jit(solution)/shard_map/ppermute | solution.py:37
  63.3 6.7 %collective-permute-done.12 = bf16[96,768]{1,0:T(8,128)(2,1)S(1)} collective-permute-done((bf16[96,768]{1,0:T(8,128)(2,1)S(1)}, bf16[96,768]{1,0:T(8,128)(2,1)S(1)}, u32[]{:S(2)}, u32[]{:S(2)}) %collective-permute-start.12) | collective-permute-done | bytes 147488 | tf_op jit(solution)/shard_map/ppermute | solution.py:37
  70.0 1.6 %collective-permute-start.22 = (bf16[384,768]{1,0:T(8,128)(2,1)S(1)}, bf16[384,768]{1,0:T(8,128)(2,1)S(1)}, u32[]{:S(2)}, u32[]{:S(2)}) collective-permute-start(bf16[384,768]{1,0:T(8,128)(2,1)S(1)} %constant_dynamic-update-slice_fusion), channel_id=1, source_target_pairs={{0,16},{4,20},{8,24},{12,28},{16,0},{20,4},{24,8},{28,12},{1,17},{... | collective-permute-start | bytes 1769480 | tf_op jit(solution)/shard_map/ppermute | solution.py:32
  71.6 0.5 collective-permute-start.20
  72.2 2.1 %collective-permute-start.14 = (f32[768]{0:T(1024)S(1)}, f32[768]{0:T(1024)S(1)}, u32[]{:S(2)}, u32[]{:S(2)}) collective-permute-start(f32[768]{0:T(1024)S(1)} %get-tuple-element.28), channel_id=1, source_target_pairs={{0,1},{1,0},{2,3},{3,2},{4,5},{5,4},{6,7},{7,6},{8,9},{9,8},{10,11... | collective-permute-start | bytes 9224 | tf_op jit(solution)/shard_map/ppermute | solution.py:37
  74.3 1.6 %collective-permute-done.14 = f32[768]{0:T(1024)S(1)} collective-permute-done((f32[768]{0:T(1024)S(1)}, f32[768]{0:T(1024)S(1)}, u32[]{:S(2)}, u32[]{:S(2)}) %collective-permute-start.14) | collective-permute-done | bytes 3104 | tf_op jit(solution)/shard_map/ppermute | solution.py:37
  75.9 2.9 %collective-permute-start.15 = (f32[768]{0:T(1024)S(1)}, f32[768]{0:T(1024)S(1)}, u32[]{:S(2)}, u32[]{:S(2)}) collective-permute-start(f32[768]{0:T(1024)S(1)} %add.169), channel_id=1, source_target_pairs={{0,2},{1,3},{2,0},{3,1},{4,6},{5,7},{6,4},{7,5},{8,10},{9,11},{10,... | collective-permute-start | bytes 9224 | tf_op jit(solution)/shard_map/ppermute | solution.py:37
  78.8 1.6 %collective-permute-done.15 = f32[768]{0:T(1024)S(1)} collective-permute-done((f32[768]{0:T(1024)S(1)}, f32[768]{0:T(1024)S(1)}, u32[]{:S(2)}, u32[]{:S(2)}) %collective-permute-start.15) | collective-permute-done | bytes 3104 | tf_op jit(solution)/shard_map/ppermute | solution.py:37
  80.4 1.2 %collective-permute-done.16 = f32[768]{0:T(1024)S(1)} collective-permute-done((f32[768]{0:T(1024)S(1)}, f32[768]{0:T(1024)S(1)}, u32[]{:S(2)}, u32[]{:S(2)}) %collective-permute-start.16) | collective-permute-done | bytes 3104 | tf_op jit(solution)/shard_map/ppermute | solution.py:32
  81.6 1.5 %collective-permute-start.17 = (f32[768]{0:T(1024)S(1)}, f32[768]{0:T(1024)S(1)}, u32[]{:S(2)}, u32[]{:S(2)}) collective-permute-start(f32[768]{0:T(1024)S(1)} %add.171), channel_id=1, source_target_pairs={{0,8},{4,12},{8,0},{12,4},{16,24},{20,28},{24,16},{28,20},{1,9},{5... | collective-permute-start | bytes 9224 | tf_op jit(solution)/shard_map/ppermute | solution.py:32
  83.0 2.1 %collective-permute-done.17 = f32[768]{0:T(1024)S(1)} collective-permute-done((f32[768]{0:T(1024)S(1)}, f32[768]{0:T(1024)S(1)}, u32[]{:S(2)}, u32[]{:S(2)}) %collective-permute-start.17) | collective-permute-done | bytes 3104 | tf_op jit(solution)/shard_map/ppermute | solution.py:32
  85.2 0.5 collective-permute-start.18
  85.7 3.1 %collective-permute-done.18 = f32[768]{0:T(1024)S(1)} collective-permute-done((f32[768]{0:T(1024)S(1)}, f32[768]{0:T(1024)S(1)}, u32[]{:S(2)}, u32[]{:S(2)}) %collective-permute-start.18) | collective-permute-done | bytes 3104 | tf_op jit(solution)/shard_map/ppermute | solution.py:32
  88.8 0.6 multiply_add_fusion.1
  89.4 1.8 %fusion.32 = (bf16[96,768]{1,0:T(8,128)(2,1)}, bf16[96,768]{1,0:T(8,128)(2,1)}) fusion(f32[96,768]{1,0:T(8,128)} %get-tuple-element.16, bf16[96,768]{1,0:T(8,128)(2,1)S(1)} %copy-done.3, bf16[96,768]{1,0:T(8,128)(2,1)} %param.20), kind=kLoop, calls=%fused_computation.48 | loop fusion | flops 811008 | bytes 884736 | tf_op jit(solution)/shard_map/convert_element_type | solution.py:141
  91.3 1.6 %collective-permute-start.26 = (bf16[192,768]{1,0:T(8,128)(2,1)S(1)}, bf16[192,768]{1,0:T(8,128)(2,1)S(1)}, u32[]{:S(2)}, u32[]{:S(2)}) collective-permute-start(bf16[192,768]{1,0:T(8,128)(2,1)S(1)} %slice.45), channel_id=1, source_target_pairs={{0,8},{4,12},{8,0},{12,4},{16,24},{20,28},{24,16},{28,20},{1,9},{5... | collective-permute-start | bytes 884744 | tf_op jit(solution)/shard_map/ppermute | solution.py:32
  92.8 0.6 collective-permute-start.24
  93.4 0.4 fusion.26
  93.8 0.4 fusion.28
  94.2 0.4 fusion
  94.5 0.4 fusion.23
  95.0 0.5 collective-permute-start.23
  95.5 4.2 %collective-permute-done.24 = bf16[192,768]{1,0:T(8,128)(2,1)S(1)} collective-permute-done((bf16[192,768]{1,0:T(8,128)(2,1)S(1)}, bf16[192,768]{1,0:T(8,128)(2,1)S(1)}, u32[]{:S(2)}, u32[]{:S(2)}) %collective-permute-start.24) | collective-permute-done | bytes 294944 | tf_op jit(solution)/shard_map/ppermute | solution.py:32
  99.6 0.3 fusion.39
  100.0 0.6 collective-permute-start.27
  100.5 0.3 fusion.35
  100.8 0.4 collective-permute-done.25
  101.2 0.3 fusion.37
  101.5 0.2 collective-permute-done.27
  101.7 0.3 fusion.33
  102.1 0.4 fusion.1
  102.5 0.6 copy-done.4
  103.1 1.2 %fusion.8 = bf16[256,768]{1,0:T(8,128)(2,1)} fusion(f32[256,768]{1,0:T(8,128)S(1)} %fusion.33, f32[256,768]{1,0:T(8,128)S(1)} %fusion.35, f32[256,768]{1,0:T(8,128)S(1)} %fusion.37, f32[256,768]{1,0:T(8,128)S(1)} %fusion.39, f32[256,768]{1,0:T(8,128)S(1)} %fusion.1, bf16[384,768]{1,0:T(8,128)(2,1)S(1)} %collective-permute-done.23, ...), kind=kOutput, calls=%fused_computation.12 | convolution fusion | flops 152764416 | bytes 5509124 | tf_op jit(solution)/shard_map/dot_general | solution.py:132
  (53 shorter events, 0.5 us)
Async XLA Ops:
  0.6 92.8 %copy-start = (bf16[256,3072]{1,0:T(8,128)(2,1)S(1)}, bf16[256,3072]{1,0:T(8,128)(2,1)}, u32[]{:S(2)}) copy-start(bf16[256,3072]{1,0:T(8,128)(2,1)} %param.24) | copy-start | bytes 4718596
  1.9 10.8 %collective-permute-start.1 = (bf16[192,768]{1,0:T(8,128)(2,1)S(1)}, bf16[192,768]{1,0:T(8,128)(2,1)S(1)}, u32[]{:S(2)}, u32[]{:S(2)}) collective-permute-start(bf16[192,768]{1,0:T(8,128)(2,1)S(1)} %get-tuple-element.29), channel_id=1, source_target_pairs={{0,8},{4,12},{8,0},{12,4},{16,24},{20,28},{24,16},{28,20},{1,9},{5... | collective-permute-start | bytes 884744 | tf_op jit(solution)/shard_map/ppermute | solution.py:32
  5.0 10.0 %collective-permute-start.3 = (bf16[192,768]{1,0:T(8,128)(2,1)S(1)}, bf16[192,768]{1,0:T(8,128)(2,1)S(1)}, u32[]{:S(2)}, u32[]{:S(2)}) collective-permute-start(bf16[192,768]{1,0:T(8,128)(2,1)S(1)} %get-tuple-element.29), channel_id=1, source_target_pairs={{0,16},{4,20},{8,24},{12,28},{16,0},{20,4},{24,8},{28,12},{1,17},{... | collective-permute-start | bytes 884744 | tf_op jit(solution)/shard_map/ppermute | solution.py:32
  8.0 11.1 %collective-permute-start = (bf16[192,768]{1,0:T(8,128)(2,1)S(1)}, bf16[192,768]{1,0:T(8,128)(2,1)S(1)}, u32[]{:S(2)}, u32[]{:S(2)}) collective-permute-start(bf16[192,768]{1,0:T(8,128)(2,1)S(1)} %pad_maximum_fusion), channel_id=1, source_target_pairs={{0,8},{4,12},{8,0},{12,4},{16,24},{20,28},{24,16},{28,20},{1,9},{5... | collective-permute-start | bytes 884744 | tf_op jit(solution)/shard_map/ppermute | solution.py:32
  8.6 18.9 %collective-permute-start.2 = (bf16[192,768]{1,0:T(8,128)(2,1)S(1)}, bf16[192,768]{1,0:T(8,128)(2,1)S(1)}, u32[]{:S(2)}, u32[]{:S(2)}) collective-permute-start(bf16[192,768]{1,0:T(8,128)(2,1)S(1)} %pad_maximum_fusion.1), channel_id=1, source_target_pairs={{0,16},{4,20},{8,24},{12,28},{16,0},{20,4},{24,8},{28,12},{1,17},{... | collective-permute-start | bytes 884744 | tf_op jit(solution)/shard_map/ppermute | solution.py:32
  8.8 19.3 %collective-permute-start.4 = (bf16[192,768]{1,0:T(8,128)(2,1)S(1)}, bf16[192,768]{1,0:T(8,128)(2,1)S(1)}, u32[]{:S(2)}, u32[]{:S(2)}) collective-permute-start(bf16[192,768]{1,0:T(8,128)(2,1)S(1)} %pad_maximum_fusion.2), channel_id=1, source_target_pairs={{0,24},{4,28},{8,16},{12,20},{16,8},{20,12},{24,0},{28,4},{1,25},{... | collective-permute-start | bytes 884744 | tf_op jit(solution)/shard_map/ppermute | solution.py:32
  12.8 16.4 %collective-permute-start.5 = (bf16[96,768]{1,0:T(8,128)(2,1)S(1)}, bf16[96,768]{1,0:T(8,128)(2,1)S(1)}, u32[]{:S(2)}, u32[]{:S(2)}) collective-permute-start(bf16[96,768]{1,0:T(8,128)(2,1)S(1)} %slice.40), channel_id=1, source_target_pairs={{0,16},{4,20},{8,24},{12,28},{16,0},{20,4},{24,8},{28,12},{1,17},{... | collective-permute-start | bytes 442376 | tf_op jit(solution)/shard_map/ppermute | solution.py:32
  15.0 14.2 %collective-permute-start.6 = (bf16[96,768]{1,0:T(8,128)(2,1)S(1)}, bf16[96,768]{1,0:T(8,128)(2,1)S(1)}, u32[]{:S(2)}, u32[]{:S(2)}) collective-permute-start(bf16[96,768]{1,0:T(8,128)(2,1)S(1)} %slice.41), channel_id=1, source_target_pairs={{0,8},{4,12},{8,0},{12,4},{16,24},{20,28},{24,16},{28,20},{1,9},{5... | collective-permute-start | bytes 442376 | tf_op jit(solution)/shard_map/ppermute | solution.py:32
  29.8 1.4 %copy-start.1 = (f32[768,768]{1,0:T(8,128)}, f32[768,768]{1,0:T(8,128)S(1)}, u32[]{:S(2)}) copy-start(f32[768,768]{1,0:T(8,128)S(1)} %add_add_fusion) | copy-start | bytes 7077892
  31.3 3.0 %collective-permute-start.7 = (f32[384,768]{1,0:T(8,128)S(1)}, f32[384,768]{1,0:T(8,128)}, u32[]{:S(2)}, u32[]{:S(2)}) collective-permute-start(f32[384,768]{1,0:T(8,128)S(1)} %slice.43), channel_id=1, source_target_pairs={{0,4},{4,0},{8,12},{12,8},{16,20},{20,16},{24,28},{28,24},{1,5},{5... | collective-permute-start | bytes 3538952 | tf_op jit(solution)/shard_map/ppermute | solution.py:32
  36.1 17.5 %copy-start.3 = (bf16[96,768]{1,0:T(8,128)(2,1)S(1)}, bf16[96,768]{1,0:T(8,128)(2,1)}, u32[]{:S(2)}) copy-start(bf16[96,768]{1,0:T(8,128)(2,1)} %param.21) | copy-start | bytes 442372
  36.8 8.7 %collective-permute-start.10 = (bf16[96,768]{1,0:T(8,128)(2,1)}, bf16[96,768]{1,0:T(8,128)(2,1)S(1)}, u32[]{:S(2)}, u32[]{:S(2)}) collective-permute-start(bf16[96,768]{1,0:T(8,128)(2,1)} %get-tuple-element.18), channel_id=1, source_target_pairs={{0,3},{1,2},{2,1},{3,0},{4,7},{5,6},{6,5},{7,4},{8,11},{9,10},{10,... | collective-permute-start | bytes 442376 | tf_op jit(solution)/shard_map/ppermute | solution.py:37
  40.4 8.6 %collective-permute-start.8 = (bf16[96,768]{1,0:T(8,128)(2,1)S(1)}, bf16[96,768]{1,0:T(8,128)(2,1)S(1)}, u32[]{:S(2)}, u32[]{:S(2)}) collective-permute-start(bf16[96,768]{1,0:T(8,128)(2,1)S(1)} %get-tuple-element.17), channel_id=1, source_target_pairs={{0,1},{1,0},{2,3},{3,2},{4,5},{5,4},{6,7},{7,6},{8,9},{9,8},{10,11... | collective-permute-start | bytes 442376 | tf_op jit(solution)/shard_map/ppermute | solution.py:37
  40.4 13.1 %collective-permute-start.9 = (bf16[96,768]{1,0:T(8,128)(2,1)S(1)}, bf16[96,768]{1,0:T(8,128)(2,1)}, u32[]{:S(2)}, u32[]{:S(2)}) collective-permute-start(bf16[96,768]{1,0:T(8,128)(2,1)S(1)} %get-tuple-element.19), channel_id=1, source_target_pairs={{0,2},{1,3},{2,0},{3,1},{4,6},{5,7},{6,4},{7,5},{8,10},{9,11},{10,... | collective-permute-start | bytes 442376 | tf_op jit(solution)/shard_map/ppermute | solution.py:37
  45.6 3.5 %copy-start.5 = (bf16[96,768]{1,0:T(8,128)(2,1)}, bf16[96,768]{1,0:T(8,128)(2,1)S(1)}, u32[]{:S(2)}) copy-start(bf16[96,768]{1,0:T(8,128)(2,1)S(1)} %collective-permute-done.10) | copy-start | bytes 442372
  49.1 0.7 copy-start.6
  53.6 35.2 %copy-start.7 = (f32[768]{0:T(1024)S(1)}, f32[768]{0:T(1024)}, u32[]{:S(2)}) copy-start(f32[768]{0:T(1024)} %param.16) | copy-start | bytes 9220
  53.6 35.2 %copy-start.9 = (f32[768]{0:T(1024)S(1)}, f32[768]{0:T(1024)}, u32[]{:S(2)}) copy-start(f32[768]{0:T(1024)} %param.23) | copy-start | bytes 9220
  53.6 35.2 %copy-start.10 = (f32[768]{0:T(1024)S(1)}, f32[768]{0:T(1024)}, u32[]{:S(2)}) copy-start(f32[768]{0:T(1024)} %param.17) | copy-start | bytes 9220
  53.6 35.2 %copy-start.11 = (f32[768]{0:T(1024)S(1)}, f32[768]{0:T(1024)}, u32[]{:S(2)}) copy-start(f32[768]{0:T(1024)} %param.18) | copy-start | bytes 9220
  56.0 7.3 %collective-permute-start.11 = (bf16[96,768]{1,0:T(8,128)(2,1)S(1)}, bf16[96,768]{1,0:T(8,128)(2,1)S(1)}, u32[]{:S(2)}, u32[]{:S(2)}) collective-permute-start(bf16[96,768]{1,0:T(8,128)(2,1)S(1)} %get-tuple-element.14), channel_id=1, source_target_pairs={{0,1},{1,0},{2,3},{3,2},{4,5},{5,4},{6,7},{7,6},{8,9},{9,8},{10,11... | collective-permute-start | bytes 442376 | tf_op jit(solution)/shard_map/ppermute | solution.py:37
  56.0 14.0 %collective-permute-start.12 = (bf16[96,768]{1,0:T(8,128)(2,1)S(1)}, bf16[96,768]{1,0:T(8,128)(2,1)S(1)}, u32[]{:S(2)}, u32[]{:S(2)}) collective-permute-start(bf16[96,768]{1,0:T(8,128)(2,1)S(1)} %get-tuple-element.14), channel_id=1, source_target_pairs={{0,2},{1,3},{2,0},{3,1},{4,6},{5,7},{6,4},{7,5},{8,10},{9,11},{10,... | collective-permute-start | bytes 442376 | tf_op jit(solution)/shard_map/ppermute | solution.py:37
  59.0 11.0 %collective-permute-start.13 = (bf16[96,768]{1,0:T(8,128)(2,1)S(1)}, bf16[96,768]{1,0:T(8,128)(2,1)S(1)}, u32[]{:S(2)}, u32[]{:S(2)}) collective-permute-start(bf16[96,768]{1,0:T(8,128)(2,1)S(1)} %get-tuple-element.14), channel_id=1, source_target_pairs={{0,3},{1,2},{2,1},{3,0},{4,7},{5,6},{6,5},{7,4},{8,11},{9,10},{10,... | collective-permute-start | bytes 442376 | tf_op jit(solution)/shard_map/ppermute | solution.py:37
  70.0 24.1 %copy-start.2 = (bf16[384,768]{1,0:T(8,128)(2,1)}, bf16[384,768]{1,0:T(8,128)(2,1)S(1)}, u32[]{:S(2)}) copy-start(bf16[384,768]{1,0:T(8,128)(2,1)S(1)} %constant_dynamic-update-slice_fusion) | copy-start | bytes 1769476
  70.0 21.2 %collective-permute-start.22 = (bf16[384,768]{1,0:T(8,128)(2,1)S(1)}, bf16[384,768]{1,0:T(8,128)(2,1)S(1)}, u32[]{:S(2)}, u32[]{:S(2)}) collective-permute-start(bf16[384,768]{1,0:T(8,128)(2,1)S(1)} %constant_dynamic-update-slice_fusion), channel_id=1, source_target_pairs={{0,16},{4,20},{8,24},{12,28},{16,0},{20,4},{24,8},{28,12},{1,17},{... | collective-permute-start | bytes 1769480 | tf_op jit(solution)/shard_map/ppermute | solution.py:32
  71.6 21.2 %collective-permute-start.20 = (bf16[384,768]{1,0:T(8,128)(2,1)S(1)}, bf16[384,768]{1,0:T(8,128)(2,1)S(1)}, u32[]{:S(2)}, u32[]{:S(2)}) collective-permute-start(bf16[384,768]{1,0:T(8,128)(2,1)S(1)} %constant_dynamic-update-slice_fusion), channel_id=1, source_target_pairs={{0,8},{4,12},{8,0},{12,4},{16,24},{20,28},{24,16},{28,20},{1,9},{5... | collective-permute-start | bytes 1769480 | tf_op jit(solution)/shard_map/ppermute | solution.py:32
  72.2 3.7 %collective-permute-start.14 = (f32[768]{0:T(1024)S(1)}, f32[768]{0:T(1024)S(1)}, u32[]{:S(2)}, u32[]{:S(2)}) collective-permute-start(f32[768]{0:T(1024)S(1)} %get-tuple-element.28), channel_id=1, source_target_pairs={{0,1},{1,0},{2,3},{3,2},{4,5},{5,4},{6,7},{7,6},{8,9},{9,8},{10,11... | collective-permute-start | bytes 9224 | tf_op jit(solution)/shard_map/ppermute | solution.py:37
  75.9 4.5 %collective-permute-start.15 = (f32[768]{0:T(1024)S(1)}, f32[768]{0:T(1024)S(1)}, u32[]{:S(2)}, u32[]{:S(2)}) collective-permute-start(f32[768]{0:T(1024)S(1)} %add.169), channel_id=1, source_target_pairs={{0,2},{1,3},{2,0},{3,1},{4,6},{5,7},{6,4},{7,5},{8,10},{9,11},{10,... | collective-permute-start | bytes 9224 | tf_op jit(solution)/shard_map/ppermute | solution.py:37
  80.4 1.2 %collective-permute-start.16 = (f32[768]{0:T(1024)S(1)}, f32[768]{0:T(1024)S(1)}, u32[]{:S(2)}, u32[]{:S(2)}) collective-permute-start(f32[768]{0:T(1024)S(1)} %add.170), channel_id=1, source_target_pairs={{0,4},{4,0},{8,12},{12,8},{16,20},{20,16},{24,28},{28,24},{1,5},{5... | collective-permute-start | bytes 9224 | tf_op jit(solution)/shard_map/ppermute | solution.py:32
  81.6 3.6 %collective-permute-start.17 = (f32[768]{0:T(1024)S(1)}, f32[768]{0:T(1024)S(1)}, u32[]{:S(2)}, u32[]{:S(2)}) collective-permute-start(f32[768]{0:T(1024)S(1)} %add.171), channel_id=1, source_target_pairs={{0,8},{4,12},{8,0},{12,4},{16,24},{20,28},{24,16},{28,20},{1,9},{5... | collective-permute-start | bytes 9224 | tf_op jit(solution)/shard_map/ppermute | solution.py:32
  85.2 3.6 %collective-permute-start.18 = (f32[768]{0:T(1024)S(1)}, f32[768]{0:T(1024)S(1)}, u32[]{:S(2)}, u32[]{:S(2)}) collective-permute-start(f32[768]{0:T(1024)S(1)} %add.172), channel_id=1, source_target_pairs={{0,16},{4,20},{8,24},{12,28},{16,0},{20,4},{24,8},{28,12},{1,17},{... | collective-permute-start | bytes 9224 | tf_op jit(solution)/shard_map/ppermute | solution.py:32
  85.7 8.1 %collective-permute-start.19 = (bf16[384,768]{1,0:T(8,128)(2,1)S(1)}, bf16[384,768]{1,0:T(8,128)(2,1)S(1)}, u32[]{:S(2)}, u32[]{:S(2)}) collective-permute-start(bf16[384,768]{1,0:T(8,128)(2,1)S(1)} %constant_dynamic-update-slice_fusion), channel_id=1, source_target_pairs={{0,4},{4,0},{8,12},{12,8},{16,20},{20,16},{24,28},{28,24},{1,5},{5... | collective-permute-start | bytes 1769480 | tf_op jit(solution)/shard_map/ppermute | solution.py:32
  89.4 13.1 %copy-start.8 = (f32[768]{0:T(1024)}, f32[768]{0:T(1024)S(1)}, u32[]{:S(2)}) copy-start(f32[768]{0:T(1024)S(1)} %get-tuple-element.9) | copy-start | bytes 9220
  91.3 8.7 %collective-permute-start.26 = (bf16[192,768]{1,0:T(8,128)(2,1)S(1)}, bf16[192,768]{1,0:T(8,128)(2,1)S(1)}, u32[]{:S(2)}, u32[]{:S(2)}) collective-permute-start(bf16[192,768]{1,0:T(8,128)(2,1)S(1)} %slice.45), channel_id=1, source_target_pairs={{0,8},{4,12},{8,0},{12,4},{16,24},{20,28},{24,16},{28,20},{1,9},{5... | collective-permute-start | bytes 884744 | tf_op jit(solution)/shard_map/ppermute | solution.py:32
  92.8 6.8 %collective-permute-start.24 = (bf16[192,768]{1,0:T(8,128)(2,1)S(1)}, bf16[192,768]{1,0:T(8,128)(2,1)S(1)}, u32[]{:S(2)}, u32[]{:S(2)}) collective-permute-start(bf16[192,768]{1,0:T(8,128)(2,1)S(1)} %slice.44), channel_id=1, source_target_pairs={{0,16},{4,20},{8,24},{12,28},{16,0},{20,4},{24,8},{28,12},{1,17},{... | collective-permute-start | bytes 884744 | tf_op jit(solution)/shard_map/ppermute | solution.py:32
  94.9 7.2 %collective-permute-start.21 = (bf16[384,768]{1,0:T(8,128)(2,1)S(1)}, bf16[384,768]{1,0:T(8,128)(2,1)S(1)}, u32[]{:S(2)}, u32[]{:S(2)}) collective-permute-start(bf16[384,768]{1,0:T(8,128)(2,1)S(1)} %collective-permute-done.20), channel_id=1, source_target_pairs={{0,4},{4,0},{8,12},{12,8},{16,20},{20,16},{24,28},{28,24},{1,5},{5... | collective-permute-start | bytes 1769480 | tf_op jit(solution)/shard_map/ppermute | solution.py:32
  95.0 7.5 %collective-permute-start.23 = (bf16[384,768]{1,0:T(8,128)(2,1)S(1)}, bf16[384,768]{1,0:T(8,128)(2,1)S(1)}, u32[]{:S(2)}, u32[]{:S(2)}) collective-permute-start(bf16[384,768]{1,0:T(8,128)(2,1)S(1)} %collective-permute-done.22), channel_id=1, source_target_pairs={{0,4},{4,0},{8,12},{12,8},{16,20},{20,16},{24,28},{28,24},{1,5},{5... | collective-permute-start | bytes 1769480 | tf_op jit(solution)/shard_map/ppermute | solution.py:32
  99.6 1.6 %collective-permute-start.25 = (bf16[192,768]{1,0:T(8,128)(2,1)S(1)}, bf16[192,768]{1,0:T(8,128)(2,1)S(1)}, u32[]{:S(2)}, u32[]{:S(2)}) collective-permute-start(bf16[192,768]{1,0:T(8,128)(2,1)S(1)} %collective-permute-done.24), channel_id=1, source_target_pairs={{0,4},{4,0},{8,12},{12,8},{16,20},{20,16},{24,28},{28,24},{1,5},{5... | collective-permute-start | bytes 884744 | tf_op jit(solution)/shard_map/ppermute | solution.py:32
  100.0 1.8 %collective-permute-start.27 = (bf16[192,768]{1,0:T(8,128)(2,1)S(1)}, bf16[192,768]{1,0:T(8,128)(2,1)S(1)}, u32[]{:S(2)}, u32[]{:S(2)}) collective-permute-start(bf16[192,768]{1,0:T(8,128)(2,1)S(1)} %collective-permute-done.26), channel_id=1, source_target_pairs={{0,4},{4,0},{8,12},{12,8},{16,20},{20,16},{24,28},{28,24},{1,5},{5... | collective-permute-start | bytes 884744 | tf_op jit(solution)/shard_map/ppermute | solution.py:32
  102.1 1.0 copy-start.4

commit v2 on v1

--- a/solution.py
+++ b/solution.py
@@ -1,6 +1,8 @@
 import jax
 import jax.numpy as jnp
 from jax import lax
+from jax.experimental import pallas as pl
+from jax.experimental.pallas import tpu as pltpu
 from jax.sharding import PartitionSpec as P
 
 beta_one = 0.9
@@ -60,7 +62,7 @@
     return value
 
 
-def shards(
+def general_shards(
     student_hidden,
     out_cotangent,
     student_branch,
@@ -148,6 +150,199 @@
     )
 
 
+def after(value, *others):
+    return lax.optimization_barrier((value,) + others)[0]
+
+
+MIB = 1024 * 1024
+VMEM = pl.BlockSpec(memory_space=pltpu.VMEM)
+SMEM = pl.BlockSpec(memory_space=pltpu.SMEM)
+
+
+def three_parts(value):
+    high = lax.reduce_precision(value, 8, 7)
+    rest = value - high
+    mid = lax.reduce_precision(rest, 8, 7)
+    return [high, mid, rest - mid]
+
+
+def split_kernel(place, keep, arrived, own, *outgoing):
+    rows = own.shape[0]
+    for j in range(len(outgoing) + 1):
+        at = pl.ds(pl.multiple_of((place[0] ^ j) * rows, 32), rows)
+        total = keep[at, :] + arrived[at, :]
+        if j:
+            outgoing[j - 1][...] = total.astype(jnp.bfloat16)
+        else:
+            own[...] = total
+
+
+def split_rows(place, keep, arrived, rows, count):
+    width = keep.shape[1]
+    return pl.pallas_call(
+        split_kernel,
+        out_shape=[jax.ShapeDtypeStruct((rows, width), jnp.float32)]
+        + [jax.ShapeDtypeStruct((rows, width), jnp.bfloat16)] * (count - 1),
+        in_specs=[SMEM, VMEM, VMEM],
+        out_specs=[VMEM] * count,
+        compiler_params=pltpu.CompilerParams(vmem_limit_bytes=24 * MIB),
+        cost_estimate=pl.CostEstimate(
+            flops=keep.size, bytes_accessed=11 * keep.size, transcendentals=0
+        ),
+        name="split_rows",
+    )(place, keep, arrived)
+
+
+def update_kernel(place, own, one, two, three, weight, first, second, teacher, *outs):
+    new_weight, new_first, new_second, sent = outs
+    rows = own.shape[0]
+    gradient = own[...] + one[...].astype(jnp.float32)
+    gradient = gradient + two[...].astype(jnp.float32) + three[...].astype(jnp.float32)
+    weight_new, first_new, second_new = adam_step(
+        weight[...], first[...], second[...], gradient
+    )
+    new_weight[...] = weight_new.astype(jnp.bfloat16)
+    new_first[...] = first_new.astype(jnp.bfloat16)
+    new_second[...] = second_new.astype(jnp.bfloat16)
+    held = teacher[pl.ds(pl.multiple_of(place[0] * rows, 32), rows), :].astype(jnp.float32)
+    sent[...] = (teacher_keep * held + (1.0 - teacher_keep) * weight_new).astype(jnp.bfloat16)
+
+
+def update_rows(place, own, arrived, weight, first, second, teacher):
+    rows, width = own.shape
+    stored = jax.ShapeDtypeStruct((rows, width), jnp.bfloat16)
+    return pl.pallas_call(
+        update_kernel,
+        out_shape=[stored] * 4,
+        in_specs=[SMEM] + [VMEM] * 8,
+        out_specs=[VMEM] * 4,
+        compiler_params=pltpu.CompilerParams(vmem_limit_bytes=24 * MIB),
+        cost_estimate=pl.CostEstimate(
+            flops=20 * own.size, bytes_accessed=30 * own.size, transcendentals=2 * own.size
+        ),
+        name="update_rows",
+    )(place, own, *arrived, weight, first, second, teacher)
+
+
+def block_shards(
+    student_hidden,
+    out_cotangent,
+    student_branch,
+    layer_scale,
+    scale_first,
+    scale_second,
+    student_weight,
+    first_moment,
+    second_moment,
+    teacher_weight,
+    teacher_scale,
+    teacher_hidden,
+    teacher_input,
+):
+    rep_count = 4
+    tokens = student_hidden.shape[0]
+    own_rows, model_width = student_weight.shape
+    width = rep_count * own_rows
+    pair_rows = 2 * own_rows
+    me = lax.axis_index("fsdp")
+    my_rep = lax.axis_index("rep")
+    place = my_rep.astype(jnp.int32).reshape(1)
+
+    def columns(array, flip):
+        return lax.dynamic_slice_in_dim(array, (me ^ flip) * width, width, 1)
+
+    cot_x, cot_y = swap_fsdp(out_cotangent, 2), swap_fsdp(out_cotangent, 4)
+    share = jnp.sum(
+        out_cotangent.astype(jnp.float32) * student_branch.astype(jnp.float32), axis=0
+    )
+    tail = jnp.stack(three_parts(share)).astype(jnp.bfloat16)
+    tail = jnp.pad(tail, ((0, 8 - 3), (0, 0)))
+    hidden_of = [jnp.concatenate([columns(student_hidden, 0), columns(student_hidden, 1)], 1)]
+    for flip in (2, 4, 6):
+        sent = jnp.concatenate([columns(student_hidden, flip), columns(student_hidden, flip + 1)], 1)
+        hidden_of.append(swap_fsdp(jnp.concatenate([sent, tail], 0), flip))
+    half = tokens // 2
+    corner = [swap_fsdp(cot_x[:half], 4), swap_fsdp(cot_y[half:], 2)]
+    cotangents = [[out_cotangent], [cot_x], [cot_y], corner]
+    for hidden in hidden_of[1:]:
+        share = share + jnp.sum(hidden[tokens : tokens + 3].astype(jnp.float32), axis=0)
+
+    def scale_it(block):
+        scaled = (block.astype(jnp.float32) * layer_scale).astype(jnp.bfloat16)
+        return lax.optimization_barrier(scaled)
+
+    keep = send = None
+    for hidden, blocks in zip(hidden_of, cotangents):
+        start = 0
+        for block in blocks:
+            stop = start + block.shape[0]
+            scaled = scale_it(block)
+            term = token_fold(hidden[start:stop, width:], scaled)
+            send = term if send is None else send + term
+            term = token_fold(hidden[start:stop, :width], scaled)
+            keep = term if keep is None else keep + term
+            start = stop
+    share = share + swap_fsdp(share, 1)
+    own, *outgoing = split_rows(place, keep, swap_fsdp(send, 1), own_rows, rep_count)
+    arrived = [swap_rep(piece, j + 1) for j, piece in enumerate(outgoing)]
+    new_weight, new_first, new_second, sent_rows = update_rows(
+        place,
+        own,
+        arrived,
+        student_weight,
+        first_moment,
+        second_moment,
+        teacher_weight,
+    )
+
+    teacher_shard = lax.all_gather(sent_rows, "rep", axis=0, tiled=True)
+    share = sum([swap_rep(share, j) for j in range(1, rep_count)], share)
+    scale_new, scale_first_new, scale_second_new = adam_step(
+        layer_scale, scale_first, scale_second, share
+    )
+    teacher_scale_new = teacher_keep * teacher_scale + (1.0 - teacher_keep) * scale_new
+
+    along_x, along_y = swap_fsdp(teacher_shard, 2), swap_fsdp(teacher_shard, 4)
+    corner_x = swap_fsdp(along_x[:pair_rows], 4)
+    corner_y = swap_fsdp(along_y[pair_rows:], 2)
+    held = [(teacher_shard, 0, 0), (along_x, 2, 0), (along_y, 4, 0)]
+    held += [(corner_x, 6, 0), (corner_y, 6, pair_rows)]
+    projected = None
+    for block, flip, start in held:
+        for weights, f in ((block, flip), (swap_fsdp(block, 1), flip + 1)):
+            units = columns(teacher_hidden, f)[:, start : start + block.shape[0]]
+            term = jnp.dot(units, weights, preferred_element_type=jnp.float32)
+            projected = term if projected is None else projected + term
+    teacher_out = (teacher_input.astype(jnp.float32) + teacher_scale_new * projected).astype(
+        jnp.bfloat16
+    )
+    return (
+        new_weight,
+        new_first,
+        new_second,
+        teacher_shard,
+        scale_new,
+        scale_first_new,
+        scale_second_new,
+        teacher_scale_new,
+        teacher_out,
+    )
+
+
+def shards(*args):
+    hidden, weight = args[0], args[6]
+    rows, model_width = weight.shape
+    fits = (
+        lax.axis_size("fsdp") == 8
+        and lax.axis_size("rep") == 4
+        and rows % 32 == 0
+        and hidden.shape[0] % 32 == 0
+        and 8 * rows == model_width
+        and model_width % 256 == 0
+    )
+    return block_shards(*args) if fits else general_shards(*args)
+
+
 def solution(mesh):
     in_specs = (
         P(("fsdp", "rep"), None),

time: 105 us -> 97.3 us (0.927)
  blocking collectives: 0 us -> 15.7 us
  waiting for transfers between devices: 50.7 us -> 37.1 us
  other arithmetic: 7.89 us -> 1.05 us
  starting transfers between devices: 33.2 us -> 27.4 us
  matrix products: 6.36 us -> 10.8 us
  local copies, waits for them, and re-layouts: 5.14 us -> 2.87 us
  Pallas kernels: 0 us -> 1.12 us
    all_gather x0 -> x1, blocking collectives: none -> 15.7 us  [block_shards(): teacher_shard = lax.all_gather(sent_rows, 'rep', axis=0, tiled=True)]
    ppermute x8 -> x6, waiting for transfers between devices: 24.4 us -> 14.7 us  [swap_rep(): return lax.ppermute(value, 'rep', [(i, i ^ flip) for i in range(count)])]
    ppermute x20 -> x18, waiting for transfers between devices: 26.3 us -> 22.4 us  [swap_fsdp(): return lax.ppermute(value, 'fsdp', [(i, i ^ flip) for i in range(count)])]
    dot_general x4 -> x10, matrix products: 2.1 us -> 5.43 us  [token_fold(): lax.dot_general(arrived, portion, (((0,), (0,)), ((), ())), preferred_ele...]
    ppermute x20 -> x18, starting transfers between devices: 19.4 us -> 16.2 us  [swap_fsdp(): return lax.ppermute(value, 'fsdp', [(i, i ^ flip) for i in range(count)])]
    ppermute x8 -> x6, starting transfers between devices: 13.8 us -> 11.2 us  [swap_rep(): return lax.ppermute(value, 'rep', [(i, i ^ flip) for i in range(count)])]
    dynamic_update_slice x1 -> x0, other arithmetic: 2.32 us -> none  [shards(): lax.dynamic_update_slice_in_dim(teacher_shard, piece, (my_rep ^ j) * own_...]
    add x6 -> x3, other arithmetic: 2.4 us -> 0.63 us  [the longest x1 0.62 us: block_shards(): teacher_keep * teacher_scale + (1.0 - teacher_keep) * scale_new]
  transfers between devices with their start and end apart: 28 -> 24, of which waited for: 18 -> 14; matrix products, arithmetic and copies ran while one was open for 8% -> 12% of each run, Pallas kernels for 0% -> 0%
where the time goes in v2:
time: 97.3 us; the launch traced here: 97 us
  waiting for transfers between devices  37.1 us (38%)
  starting transfers between devices  27.4 us (28%)
  blocking collectives  15.7 us (16%)
  matrix products  10.8 us (11%)
  local copies, waits for them, and re-layouts  2.87 us (3%)
  Pallas kernels  1.12 us (1%)
  other arithmetic  1.05 us (1%)
  between operations  1 us (1%)
    ppermute x18, waiting for transfers between devices, swap_fsdp(): return lax.ppermute(value, 'fsdp', [(i, i ^ flip) for i in range(count)])  22.4 us
    ppermute x18, starting transfers between devices, swap_fsdp(): return lax.ppermute(value, 'fsdp', [(i, i ^ flip) for i in range(count)])  16.2 us
    all_gather x1, blocking collectives, block_shards(): teacher_shard = lax.all_gather(sent_rows, 'rep', axis=0, tiled=True)  15.7 us
    ppermute x6, waiting for transfers between devices, swap_rep(): return lax.ppermute(value, 'rep', [(i, i ^ flip) for i in range(count)])  14.7 us
    ppermute x6, starting transfers between devices, swap_rep(): return lax.ppermute(value, 'rep', [(i, i ^ flip) for i in range(count)])  11.2 us
    dot_general x10, matrix products, token_fold(): lax.dot_general(arrived, portion, (((0,), (0,)), ((), ())), preferred_ele...  5.43 us
    dot_general x10, matrix products, block_shards(): term = jnp.dot(units, weights, preferred_element_type=jnp.float32)  5.34 us
  transfers between devices with their start and end apart: 24, of which 14 were waited for; matrix products, arithmetic and copies ran while one was open for 12% of the time, Pallas kernels for 0%

profile of v2, /device:TPU:0, one launch (start us, length us, event | category | flops | bytes accessed | tf_op | source)
XLA Modules:
  0.0 97.0 jit_solution(10944123693881435568)
XLA Ops:
  0.7 3.0 %collective-permute-start.1 = (bf16[192,768]{1,0:T(8,128)(2,1)}, bf16[192,768]{1,0:T(8,128)(2,1)S(1)}, u32[]{:S(2)}, u32[]{:S(2)}) collective-permute-start(bf16[192,768]{1,0:T(8,128)(2,1)} %param.14), channel_id=1, source_target_pairs={{0,8},{4,12},{8,0},{12,4},{16,24},{20,28},{24,16},{28,20},{1,9},{5... | collective-permute-start | bytes 884744 | tf_op jit(solution)/shard_map/ppermute | solution.py:34
  3.7 1.5 %collective-permute-start.3 = (bf16[192,768]{1,0:T(8,128)(2,1)}, bf16[192,768]{1,0:T(8,128)(2,1)S(1)}, u32[]{:S(2)}, u32[]{:S(2)}) collective-permute-start(bf16[192,768]{1,0:T(8,128)(2,1)} %param.14), channel_id=1, source_target_pairs={{0,16},{4,20},{8,24},{12,28},{16,0},{20,4},{24,8},{28,12},{1,17},{... | collective-permute-start | bytes 884744 | tf_op jit(solution)/shard_map/ppermute | solution.py:34
  5.2 1.3 %constant_dynamic-slice_fusion.3 = (bf16[192,384]{1,0:T(8,128)(2,1)S(1)}, bf16[192,384]{1,0:T(8,128)(2,1)S(1)}, bf16[192,384]{1,0:T(8,128)(2,1)S(1)}, bf16[192,3...) fusion(bf16[192,3072]{1,0:T(8,128)(2,1)} %param.13, s32[]{:T(128)S(6)} %select_n.37, ...), kind=kLoop, calls=%fused_computation.88 | loop fusion | bytes 1769496 | tf_op jit(solution)/shard_map/dynamic_slice | solution.py:252
  6.6 4.4 %collective-permute-done.1 = bf16[192,768]{1,0:T(8,128)(2,1)S(1)} collective-permute-done((bf16[192,768]{1,0:T(8,128)(2,1)}, bf16[192,768]{1,0:T(8,128)(2,1)S(1)}, u32[]{:S(2)}, u32[]{:S(2)}) %collective-permute-start.1) | collective-permute-done | bytes 294944 | tf_op jit(solution)/shard_map/ppermute | solution.py:34
  10.9 1.5 %collective-permute-done.3 = bf16[192,768]{1,0:T(8,128)(2,1)S(1)} collective-permute-done((bf16[192,768]{1,0:T(8,128)(2,1)}, bf16[192,768]{1,0:T(8,128)(2,1)S(1)}, u32[]{:S(2)}, u32[]{:S(2)}) %collective-permute-start.3) | collective-permute-done | bytes 294944 | tf_op jit(solution)/shard_map/ppermute | solution.py:34
  12.4 0.2 multiply_convert_fusion
  12.7 0.1 pad_maximum_fusion.1
  12.7 0.4 collective-permute-start
  13.2 2.6 %collective-permute-start.4 = (bf16[200,768]{1,0:T(8,128)(2,1)S(1)}, bf16[200,768]{1,0:T(8,128)(2,1)S(1)}, u32[]{:S(2)}, u32[]{:S(2)}) collective-permute-start(bf16[200,768]{1,0:T(8,128)(2,1)S(1)} %get-tuple-element.38), channel_id=1, source_target_pairs={{0,24},{4,28},{8,16},{12,20},{16,8},{20,12},{24,0},{28,4},{1,25},{... | collective-permute-start | bytes 921608 | tf_op jit(solution)/shard_map/ppermute | solution.py:34
  15.8 0.6 collective-permute-start.5
  16.4 0.4 collective-permute-start.6
  16.8 1.7 %collective-permute-start.2 = (bf16[200,768]{1,0:T(8,128)(2,1)S(1)}, bf16[200,768]{1,0:T(8,128)(2,1)S(1)}, u32[]{:S(2)}, u32[]{:S(2)}) collective-permute-start(bf16[200,768]{1,0:T(8,128)(2,1)S(1)} %get-tuple-element.37), channel_id=1, source_target_pairs={{0,16},{4,20},{8,24},{12,28},{16,0},{20,4},{24,8},{28,12},{1,17},{... | collective-permute-start | bytes 921608 | tf_op jit(solution)/shard_map/ppermute | solution.py:34
  18.5 1.3 %fusion.28 = f32[384,768]{1,0:T(8,128)S(1)} fusion(bf16[192,768]{1,0:T(8,128)(2,1)S(1)} %get-tuple-element.43, bf16[192,3072]{1,0:T(8,128)(2,1)} %param.13, s32[]{:T(128)S(6)} %select_n.41), kind=kOutput, calls=%fused_computation.44 | convolution fusion | flops 113246208 | bytes 1622020 | tf_op jit(solution)/shard_map/dot_general | solution.py:27
  19.8 7.9 %collective-permute-done.5 = bf16[96,768]{1,0:T(8,128)(2,1)S(1)} collective-permute-done((bf16[96,768]{1,0:T(8,128)(2,1)S(1)}, bf16[96,768]{1,0:T(8,128)(2,1)S(1)}, u32[]{:S(2)}, u32[]{:S(2)}) %collective-permute-start.5) | collective-permute-done | bytes 147488 | tf_op jit(solution)/shard_map/ppermute | solution.py:34
  27.6 2.8 %collective-permute-done.6 = bf16[96,768]{1,0:T(8,128)(2,1)S(1)} collective-permute-done((bf16[96,768]{1,0:T(8,128)(2,1)S(1)}, bf16[96,768]{1,0:T(8,128)(2,1)S(1)}, u32[]{:S(2)}, u32[]{:S(2)}) %collective-permute-start.6) | collective-permute-done | bytes 147488 | tf_op jit(solution)/shard_map/ppermute | solution.py:34
  30.5 0.3 fusion.40
  30.8 0.3 fusion.42
  31.2 0.4 convolution_add_fusion.1
  31.5 1.3 %collective-permute-done.2 = bf16[200,768]{1,0:T(8,128)(2,1)S(1)} collective-permute-done((bf16[200,768]{1,0:T(8,128)(2,1)S(1)}, bf16[200,768]{1,0:T(8,128)(2,1)S(1)}, u32[]{:S(2)}, u32[]{:S(2)}) %collective-permute-start.2) | collective-permute-done | bytes 307232 | tf_op jit(solution)/shard_map/ppermute | solution.py:34
  32.9 0.4 fusion.1
  33.2 0.1 collective-permute-start.7
  33.3 1.3 %fusion.30 = f32[384,768]{1,0:T(8,128)S(1)} fusion(bf16[192,768]{1,0:T(8,128)(2,1)S(1)} %get-tuple-element.43, bf16[192,3072]{1,0:T(8,128)(2,1)} %param.13, s32[]{:T(128)S(6)} %select_n.16), kind=kOutput, calls=%fused_computation.46 | convolution fusion | flops 113246208 | bytes 1622020 | tf_op jit(solution)/shard_map/dot_general | solution.py:27
  34.6 0.3 fusion.46
  34.9 0.3 fusion.44
  35.3 0.4 convolution_add_fusion.3
  35.7 0.4 fusion.3.keep
  36.2 0.1 split_rows.1
  36.3 3.7 %collective-permute-start.10 = (bf16[96,768]{1,0:T(8,128)(2,1)S(1)}, bf16[96,768]{1,0:T(8,128)(2,1)S(1)}, u32[]{:S(2)}, u32[]{:S(2)}) collective-permute-start(bf16[96,768]{1,0:T(8,128)(2,1)S(1)} %get-tuple-element.20), channel_id=1, source_target_pairs={{0,3},{1,2},{2,1},{3,0},{4,7},{5,6},{6,5},{7,4},{8,11},{9,10},{10,... | collective-permute-start | bytes 442376 | tf_op jit(solution)/shard_map/ppermute | solution.py:39
  40.0 0.8 collective-permute-start.9
  40.8 4.1 %collective-permute-done.10.three = bf16[96,768]{1,0:T(8,128)(2,1)S(1)} collective-permute-done((bf16[96,768]{1,0:T(8,128)(2,1)S(1)}, bf16[96,768]{1,0:T(8,128)(2,1)S(1)}, u32[]{:S(2)}, u32[]{:S(2)}) %collective-permute-start.10) | collective-permute-done | bytes 147488 | tf_op jit(solution)/shard_map/ppermute | solution.py:39
  44.8 3.9 %collective-permute-done.8.one = bf16[96,768]{1,0:T(8,128)(2,1)S(1)} collective-permute-done((bf16[96,768]{1,0:T(8,128)(2,1)S(1)}, bf16[96,768]{1,0:T(8,128)(2,1)S(1)}, u32[]{:S(2)}, u32[]{:S(2)}) %collective-permute-start.8) | collective-permute-done | bytes 147488 | tf_op jit(solution)/shard_map/ppermute | solution.py:39
  48.7 4.4 %collective-permute-done.9.two = bf16[96,768]{1,0:T(8,128)(2,1)S(1)} collective-permute-done((bf16[96,768]{1,0:T(8,128)(2,1)S(1)}, bf16[96,768]{1,0:T(8,128)(2,1)S(1)}, u32[]{:S(2)}, u32[]{:S(2)}) %collective-permute-start.9) | collective-permute-done | bytes 147488 | tf_op jit(solution)/shard_map/ppermute | solution.py:39
  53.1 1.0 %update_rows.1 = (bf16[96,768]{1,0:T(8,128)(2,1)}, bf16[96,768]{1,0:T(8,128)(2,1)}, bf16[96,768]{1,0:T(8,128)(2,1)}, bf16[96,768]{1,0:T(8,128)(2,1)S(1)}) custom-call(s32[1]{0:T(128)} %bitcast.place, f32[96,768]{1,0:T(8,128)S(1)} %get-tuple-element.17.own, bf16[96,768]{1,0:T(8,128)(2,1)S(1)} %collective-permute-done.8.one, ...), custom_call_target="tpu_custom_call" | custom-call | flops 1474560 | bytes 2211840 | tf_op jit(solution)/shard_map/update_rows/pallas_call | solution.py:214
  54.1 15.7 %all_gather.3 = bf16[384,768]{1,0:T(8,128)(2,1)S(1)} all-gather(bf16[96,768]{1,0:T(8,128)(2,1)S(1)} %get-tuple-element.24), channel_id=1, replica_groups=mesh['fsdp'=8,'rep'=4] {'rep'}, dimensions={0}, use_global_device_ids=true | all-gather | bytes 737280 | tf_op jit(solution)/shard_map/all_gather | solution.py:298
  69.9 0.6 collective-permute-start.16
  70.5 1.4 %collective-permute-start.18 = (bf16[384,768]{1,0:T(8,128)(2,1)S(1)}, bf16[384,768]{1,0:T(8,128)(2,1)S(1)}, u32[]{:S(2)}, u32[]{:S(2)}) collective-permute-start(bf16[384,768]{1,0:T(8,128)(2,1)S(1)} %all_gather.3), channel_id=1, source_target_pairs={{0,16},{4,20},{8,24},{12,28},{16,0},{20,4},{24,8},{28,12},{1,17},{... | collective-permute-start | bytes 1769480 | tf_op jit(solution)/shard_map/ppermute | solution.py:34
  71.9 0.1 collective-permute-start.15
  72.0 0.5 collective-permute-start.11
  72.5 1.5 %collective-permute-done.11 = f32[768]{0:T(1024)S(1)} collective-permute-done((f32[768]{0:T(1024)S(1)}, f32[768]{0:T(1024)S(1)}, u32[]{:S(2)}, u32[]{:S(2)}) %collective-permute-start.11) | collective-permute-done | bytes 3104 | tf_op jit(solution)/shard_map/ppermute | solution.py:34
  74.0 1.1 %collective-permute-start.12 = (f32[768]{0:T(1024)S(1)}, f32[768]{0:T(1024)S(1)}, u32[]{:S(2)}, u32[]{:S(2)}) collective-permute-start(f32[768]{0:T(1024)S(1)} %add.145), channel_id=1, source_target_pairs={{0,1},{1,0},{2,3},{3,2},{4,5},{5,4},{6,7},{7,6},{8,9},{9,8},{10,11... | collective-permute-start | bytes 9224 | tf_op jit(solution)/shard_map/ppermute | solution.py:39
  75.1 2.6 %collective-permute-start.13 = (f32[768]{0:T(1024)S(1)}, f32[768]{0:T(1024)S(1)}, u32[]{:S(2)}, u32[]{:S(2)}) collective-permute-start(f32[768]{0:T(1024)S(1)} %add.145), channel_id=1, source_target_pairs={{0,2},{1,3},{2,0},{3,1},{4,6},{5,7},{6,4},{7,5},{8,10},{9,11},{10,... | collective-permute-start | bytes 9224 | tf_op jit(solution)/shard_map/ppermute | solution.py:39
  77.7 3.0 %collective-permute-start.14 = (f32[768]{0:T(1024)S(1)}, f32[768]{0:T(1024)S(1)}, u32[]{:S(2)}, u32[]{:S(2)}) collective-permute-start(f32[768]{0:T(1024)S(1)} %add.145), channel_id=1, source_target_pairs={{0,3},{1,2},{2,1},{3,0},{4,7},{5,6},{6,5},{7,4},{8,11},{9,10},{10,... | collective-permute-start | bytes 9224 | tf_op jit(solution)/shard_map/ppermute | solution.py:39
  80.7 2.4 %collective-permute-done.14 = f32[768]{0:T(1024)S(1)} collective-permute-done((f32[768]{0:T(1024)S(1)}, f32[768]{0:T(1024)S(1)}, u32[]{:S(2)}, u32[]{:S(2)}) %collective-permute-start.14) | collective-permute-done | bytes 3104 | tf_op jit(solution)/shard_map/ppermute | solution.py:39
  83.1 0.6 multiply_add_fusion
  83.7 1.0 %collective-permute-start.22 = (bf16[192,768]{1,0:T(8,128)(2,1)S(1)}, bf16[192,768]{1,0:T(8,128)(2,1)S(1)}, u32[]{:S(2)}, u32[]{:S(2)}) collective-permute-start(bf16[192,768]{1,0:T(8,128)(2,1)S(1)} %slice.90), channel_id=1, source_target_pairs={{0,8},{4,12},{8,0},{12,4},{16,24},{20,28},{24,16},{28,20},{1,9},{5... | collective-permute-start | bytes 884744 | tf_op jit(solution)/shard_map/ppermute | solution.py:34
  84.8 1.1 %collective-permute-start.20 = (bf16[192,768]{1,0:T(8,128)(2,1)S(1)}, bf16[192,768]{1,0:T(8,128)(2,1)S(1)}, u32[]{:S(2)}, u32[]{:S(2)}) collective-permute-start(bf16[192,768]{1,0:T(8,128)(2,1)S(1)} %slice.89), channel_id=1, source_target_pairs={{0,16},{4,20},{8,24},{12,28},{16,0},{20,4},{24,8},{28,12},{1,17},{... | collective-permute-start | bytes 884744 | tf_op jit(solution)/shard_map/ppermute | solution.py:34
  86.0 0.4 fusion.19
  86.3 1.4 %fusion.21 = f32[256,768]{1,0:T(8,128)S(1)} fusion(bf16[384,768]{1,0:T(8,128)(2,1)} %collective-permute-done.15, bf16[256,3072]{1,0:T(8,128)(2,1)S(1)} %copy-done, s32[]{:T(128)S(6)} %select_n.41), kind=kOutput, calls=%fused_computation.37 | convolution fusion | flops 150994944 | bytes 1572868 | tf_op jit(solution)/shard_map/dot_general | solution.py:314
  87.8 0.4 fusion.4
  88.1 0.4 fusion.16
  88.5 0.1 collective-permute-start.17
  88.6 0.5 collective-permute-start.19
  89.1 2.5 %collective-permute-done.20 = bf16[192,768]{1,0:T(8,128)(2,1)S(1)} collective-permute-done((bf16[192,768]{1,0:T(8,128)(2,1)S(1)}, bf16[192,768]{1,0:T(8,128)(2,1)S(1)}, u32[]{:S(2)}, u32[]{:S(2)}) %collective-permute-start.20) | collective-permute-done | bytes 294944 | tf_op jit(solution)/shard_map/ppermute | solution.py:34
  91.6 0.3 fusion.38
  91.9 0.6 collective-permute-start.23
  92.5 0.3 fusion.34
  92.8 0.4 collective-permute-done.21
  93.2 0.3 fusion.36
  93.5 0.2 collective-permute-done.23
  93.7 0.3 fusion.32
  94.0 0.4 fusion.5
  94.4 0.6 copy-done.5
  95.0 1.2 %fusion.12 = bf16[256,768]{1,0:T(8,128)(2,1)} fusion(f32[256,768]{1,0:T(8,128)S(1)} %fusion.32, f32[256,768]{1,0:T(8,128)S(1)} %fusion.34, f32[256,768]{1,0:T(8,128)S(1)} %fusion.36, f32[256,768]{1,0:T(8,128)S(1)} %fusion.38, f32[256,768]{1,0:T(8,128)S(1)} %fusion.5, bf16[384,768]{1,0:T(8,128)(2,1)S(1)} %collective-permute-done.19, ...), kind=kOutput, calls=%fused_computation.19 | convolution fusion | flops 152764416 | bytes 5509124 | tf_op jit(solution)/shard_map/dot_general | solution.py:314
  96.2 0.8 copy.23
  (50 shorter events, 0.3 us)
Async XLA Ops:
  0.6 85.3 %copy-start = (bf16[256,3072]{1,0:T(8,128)(2,1)S(1)}, bf16[256,3072]{1,0:T(8,128)(2,1)}, u32[]{:S(2)}) copy-start(bf16[256,3072]{1,0:T(8,128)(2,1)} %param.24) | copy-start | bytes 4718596
  0.7 11.7 %copy-start.6 = (bf16[192,768]{1,0:T(8,128)(2,1)S(1)}, bf16[192,768]{1,0:T(8,128)(2,1)}, u32[]{:S(2)}) copy-start(bf16[192,768]{1,0:T(8,128)(2,1)} %param.14) | copy-start | bytes 884740
  0.7 11.7 %copy-start.7 = (bf16[192,768]{1,0:T(8,128)(2,1)S(1)}, bf16[192,768]{1,0:T(8,128)(2,1)}, u32[]{:S(2)}) copy-start(bf16[192,768]{1,0:T(8,128)(2,1)} %param.15) | copy-start | bytes 884740
  0.7 11.7 %copy-start.8 = (f32[768]{0:T(1024)S(1)}, f32[768]{0:T(1024)}, u32[]{:S(2)}) copy-start(f32[768]{0:T(1024)} %param.16) | copy-start | bytes 9220
  0.7 10.2 %collective-permute-start.1 = (bf16[192,768]{1,0:T(8,128)(2,1)}, bf16[192,768]{1,0:T(8,128)(2,1)S(1)}, u32[]{:S(2)}, u32[]{:S(2)}) collective-permute-start(bf16[192,768]{1,0:T(8,128)(2,1)} %param.14), channel_id=1, source_target_pairs={{0,8},{4,12},{8,0},{12,4},{16,24},{20,28},{24,16},{28,20},{1,9},{5... | collective-permute-start | bytes 884744 | tf_op jit(solution)/shard_map/ppermute | solution.py:34
  3.7 8.7 %collective-permute-start.3 = (bf16[192,768]{1,0:T(8,128)(2,1)}, bf16[192,768]{1,0:T(8,128)(2,1)S(1)}, u32[]{:S(2)}, u32[]{:S(2)}) collective-permute-start(bf16[192,768]{1,0:T(8,128)(2,1)} %param.14), channel_id=1, source_target_pairs={{0,16},{4,20},{8,24},{12,28},{16,0},{20,4},{24,8},{28,12},{1,17},{... | collective-permute-start | bytes 884744 | tf_op jit(solution)/shard_map/ppermute | solution.py:34
  12.7 18.4 %collective-permute-start = (bf16[200,768]{1,0:T(8,128)(2,1)S(1)}, bf16[200,768]{1,0:T(8,128)(2,1)S(1)}, u32[]{:S(2)}, u32[]{:S(2)}) collective-permute-start(bf16[200,768]{1,0:T(8,128)(2,1)S(1)} %get-tuple-element.39), channel_id=1, source_target_pairs={{0,8},{4,12},{8,0},{12,4},{16,24},{20,28},{24,16},{28,20},{1,9},{5... | collective-permute-start | bytes 921608 | tf_op jit(solution)/shard_map/ppermute | solution.py:34
  13.2 17.3 %collective-permute-start.4 = (bf16[200,768]{1,0:T(8,128)(2,1)S(1)}, bf16[200,768]{1,0:T(8,128)(2,1)S(1)}, u32[]{:S(2)}, u32[]{:S(2)}) collective-permute-start(bf16[200,768]{1,0:T(8,128)(2,1)S(1)} %get-tuple-element.38), channel_id=1, source_target_pairs={{0,24},{4,28},{8,16},{12,20},{16,8},{20,12},{24,0},{28,4},{1,25},{... | collective-permute-start | bytes 921608 | tf_op jit(solution)/shard_map/ppermute | solution.py:34
  15.8 11.8 %collective-permute-start.5 = (bf16[96,768]{1,0:T(8,128)(2,1)S(1)}, bf16[96,768]{1,0:T(8,128)(2,1)S(1)}, u32[]{:S(2)}, u32[]{:S(2)}) collective-permute-start(bf16[96,768]{1,0:T(8,128)(2,1)S(1)} %slice.79), channel_id=1, source_target_pairs={{0,16},{4,20},{8,24},{12,28},{16,0},{20,4},{24,8},{28,12},{1,17},{... | collective-permute-start | bytes 442376 | tf_op jit(solution)/shard_map/ppermute | solution.py:34
  16.4 14.0 %collective-permute-start.6 = (bf16[96,768]{1,0:T(8,128)(2,1)S(1)}, bf16[96,768]{1,0:T(8,128)(2,1)S(1)}, u32[]{:S(2)}, u32[]{:S(2)}) collective-permute-start(bf16[96,768]{1,0:T(8,128)(2,1)S(1)} %slice.81), channel_id=1, source_target_pairs={{0,8},{4,12},{8,0},{12,4},{16,24},{20,28},{24,16},{28,20},{1,9},{5... | collective-permute-start | bytes 442376 | tf_op jit(solution)/shard_map/ppermute | solution.py:34
  16.8 16.0 %collective-permute-start.2 = (bf16[200,768]{1,0:T(8,128)(2,1)S(1)}, bf16[200,768]{1,0:T(8,128)(2,1)S(1)}, u32[]{:S(2)}, u32[]{:S(2)}) collective-permute-start(bf16[200,768]{1,0:T(8,128)(2,1)S(1)} %get-tuple-element.37), channel_id=1, source_target_pairs={{0,16},{4,20},{8,24},{12,28},{16,0},{20,4},{24,8},{28,12},{1,17},{... | collective-permute-start | bytes 921608 | tf_op jit(solution)/shard_map/ppermute | solution.py:34
  33.2 2.9 %collective-permute-start.7 = (f32[384,768]{1,0:T(8,128)S(1)}, f32[384,768]{1,0:T(8,128)S(1)}, u32[]{:S(2)}, u32[]{:S(2)}) collective-permute-start(f32[384,768]{1,0:T(8,128)S(1)} %fusion.1), channel_id=1, source_target_pairs={{0,4},{4,0},{8,12},{12,8},{16,20},{20,16},{24,28},{28,24},{1,5},{5... | collective-permute-start | bytes 3538952 | tf_op jit(solution)/shard_map/ppermute | solution.py:34
  36.2 16.9 %copy-start.1 = (bf16[384,768]{1,0:T(8,128)(2,1)S(1)}, bf16[384,768]{1,0:T(8,128)(2,1)}, u32[]{:S(2)}) copy-start(bf16[384,768]{1,0:T(8,128)(2,1)} %teacher.1) | copy-start | bytes 1769476
  36.2 16.9 %copy-start.2 = (bf16[96,768]{1,0:T(8,128)(2,1)S(1)}, bf16[96,768]{1,0:T(8,128)(2,1)}, u32[]{:S(2)}) copy-start(bf16[96,768]{1,0:T(8,128)(2,1)} %weight.1) | copy-start | bytes 442372
  36.2 16.9 %copy-start.3 = (bf16[96,768]{1,0:T(8,128)(2,1)S(1)}, bf16[96,768]{1,0:T(8,128)(2,1)}, u32[]{:S(2)}) copy-start(bf16[96,768]{1,0:T(8,128)(2,1)} %first.1) | copy-start | bytes 442372
  36.2 16.9 %copy-start.4 = (bf16[96,768]{1,0:T(8,128)(2,1)S(1)}, bf16[96,768]{1,0:T(8,128)(2,1)}, u32[]{:S(2)}) copy-start(bf16[96,768]{1,0:T(8,128)(2,1)} %second.1) | copy-start | bytes 442372
  36.3 8.6 %collective-permute-start.10 = (bf16[96,768]{1,0:T(8,128)(2,1)S(1)}, bf16[96,768]{1,0:T(8,128)(2,1)S(1)}, u32[]{:S(2)}, u32[]{:S(2)}) collective-permute-start(bf16[96,768]{1,0:T(8,128)(2,1)S(1)} %get-tuple-element.20), channel_id=1, source_target_pairs={{0,3},{1,2},{2,1},{3,0},{4,7},{5,6},{6,5},{7,4},{8,11},{9,10},{10,... | collective-permute-start | bytes 442376 | tf_op jit(solution)/shard_map/ppermute | solution.py:39
  40.0 8.8 %collective-permute-start.8 = (bf16[96,768]{1,0:T(8,128)(2,1)S(1)}, bf16[96,768]{1,0:T(8,128)(2,1)S(1)}, u32[]{:S(2)}, u32[]{:S(2)}) collective-permute-start(bf16[96,768]{1,0:T(8,128)(2,1)S(1)} %get-tuple-element.18), channel_id=1, source_target_pairs={{0,1},{1,0},{2,3},{3,2},{4,5},{5,4},{6,7},{7,6},{8,9},{9,8},{10,11... | collective-permute-start | bytes 442376 | tf_op jit(solution)/shard_map/ppermute | solution.py:39
  40.0 13.1 %collective-permute-start.9 = (bf16[96,768]{1,0:T(8,128)(2,1)S(1)}, bf16[96,768]{1,0:T(8,128)(2,1)S(1)}, u32[]{:S(2)}, u32[]{:S(2)}) collective-permute-start(bf16[96,768]{1,0:T(8,128)(2,1)S(1)} %get-tuple-element.19), channel_id=1, source_target_pairs={{0,2},{1,3},{2,0},{3,1},{4,6},{5,7},{6,4},{7,5},{8,10},{9,11},{10,... | collective-permute-start | bytes 442376 | tf_op jit(solution)/shard_map/ppermute | solution.py:39
  53.1 30.0 %copy-start.10 = (f32[768]{0:T(1024)S(1)}, f32[768]{0:T(1024)}, u32[]{:S(2)}) copy-start(f32[768]{0:T(1024)} %param.23) | copy-start | bytes 9220
  53.1 30.0 %copy-start.11 = (f32[768]{0:T(1024)S(1)}, f32[768]{0:T(1024)}, u32[]{:S(2)}) copy-start(f32[768]{0:T(1024)} %param.17) | copy-start | bytes 9220
  53.1 29.9 %copy-start.12 = (f32[768]{0:T(1024)S(1)}, f32[768]{0:T(1024)}, u32[]{:S(2)}) copy-start(f32[768]{0:T(1024)} %param.18) | copy-start | bytes 9220
  69.9 14.9 %collective-permute-start.16 = (bf16[384,768]{1,0:T(8,128)(2,1)S(1)}, bf16[384,768]{1,0:T(8,128)(2,1)S(1)}, u32[]{:S(2)}, u32[]{:S(2)}) collective-permute-start(bf16[384,768]{1,0:T(8,128)(2,1)S(1)} %all_gather.3), channel_id=1, source_target_pairs={{0,8},{4,12},{8,0},{12,4},{16,24},{20,28},{24,16},{28,20},{1,9},{5... | collective-permute-start | bytes 1769480 | tf_op jit(solution)/shard_map/ppermute | solution.py:34
  70.5 13.2 %collective-permute-start.18 = (bf16[384,768]{1,0:T(8,128)(2,1)S(1)}, bf16[384,768]{1,0:T(8,128)(2,1)S(1)}, u32[]{:S(2)}, u32[]{:S(2)}) collective-permute-start(bf16[384,768]{1,0:T(8,128)(2,1)S(1)} %all_gather.3), channel_id=1, source_target_pairs={{0,16},{4,20},{8,24},{12,28},{16,0},{20,4},{24,8},{28,12},{1,17},{... | collective-permute-start | bytes 1769480 | tf_op jit(solution)/shard_map/ppermute | solution.py:34
  71.9 14.4 %collective-permute-start.15 = (bf16[384,768]{1,0:T(8,128)(2,1)S(1)}, bf16[384,768]{1,0:T(8,128)(2,1)}, u32[]{:S(2)}, u32[]{:S(2)}) collective-permute-start(bf16[384,768]{1,0:T(8,128)(2,1)S(1)} %all_gather.3), channel_id=1, source_target_pairs={{0,4},{4,0},{8,12},{12,8},{16,20},{20,16},{24,28},{28,24},{1,5},{5... | collective-permute-start | bytes 1769480 | tf_op jit(solution)/shard_map/ppermute | solution.py:34
  72.0 2.0 %collective-permute-start.11 = (f32[768]{0:T(1024)S(1)}, f32[768]{0:T(1024)S(1)}, u32[]{:S(2)}, u32[]{:S(2)}) collective-permute-start(f32[768]{0:T(1024)S(1)} %add_add_fusion.1), channel_id=1, source_target_pairs={{0,4},{4,0},{8,12},{12,8},{16,20},{20,16},{24,28},{28,24},{1,5},{5... | collective-permute-start | bytes 9224 | tf_op jit(solution)/shard_map/ppermute | solution.py:34
  74.0 3.7 %collective-permute-start.12 = (f32[768]{0:T(1024)S(1)}, f32[768]{0:T(1024)S(1)}, u32[]{:S(2)}, u32[]{:S(2)}) collective-permute-start(f32[768]{0:T(1024)S(1)} %add.145), channel_id=1, source_target_pairs={{0,1},{1,0},{2,3},{3,2},{4,5},{5,4},{6,7},{7,6},{8,9},{9,8},{10,11... | collective-permute-start | bytes 9224 | tf_op jit(solution)/shard_map/ppermute | solution.py:39
  75.1 5.6 %collective-permute-start.13 = (f32[768]{0:T(1024)S(1)}, f32[768]{0:T(1024)S(1)}, u32[]{:S(2)}, u32[]{:S(2)}) collective-permute-start(f32[768]{0:T(1024)S(1)} %add.145), channel_id=1, source_target_pairs={{0,2},{1,3},{2,0},{3,1},{4,6},{5,7},{6,4},{7,5},{8,10},{9,11},{10,... | collective-permute-start | bytes 9224 | tf_op jit(solution)/shard_map/ppermute | solution.py:39
  77.7 5.4 %collective-permute-start.14 = (f32[768]{0:T(1024)S(1)}, f32[768]{0:T(1024)S(1)}, u32[]{:S(2)}, u32[]{:S(2)}) collective-permute-start(f32[768]{0:T(1024)S(1)} %add.145), channel_id=1, source_target_pairs={{0,3},{1,2},{2,1},{3,0},{4,7},{5,6},{6,5},{7,4},{8,11},{9,10},{10,... | collective-permute-start | bytes 9224 | tf_op jit(solution)/shard_map/ppermute | solution.py:39
  83.7 10.7 %copy-start.9 = (f32[768]{0:T(1024)}, f32[768]{0:T(1024)S(1)}, u32[]{:S(2)}) copy-start(f32[768]{0:T(1024)S(1)} %get-tuple-element.65) | copy-start | bytes 9220
  83.7 8.2 %collective-permute-start.22 = (bf16[192,768]{1,0:T(8,128)(2,1)S(1)}, bf16[192,768]{1,0:T(8,128)(2,1)S(1)}, u32[]{:S(2)}, u32[]{:S(2)}) collective-permute-start(bf16[192,768]{1,0:T(8,128)(2,1)S(1)} %slice.90), channel_id=1, source_target_pairs={{0,8},{4,12},{8,0},{12,4},{16,24},{20,28},{24,16},{28,20},{1,9},{5... | collective-permute-start | bytes 884744 | tf_op jit(solution)/shard_map/ppermute | solution.py:34
  84.8 6.8 %collective-permute-start.20 = (bf16[192,768]{1,0:T(8,128)(2,1)S(1)}, bf16[192,768]{1,0:T(8,128)(2,1)S(1)}, u32[]{:S(2)}, u32[]{:S(2)}) collective-permute-start(bf16[192,768]{1,0:T(8,128)(2,1)S(1)} %slice.89), channel_id=1, source_target_pairs={{0,16},{4,20},{8,24},{12,28},{16,0},{20,4},{24,8},{28,12},{1,17},{... | collective-permute-start | bytes 884744 | tf_op jit(solution)/shard_map/ppermute | solution.py:34
  88.5 5.5 %collective-permute-start.17 = (bf16[384,768]{1,0:T(8,128)(2,1)S(1)}, bf16[384,768]{1,0:T(8,128)(2,1)S(1)}, u32[]{:S(2)}, u32[]{:S(2)}) collective-permute-start(bf16[384,768]{1,0:T(8,128)(2,1)S(1)} %collective-permute-done.16), channel_id=1, source_target_pairs={{0,4},{4,0},{8,12},{12,8},{16,20},{20,16},{24,28},{28,24},{1,5},{5... | collective-permute-start | bytes 1769480 | tf_op jit(solution)/shard_map/ppermute | solution.py:34
  88.6 5.8 %collective-permute-start.19 = (bf16[384,768]{1,0:T(8,128)(2,1)S(1)}, bf16[384,768]{1,0:T(8,128)(2,1)S(1)}, u32[]{:S(2)}, u32[]{:S(2)}) collective-permute-start(bf16[384,768]{1,0:T(8,128)(2,1)S(1)} %collective-permute-done.18), channel_id=1, source_target_pairs={{0,4},{4,0},{8,12},{12,8},{16,20},{20,16},{24,28},{28,24},{1,5},{5... | collective-permute-start | bytes 1769480 | tf_op jit(solution)/shard_map/ppermute | solution.py:34
  91.6 1.6 %collective-permute-start.21 = (bf16[192,768]{1,0:T(8,128)(2,1)S(1)}, bf16[192,768]{1,0:T(8,128)(2,1)S(1)}, u32[]{:S(2)}, u32[]{:S(2)}) collective-permute-start(bf16[192,768]{1,0:T(8,128)(2,1)S(1)} %collective-permute-done.20), channel_id=1, source_target_pairs={{0,4},{4,0},{8,12},{12,8},{16,20},{20,16},{24,28},{28,24},{1,5},{5... | collective-permute-start | bytes 884744 | tf_op jit(solution)/shard_map/ppermute | solution.py:34
  91.9 1.8 %collective-permute-start.23 = (bf16[192,768]{1,0:T(8,128)(2,1)S(1)}, bf16[192,768]{1,0:T(8,128)(2,1)S(1)}, u32[]{:S(2)}, u32[]{:S(2)}) collective-permute-start(bf16[192,768]{1,0:T(8,128)(2,1)S(1)} %collective-permute-done.22), channel_id=1, source_target_pairs={{0,4},{4,0},{8,12},{12,8},{16,20},{20,16},{24,28},{28,24},{1,5},{5... | collective-permute-start | bytes 884744 | tf_op jit(solution)/shard_map/ppermute | solution.py:34
  94.0 1.0 %copy-start.5 = (bf16[256,768]{1,0:T(8,128)(2,1)S(1)}, bf16[256,768]{1,0:T(8,128)(2,1)}, u32[]{:S(2)}) copy-start(bf16[256,768]{1,0:T(8,128)(2,1)} %param.25) | copy-start | bytes 1179652

commit v3 on v2

--- a/solution.py
+++ b/solution.py
@@ -164,6 +164,38 @@
     rest = value - high
     mid = lax.reduce_precision(rest, 8, 7)
     return [high, mid, rest - mid]
+
+
+def fold_kernel(scale, *refs):
+    hidden, cotangent, (keep, send) = refs[:3], refs[3:6], refs[6:]
+    width = keep.shape[0]
+    tokens = cotangent[0].shape[0]
+    parts = [None, None]
+    for h, c in zip(hidden, cotangent):
+        scaled = (c[...].astype(jnp.float32) * scale[...]).astype(jnp.bfloat16)
+        for k in range(2):
+            term = token_fold(h[:tokens, k * width : (k + 1) * width], scaled)
+            parts[k] = term if parts[k] is None else parts[k] + term
+    keep[...] = parts[0]
+    send[...] = parts[1]
+
+
+def fold_tokens(scale, hidden, cotangent, width):
+    model_width = cotangent[0].shape[1]
+    total = jax.ShapeDtypeStruct((width, model_width), jnp.float32)
+    return pl.pallas_call(
+        fold_kernel,
+        out_shape=[total, total],
+        in_specs=[VMEM] * 7,
+        out_specs=[VMEM] * 2,
+        compiler_params=pltpu.CompilerParams(vmem_limit_bytes=24 * MIB),
+        cost_estimate=pl.CostEstimate(
+            flops=12 * cotangent[0].size * width,
+            bytes_accessed=4 * model_width * width + 12 * cotangent[0].size,
+            transcendentals=0,
+        ),
+        name="fold_tokens",
+    )(scale.reshape(1, -1), *hidden, *cotangent)
 
 
 def split_kernel(place, keep, arrived, own, *outgoing):
@@ -263,7 +295,6 @@
         hidden_of.append(swap_fsdp(jnp.concatenate([sent, tail], 0), flip))
     half = tokens // 2
     corner = [swap_fsdp(cot_x[:half], 4), swap_fsdp(cot_y[half:], 2)]
-    cotangents = [[out_cotangent], [cot_x], [cot_y], corner]
     for hidden in hidden_of[1:]:
         share = share + jnp.sum(hidden[tokens : tokens + 3].astype(jnp.float32), axis=0)
 
@@ -271,17 +302,11 @@
         scaled = (block.astype(jnp.float32) * layer_scale).astype(jnp.bfloat16)
         return lax.optimization_barrier(scaled)
 
-    keep = send = None
-    for hidden, blocks in zip(hidden_of, cotangents):
-        start = 0
-        for block in blocks:
-            stop = start + block.shape[0]
-            scaled = scale_it(block)
-            term = token_fold(hidden[start:stop, width:], scaled)
-            send = term if send is None else send + term
-            term = token_fold(hidden[start:stop, :width], scaled)
-            keep = term if keep is None else keep + term
-            start = stop
+    keep, send = fold_tokens(layer_scale, hidden_of[:3], [out_cotangent, cot_x, cot_y], width)
+    scaled = scale_it(jnp.concatenate(corner, 0))
+    far = hidden_of[3][:tokens]
+    send = send + token_fold(far[:, width:], scaled)
+    keep = keep + token_fold(far[:, :width], scaled)
     share = share + swap_fsdp(share, 1)
     own, *outgoing = split_rows(place, keep, swap_fsdp(send, 1), own_rows, rep_count)
     arrived = [swap_rep(piece, j + 1) for j, piece in enumerate(outgoing)]
@@ -305,22 +330,26 @@
     along_x, along_y = swap_fsdp(teacher_shard, 2), swap_fsdp(teacher_shard, 4)
     corner_x = swap_fsdp(along_x[:pair_rows], 4)
     corner_y = swap_fsdp(along_y[pair_rows:], 2)
-    held = [(teacher_shard, 0, 0), (along_x, 2, 0), (along_y, 4, 0)]
-    held += [(corner_x, 6, 0), (corner_y, 6, pair_rows)]
-    projected = None
-    for block, flip, start in held:
+
+    def terms(block, flip, start):
+        total = None
         for weights, f in ((block, flip), (swap_fsdp(block, 1), flip + 1)):
             units = columns(teacher_hidden, f)[:, start : start + block.shape[0]]
             term = jnp.dot(units, weights, preferred_element_type=jnp.float32)
-            projected = term if projected is None else projected + term
-    teacher_out = (teacher_input.astype(jnp.float32) + teacher_scale_new * projected).astype(
-        jnp.bfloat16
-    )
+            total = term if total is None else total + term
+        return total
+
+    near = terms(teacher_shard, 0, 0) + terms(along_x, 2, 0) + terms(along_y, 4, 0)
+    near = teacher_input.astype(jnp.float32) + teacher_scale_new * near
+    stored_shard = jnp.where(me >= 0, teacher_shard, jnp.zeros_like(teacher_shard))
+    near, stored_shard = lax.optimization_barrier((near, stored_shard))
+    far = terms(corner_x, 6, 0) + terms(corner_y, 6, pair_rows)
+    teacher_out = (near + teacher_scale_new * far).astype(jnp.bfloat16)
     return (
         new_weight,
         new_first,
         new_second,
-        teacher_shard,
+        stored_shard,
         scale_new,
         scale_first_new,
         scale_second_new,

time: 97.3 us -> 95.1 us (0.977)
  waiting for transfers between devices: 37.1 us -> 30.1 us
  other arithmetic: 1.05 us -> 7.23 us
  matrix products: 10.8 us -> 6.16 us
  Pallas kernels: 1.12 us -> 3.51 us
  starting transfers between devices: 27.4 us -> 29 us
    ppermute x18, waiting for transfers between devices: 22.4 us -> 17.2 us  [swap_fsdp(): return lax.ppermute(value, 'fsdp', [(i, i ^ flip) for i in range(count)])]
    dot_general x10 -> x2, matrix products: 5.43 us -> 1.63 us  [token_fold(): lax.dot_general(arrived, portion, (((0,), (0,)), ((), ())), preferred_ele...]
    reduce_sum x3, other arithmetic: 0.04 us -> 2.16 us  [block_shards(): jnp.sum(hidden[tokens:tokens + 3].astype(jnp.float32), axis=0)]
    ppermute x6, waiting for transfers between devices: 14.7 us -> 12.9 us  [swap_rep(): return lax.ppermute(value, 'rep', [(i, i ^ flip) for i in range(count)])]
    ppermute x18, starting transfers between devices: 16.2 us -> 17.7 us  [swap_fsdp(): return lax.ppermute(value, 'fsdp', [(i, i ^ flip) for i in range(count)])]
    add x0 -> x2, other arithmetic: none -> 1.41 us  [the longest x1 1.25 us: block_shards(): send = send + token_fold(far[:, width:], scaled)]
    pallas_call x1, Pallas kernels: 0.12 us -> 1.38 us  [split_rows(): pl.pallas_call(split_kernel, out_shape=[jax.ShapeDtypeStruct((rows, width...]
    reduce_sum x0 -> x1, other arithmetic: none -> 1.14 us  [block_shards(): jnp.sum(out_cotangent.astype(jnp.float32) * student_branch.astype(jnp.flo...]
  transfers between devices with their start and end apart: 24 -> 24, of which waited for: 14 -> 13; matrix products, arithmetic and copies ran while one was open for 12% -> 13% of each run, Pallas kernels for 0% -> 1%
where the time goes in v3:
time: 95.1 us; the launch traced here: 94.7 us
  waiting for transfers between devices  30.1 us (32%)
  starting transfers between devices  29 us (30%)
  blocking collectives  15.5 us (16%)
  other arithmetic  7.23 us (8%)
  matrix products  6.16 us (6%)
  Pallas kernels  3.51 us (4%)
  local copies, waits for them, and re-layouts  2.23 us (2%)
  between operations  1.03 us (1%)
    ppermute x18, starting transfers between devices, swap_fsdp(): return lax.ppermute(value, 'fsdp', [(i, i ^ flip) for i in range(count)])  17.7 us
    ppermute x18, waiting for transfers between devices, swap_fsdp(): return lax.ppermute(value, 'fsdp', [(i, i ^ flip) for i in range(count)])  17.2 us
    all_gather x1, blocking collectives, block_shards(): teacher_shard = lax.all_gather(sent_rows, 'rep', axis=0, tiled=True)  15.5 us
    ppermute x6, waiting for transfers between devices, swap_rep(): return lax.ppermute(value, 'rep', [(i, i ^ flip) for i in range(count)])  12.9 us
    ppermute x6, starting transfers between devices, swap_rep(): return lax.ppermute(value, 'rep', [(i, i ^ flip) for i in range(count)])  11.3 us
    dot_general x10, matrix products, terms(): term = jnp.dot(units, weights, preferred_element_type=jnp.float32)  4.53 us
    reduce_sum x3, other arithmetic, block_shards(): jnp.sum(hidden[tokens:tokens + 3].astype(jnp.float32), axis=0)  2.16 us
  transfers between devices with their start and end apart: 24, of which 13 were waited for; matrix products, arithmetic and copies ran while one was open for 13% of the time, Pallas kernels for 1%

profile of v3, /device:TPU:0, one launch (start us, length us, event | category | flops | bytes accessed | tf_op | source)
XLA Modules:
  0.0 94.7 jit_solution(16557740342362645566)
XLA Ops:
  0.6 0.0 copy-start
  0.7 3.0 %collective-permute-start.2 = (bf16[192,768]{1,0:T(8,128)(2,1)}, bf16[192,768]{1,0:T(8,128)(2,1)S(1)}, u32[]{:S(2)}, u32[]{:S(2)}) collective-permute-start(bf16[192,768]{1,0:T(8,128)(2,1)} %refs_3_.1), channel_id=1, source_target_pairs={{0,8},{4,12},{8,0},{12,4},{16,24},{20,28},{24,16},{28,20},{1,9},{5... | collective-permute-start | bytes 884744 | tf_op jit(solution)/shard_map/ppermute | solution.py:34
  3.7 1.5 %collective-permute-start.3 = (bf16[192,768]{1,0:T(8,128)(2,1)}, bf16[192,768]{1,0:T(8,128)(2,1)S(1)}, u32[]{:S(2)}, u32[]{:S(2)}) collective-permute-start(bf16[192,768]{1,0:T(8,128)(2,1)} %refs_3_.1), channel_id=1, source_target_pairs={{0,16},{4,20},{8,24},{12,28},{16,0},{20,4},{24,8},{28,12},{1,17},{... | collective-permute-start | bytes 884744 | tf_op jit(solution)/shard_map/ppermute | solution.py:34
  5.2 1.1 %multiply_reduce_fusion = f32[768]{0:T(1024)S(1)} fusion(bf16[192,768]{1,0:T(8,128)(2,1)} %param.15, bf16[192,768]{1,0:T(8,128)(2,1)} %refs_3_.1), kind=kLoop, calls=%fused_computation.13 | loop fusion | flops 589056 | bytes 592896 | tf_op jit(solution)/shard_map/reduce_sum | solution.py:287
  6.4 1.5 %constant_dynamic-slice_fusion.1 = (bf16[192,384]{1,0:T(8,128)(2,1)S(1)}, bf16[192,384]{1,0:T(8,128)(2,1)S(1)}, bf16[192,384]{1,0:T(8,128)(2,1)S(1)}, bf16[192,3...) fusion(bf16[192,3072]{1,0:T(8,128)(2,1)} %param.13, ...), kind=kLoop, calls=%fused_computation.59 | loop fusion | bytes 2359328 | tf_op jit(solution)/shard_map/dynamic_slice | solution.py:284
  7.9 0.0 copy-start.10
  7.9 0.1 pad_maximum_fusion
  8.0 0.6 collective-permute-start
  8.6 0.1 collective-permute-start.1
  8.7 2.9 %collective-permute-start.4 = (bf16[200,768]{1,0:T(8,128)(2,1)S(1)}, bf16[200,768]{1,0:T(8,128)(2,1)S(1)}, u32[]{:S(2)}, u32[]{:S(2)}) collective-permute-start(bf16[200,768]{1,0:T(8,128)(2,1)S(1)} %get-tuple-element.45), channel_id=1, source_target_pairs={{0,24},{4,28},{8,16},{12,20},{16,8},{20,12},{24,0},{28,4},{1,25},{... | collective-permute-start | bytes 921608 | tf_op jit(solution)/shard_map/ppermute | solution.py:34
  11.6 0.1 collective-permute-done.2.refs_4_
  11.7 2.1 %collective-permute-start.5 = (bf16[96,768]{1,0:T(8,128)(2,1)S(1)}, bf16[96,768]{1,0:T(8,128)(2,1)S(1)}, u32[]{:S(2)}, u32[]{:S(2)}) collective-permute-start(bf16[96,768]{1,0:T(8,128)(2,1)S(1)} %slice.56), channel_id=1, source_target_pairs={{0,16},{4,20},{8,24},{12,28},{16,0},{20,4},{24,8},{28,12},{1,17},{... | collective-permute-start | bytes 442376 | tf_op jit(solution)/shard_map/ppermute | solution.py:34
  13.9 1.6 %collective-permute-start.6 = (bf16[96,768]{1,0:T(8,128)(2,1)S(1)}, bf16[96,768]{1,0:T(8,128)(2,1)S(1)}, u32[]{:S(2)}, u32[]{:S(2)}) collective-permute-start(bf16[96,768]{1,0:T(8,128)(2,1)S(1)} %slice.57), channel_id=1, source_target_pairs={{0,8},{4,12},{8,0},{12,4},{16,24},{20,28},{24,16},{28,20},{1,9},{5... | collective-permute-start | bytes 442376 | tf_op jit(solution)/shard_map/ppermute | solution.py:34
  15.5 2.8 %collective-permute-done.refs_1_ = bf16[200,768]{1,0:T(8,128)(2,1)S(1)} collective-permute-done((bf16[200,768]{1,0:T(8,128)(2,1)S(1)}, bf16[200,768]{1,0:T(8,128)(2,1)S(1)}, u32[]{:S(2)}, u32[]{:S(2)}) %collective-permute-start) | collective-permute-done | bytes 307232 | tf_op jit(solution)/shard_map/ppermute | solution.py:34
  18.3 8.7 %collective-permute-done.1.refs_2_ = bf16[200,768]{1,0:T(8,128)(2,1)S(1)} collective-permute-done((bf16[200,768]{1,0:T(8,128)(2,1)S(1)}, bf16[200,768]{1,0:T(8,128)(2,1)S(1)}, u32[]{:S(2)}, u32[]{:S(2)}) %collective-permute-start.1) | collective-permute-done | bytes 307232 | tf_op jit(solution)/shard_map/ppermute | solution.py:34
  27.0 1.1 %fold_tokens.1 = (f32[384,768]{1,0:T(8,128)S(1)}, f32[384,768]{1,0:T(8,128)S(1)}) custom-call(f32[1,768]{1,0:T(1,128)S(1)} %reshape.51.scale, bf16[192,768]{1,0:T(8,128)(2,1)S(1)} %pad_maximum_fusion.3.refs_0_, bf16[200,768]{1,0:T(8,128)(2,1)S(1)} %collective-permute-done.refs_1_, bf16[200,768]{1,0:T(8,128)(2,1)S(1)} %collective-permute-done.1.refs_2_, ...), custom_call_target="tpu_custom_call" | custom-call | flops 679477248 | bytes 2949120 | tf_op jit(solution)/shard_map/fold_tokens/pallas_call | solution.py:186
  28.1 0.6 collective-permute-done.5
  28.7 0.1 multiply_convert_fusion
  28.7 0.4 fusion.15
  29.1 1.3 %add.117 = f32[384,768]{1,0:T(8,128)} add(f32[384,768]{1,0:T(8,128)S(1)} %get-tuple-element.22, f32[384,768]{1,0:T(8,128)S(1)} %fusion.15) | non-fusion elementwise | flops 294912 | bytes 3538944 | tf_op jit(solution)/shard_map/add | solution.py:308
  30.4 0.7 convert_reduce_fusion
  31.1 1.3 %fusion.17 = f32[384,768]{1,0:T(8,128)S(1)} fusion(bf16[192,768]{1,0:T(8,128)(2,1)S(1)} %multiply_convert_fusion, bf16[200,768]{1,0:T(8,128)(2,1)} %copy-done.9), kind=kOutput, calls=%fused_computation.30 | convolution fusion | flops 113246208 | bytes 1622016 | tf_op jit(solution)/shard_map/dot_general | solution.py:27
  32.4 0.2 add.116.keep
  32.6 1.0 %collective-permute-done.7.arrived = f32[384,768]{1,0:T(8,128)} collective-permute-done((f32[384,768]{1,0:T(8,128)}, f32[384,768]{1,0:T(8,128)}, u32[]{:S(2)}, u32[]{:S(2)}) %collective-permute-start.7) | collective-permute-done | bytes 1179680 | tf_op jit(solution)/shard_map/ppermute | solution.py:34
  33.6 1.4 %split_rows.1 = (f32[96,768]{1,0:T(8,128)S(1)}, bf16[96,768]{1,0:T(8,128)(2,1)S(1)}, bf16[96,768]{1,0:T(8,128)(2,1)S(1)}, bf16[96,768]{1,0:T(8,128)(2,1)S(1)}) custom-call(s32[1]{0:T(128)} %bitcast.place, f32[384,768]{1,0:T(8,128)S(1)} %add.116.keep, f32[384,768]{1,0:T(8,128)} %collective-permute-done.7.arrived), custom_call_target="tpu_custom_call" | custom-call | flops 294912 | bytes 3244032 | tf_op jit(solution)/shard_map/split_rows/pallas_call | solution.py:214
  35.0 3.7 %collective-permute-start.10 = (bf16[96,768]{1,0:T(8,128)(2,1)S(1)}, bf16[96,768]{1,0:T(8,128)(2,1)S(1)}, u32[]{:S(2)}, u32[]{:S(2)}) collective-permute-start(bf16[96,768]{1,0:T(8,128)(2,1)S(1)} %get-tuple-element.26), channel_id=1, source_target_pairs={{0,3},{1,2},{2,1},{3,0},{4,7},{5,6},{6,5},{7,4},{8,11},{9,10},{10,... | collective-permute-start | bytes 442376 | tf_op jit(solution)/shard_map/ppermute | solution.py:39
  38.7 0.8 collective-permute-start.9
  39.5 0.7 convert_reduce_fusion.1
  40.2 0.7 convert_reduce_fusion.2
  40.9 2.7 %collective-permute-done.10.three = bf16[96,768]{1,0:T(8,128)(2,1)S(1)} collective-permute-done((bf16[96,768]{1,0:T(8,128)(2,1)S(1)}, bf16[96,768]{1,0:T(8,128)(2,1)S(1)}, u32[]{:S(2)}, u32[]{:S(2)}) %collective-permute-start.10) | collective-permute-done | bytes 147488 | tf_op jit(solution)/shard_map/ppermute | solution.py:39
  43.6 3.5 %collective-permute-done.8.one = bf16[96,768]{1,0:T(8,128)(2,1)S(1)} collective-permute-done((bf16[96,768]{1,0:T(8,128)(2,1)S(1)}, bf16[96,768]{1,0:T(8,128)(2,1)S(1)}, u32[]{:S(2)}, u32[]{:S(2)}) %collective-permute-start.8) | collective-permute-done | bytes 147488 | tf_op jit(solution)/shard_map/ppermute | solution.py:39
  47.1 4.4 %collective-permute-done.9.two = bf16[96,768]{1,0:T(8,128)(2,1)S(1)} collective-permute-done((bf16[96,768]{1,0:T(8,128)(2,1)S(1)}, bf16[96,768]{1,0:T(8,128)(2,1)S(1)}, u32[]{:S(2)}, u32[]{:S(2)}) %collective-permute-start.9) | collective-permute-done | bytes 147488 | tf_op jit(solution)/shard_map/ppermute | solution.py:39
  51.5 1.0 %update_rows.1 = (bf16[96,768]{1,0:T(8,128)(2,1)}, bf16[96,768]{1,0:T(8,128)(2,1)}, bf16[96,768]{1,0:T(8,128)(2,1)}, bf16[96,768]{1,0:T(8,128)(2,1)S(1)}) custom-call(s32[1]{0:T(128)} %bitcast.place, f32[96,768]{1,0:T(8,128)S(1)} %get-tuple-element.23.own, bf16[96,768]{1,0:T(8,128)(2,1)S(1)} %collective-permute-done.8.one, ...), custom_call_target="tpu_custom_call" | custom-call | flops 1474560 | bytes 2211840 | tf_op jit(solution)/shard_map/update_rows/pallas_call | solution.py:246
  52.5 15.5 %all_gather.3 = bf16[384,768]{1,0:T(8,128)(2,1)S(1)} all-gather(bf16[96,768]{1,0:T(8,128)(2,1)S(1)} %get-tuple-element.30), channel_id=1, replica_groups=mesh['fsdp'=8,'rep'=4] {'rep'}, dimensions={0}, use_global_device_ids=true | all-gather | bytes 737280 | tf_op jit(solution)/shard_map/all_gather | solution.py:323
  67.9 0.5 collective-permute-start.16
  68.5 1.5 %collective-permute-start.18 = (bf16[384,768]{1,0:T(8,128)(2,1)S(1)}, bf16[384,768]{1,0:T(8,128)(2,1)S(1)}, u32[]{:S(2)}, u32[]{:S(2)}) collective-permute-start(bf16[384,768]{1,0:T(8,128)(2,1)S(1)} %all_gather.3), channel_id=1, source_target_pairs={{0,16},{4,20},{8,24},{12,28},{16,0},{20,4},{24,8},{28,12},{1,17},{... | collective-permute-start | bytes 1769480 | tf_op jit(solution)/shard_map/ppermute | solution.py:34
  70.0 0.5 collective-permute-start.11
  70.5 1.3 %collective-permute-done.11 = f32[768]{0:T(1024)S(1)} collective-permute-done((f32[768]{0:T(1024)S(1)}, f32[768]{0:T(1024)S(1)}, u32[]{:S(2)}, u32[]{:S(2)}) %collective-permute-start.11) | collective-permute-done | bytes 3104 | tf_op jit(solution)/shard_map/ppermute | solution.py:34
  71.8 1.3 %collective-permute-start.12 = (f32[768]{0:T(1024)S(1)}, f32[768]{0:T(1024)S(1)}, u32[]{:S(2)}, u32[]{:S(2)}) collective-permute-start(f32[768]{0:T(1024)S(1)} %add.121), channel_id=1, source_target_pairs={{0,1},{1,0},{2,3},{3,2},{4,5},{5,4},{6,7},{7,6},{8,9},{9,8},{10,11... | collective-permute-start | bytes 9224 | tf_op jit(solution)/shard_map/ppermute | solution.py:39
  73.1 2.6 %collective-permute-start.13 = (f32[768]{0:T(1024)S(1)}, f32[768]{0:T(1024)S(1)}, u32[]{:S(2)}, u32[]{:S(2)}) collective-permute-start(f32[768]{0:T(1024)S(1)} %add.121), channel_id=1, source_target_pairs={{0,2},{1,3},{2,0},{3,1},{4,6},{5,7},{6,4},{7,5},{8,10},{9,11},{10,... | collective-permute-start | bytes 9224 | tf_op jit(solution)/shard_map/ppermute | solution.py:39
  75.7 3.0 %collective-permute-start.14 = (f32[768]{0:T(1024)S(1)}, f32[768]{0:T(1024)S(1)}, u32[]{:S(2)}, u32[]{:S(2)}) collective-permute-start(f32[768]{0:T(1024)S(1)} %add.121), channel_id=1, source_target_pairs={{0,3},{1,2},{2,1},{3,0},{4,7},{5,6},{6,5},{7,4},{8,11},{9,10},{10,... | collective-permute-start | bytes 9224 | tf_op jit(solution)/shard_map/ppermute | solution.py:39
  78.7 2.4 %collective-permute-done.14 = f32[768]{0:T(1024)S(1)} collective-permute-done((f32[768]{0:T(1024)S(1)}, f32[768]{0:T(1024)S(1)}, u32[]{:S(2)}, u32[]{:S(2)}) %collective-permute-start.14) | collective-permute-done | bytes 3104 | tf_op jit(solution)/shard_map/ppermute | solution.py:39
  81.1 0.6 multiply_add_fusion
  81.7 0.9 broadcast_select_fusion
  82.6 0.6 collective-permute-start.20
  83.2 1.6 %collective-permute-start.22 = (bf16[192,768]{1,0:T(8,128)(2,1)S(1)}, bf16[192,768]{1,0:T(8,128)(2,1)S(1)}, u32[]{:S(2)}, u32[]{:S(2)}) collective-permute-start(bf16[192,768]{1,0:T(8,128)(2,1)S(1)} %slice.63), channel_id=1, source_target_pairs={{0,8},{4,12},{8,0},{12,4},{16,24},{20,28},{24,16},{28,20},{1,9},{5... | collective-permute-start | bytes 884744 | tf_op jit(solution)/shard_map/ppermute | solution.py:34
  84.7 1.4 %fusion.12 = f32[256,768]{1,0:T(8,128)S(1)} fusion(bf16[384,768]{1,0:T(8,128)(2,1)} %collective-permute-done.15, bf16[256,3072]{1,0:T(8,128)(2,1)S(1)} %copy-done, s32[]{:T(128)S(6)} %select_n.43), kind=kOutput, calls=%fused_computation.25 | convolution fusion | flops 150994944 | bytes 1572868 | tf_op jit(solution)/shard_map/dot_general | solution.py:338
  86.2 0.4 convolution_add_fusion.2
  86.5 0.4 fusion.7
  86.9 0.1 collective-permute-start.19
  87.0 0.4 fusion.10
  87.3 0.6 collective-permute-start.17
  87.9 2.1 %collective-permute-done.20 = bf16[192,768]{1,0:T(8,128)(2,1)S(1)} collective-permute-done((bf16[192,768]{1,0:T(8,128)(2,1)S(1)}, bf16[192,768]{1,0:T(8,128)(2,1)S(1)}, u32[]{:S(2)}, u32[]{:S(2)}) %collective-permute-start.20) | collective-permute-done | bytes 294944 | tf_op jit(solution)/shard_map/ppermute | solution.py:34
  90.0 0.3 fusion.23
  90.3 0.6 collective-permute-start.23
  90.9 0.3 fusion.20
  91.2 0.4 collective-permute-done.21
  91.6 0.3 convolution_add_fusion.4
  91.9 0.2 collective-permute-done.23
  92.1 0.3 fusion.5
  92.5 0.4 convolution_add_fusion
  92.9 0.6 copy-done.8
  93.5 0.4 fusion.3
  93.9 0.8 add_convert_fusion
  (52 shorter events, 0.2 us)
Async XLA Ops:
  0.6 84.1 %copy-start = (bf16[256,3072]{1,0:T(8,128)(2,1)S(1)}, bf16[256,3072]{1,0:T(8,128)(2,1)}, u32[]{:S(2)}) copy-start(bf16[256,3072]{1,0:T(8,128)(2,1)} %param.24) | copy-start | bytes 4718596
  0.7 11.1 %collective-permute-start.2 = (bf16[192,768]{1,0:T(8,128)(2,1)}, bf16[192,768]{1,0:T(8,128)(2,1)S(1)}, u32[]{:S(2)}, u32[]{:S(2)}) collective-permute-start(bf16[192,768]{1,0:T(8,128)(2,1)} %refs_3_.1), channel_id=1, source_target_pairs={{0,8},{4,12},{8,0},{12,4},{16,24},{20,28},{24,16},{28,20},{1,9},{5... | collective-permute-start | bytes 884744 | tf_op jit(solution)/shard_map/ppermute | solution.py:34
  3.7 10.2 %collective-permute-start.3 = (bf16[192,768]{1,0:T(8,128)(2,1)}, bf16[192,768]{1,0:T(8,128)(2,1)S(1)}, u32[]{:S(2)}, u32[]{:S(2)}) collective-permute-start(bf16[192,768]{1,0:T(8,128)(2,1)} %refs_3_.1), channel_id=1, source_target_pairs={{0,16},{4,20},{8,24},{12,28},{16,0},{20,4},{24,8},{28,12},{1,17},{... | collective-permute-start | bytes 884744 | tf_op jit(solution)/shard_map/ppermute | solution.py:34
  7.9 7.6 %copy-start.10 = (f32[768]{0:T(1024)S(1)}, f32[768]{0:T(1024)}, u32[]{:S(2)}) copy-start(f32[768]{0:T(1024)} %param.16) | copy-start | bytes 9220
  7.9 19.1 %copy-start.2 = (bf16[192,768]{1,0:T(8,128)(2,1)S(1)}, bf16[192,768]{1,0:T(8,128)(2,1)}, u32[]{:S(2)}) copy-start(bf16[192,768]{1,0:T(8,128)(2,1)} %refs_3_.1) | copy-start | bytes 884740
  8.0 10.3 %collective-permute-start = (bf16[200,768]{1,0:T(8,128)(2,1)S(1)}, bf16[200,768]{1,0:T(8,128)(2,1)S(1)}, u32[]{:S(2)}, u32[]{:S(2)}) collective-permute-start(bf16[200,768]{1,0:T(8,128)(2,1)S(1)} %get-tuple-element.47), channel_id=1, source_target_pairs={{0,8},{4,12},{8,0},{12,4},{16,24},{20,28},{24,16},{28,20},{1,9},{5... | collective-permute-start | bytes 921608 | tf_op jit(solution)/shard_map/ppermute | solution.py:34
  8.6 18.3 %collective-permute-start.1 = (bf16[200,768]{1,0:T(8,128)(2,1)S(1)}, bf16[200,768]{1,0:T(8,128)(2,1)S(1)}, u32[]{:S(2)}, u32[]{:S(2)}) collective-permute-start(bf16[200,768]{1,0:T(8,128)(2,1)S(1)} %get-tuple-element.46), channel_id=1, source_target_pairs={{0,16},{4,20},{8,24},{12,28},{16,0},{20,4},{24,8},{28,12},{1,17},{... | collective-permute-start | bytes 921608 | tf_op jit(solution)/shard_map/ppermute | solution.py:34
  8.7 20.1 %collective-permute-start.4 = (bf16[200,768]{1,0:T(8,128)(2,1)S(1)}, bf16[200,768]{1,0:T(8,128)(2,1)S(1)}, u32[]{:S(2)}, u32[]{:S(2)}) collective-permute-start(bf16[200,768]{1,0:T(8,128)(2,1)S(1)} %get-tuple-element.45), channel_id=1, source_target_pairs={{0,24},{4,28},{8,16},{12,20},{16,8},{20,12},{24,0},{28,4},{1,25},{... | collective-permute-start | bytes 921608 | tf_op jit(solution)/shard_map/ppermute | solution.py:34
  11.7 16.9 %collective-permute-start.5 = (bf16[96,768]{1,0:T(8,128)(2,1)S(1)}, bf16[96,768]{1,0:T(8,128)(2,1)S(1)}, u32[]{:S(2)}, u32[]{:S(2)}) collective-permute-start(bf16[96,768]{1,0:T(8,128)(2,1)S(1)} %slice.56), channel_id=1, source_target_pairs={{0,16},{4,20},{8,24},{12,28},{16,0},{20,4},{24,8},{28,12},{1,17},{... | collective-permute-start | bytes 442376 | tf_op jit(solution)/shard_map/ppermute | solution.py:34
  13.9 14.8 %collective-permute-start.6 = (bf16[96,768]{1,0:T(8,128)(2,1)S(1)}, bf16[96,768]{1,0:T(8,128)(2,1)S(1)}, u32[]{:S(2)}, u32[]{:S(2)}) collective-permute-start(bf16[96,768]{1,0:T(8,128)(2,1)S(1)} %slice.57), channel_id=1, source_target_pairs={{0,8},{4,12},{8,0},{12,4},{16,24},{20,28},{24,16},{28,20},{1,9},{5... | collective-permute-start | bytes 442376 | tf_op jit(solution)/shard_map/ppermute | solution.py:34
  18.3 10.8 %copy-start.6 = (bf16[200,768]{1,0:T(8,128)(2,1)}, bf16[200,768]{1,0:T(8,128)(2,1)S(1)}, u32[]{:S(2)}) copy-start(bf16[200,768]{1,0:T(8,128)(2,1)S(1)} %collective-permute-done.refs_1_) | copy-start | bytes 921604
  27.0 2.2 %copy-start.7 = (bf16[200,768]{1,0:T(8,128)(2,1)}, bf16[200,768]{1,0:T(8,128)(2,1)S(1)}, u32[]{:S(2)}) copy-start(bf16[200,768]{1,0:T(8,128)(2,1)S(1)} %collective-permute-done.1.refs_2_) | copy-start | bytes 921604
  28.7 1.7 %copy-start.9 = (bf16[200,768]{1,0:T(8,128)(2,1)}, bf16[200,768]{1,0:T(8,128)(2,1)S(1)}, u32[]{:S(2)}) copy-start(bf16[200,768]{1,0:T(8,128)(2,1)S(1)} %collective-permute-done.4) | copy-start | bytes 921604
  30.4 3.2 %collective-permute-start.7 = (f32[384,768]{1,0:T(8,128)}, f32[384,768]{1,0:T(8,128)}, u32[]{:S(2)}, u32[]{:S(2)}) collective-permute-start(f32[384,768]{1,0:T(8,128)} %add.117), channel_id=1, source_target_pairs={{0,4},{4,0},{8,12},{12,8},{16,20},{20,16},{24,28},{28,24},{1,5},{5... | collective-permute-start | bytes 3538952 | tf_op jit(solution)/shard_map/ppermute | solution.py:34
  32.6 18.9 %copy-start.1 = (bf16[384,768]{1,0:T(8,128)(2,1)S(1)}, bf16[384,768]{1,0:T(8,128)(2,1)}, u32[]{:S(2)}) copy-start(bf16[384,768]{1,0:T(8,128)(2,1)} %teacher.1) | copy-start | bytes 1769476
  32.6 18.9 %copy-start.3 = (bf16[96,768]{1,0:T(8,128)(2,1)S(1)}, bf16[96,768]{1,0:T(8,128)(2,1)}, u32[]{:S(2)}) copy-start(bf16[96,768]{1,0:T(8,128)(2,1)} %weight.1) | copy-start | bytes 442372
  32.6 18.9 %copy-start.4 = (bf16[96,768]{1,0:T(8,128)(2,1)S(1)}, bf16[96,768]{1,0:T(8,128)(2,1)}, u32[]{:S(2)}) copy-start(bf16[96,768]{1,0:T(8,128)(2,1)} %first.1) | copy-start | bytes 442372
  32.6 18.9 %copy-start.5 = (bf16[96,768]{1,0:T(8,128)(2,1)S(1)}, bf16[96,768]{1,0:T(8,128)(2,1)}, u32[]{:S(2)}) copy-start(bf16[96,768]{1,0:T(8,128)(2,1)} %second.1) | copy-start | bytes 442372
  35.0 46.1 %copy-start.12 = (f32[768]{0:T(1024)S(1)}, f32[768]{0:T(1024)}, u32[]{:S(2)}) copy-start(f32[768]{0:T(1024)} %param.23) | copy-start | bytes 9220
  35.0 46.1 %copy-start.13 = (f32[768]{0:T(1024)S(1)}, f32[768]{0:T(1024)}, u32[]{:S(2)}) copy-start(f32[768]{0:T(1024)} %param.17) | copy-start | bytes 9220
  35.0 46.1 %copy-start.14 = (f32[768]{0:T(1024)S(1)}, f32[768]{0:T(1024)}, u32[]{:S(2)}) copy-start(f32[768]{0:T(1024)} %param.18) | copy-start | bytes 9220
  35.0 8.6 %collective-permute-start.10 = (bf16[96,768]{1,0:T(8,128)(2,1)S(1)}, bf16[96,768]{1,0:T(8,128)(2,1)S(1)}, u32[]{:S(2)}, u32[]{:S(2)}) collective-permute-start(bf16[96,768]{1,0:T(8,128)(2,1)S(1)} %get-tuple-element.26), channel_id=1, source_target_pairs={{0,3},{1,2},{2,1},{3,0},{4,7},{5,6},{6,5},{7,4},{8,11},{9,10},{10,... | collective-permute-start | bytes 442376 | tf_op jit(solution)/shard_map/ppermute | solution.py:39
  38.7 8.4 %collective-permute-start.8 = (bf16[96,768]{1,0:T(8,128)(2,1)S(1)}, bf16[96,768]{1,0:T(8,128)(2,1)S(1)}, u32[]{:S(2)}, u32[]{:S(2)}) collective-permute-start(bf16[96,768]{1,0:T(8,128)(2,1)S(1)} %get-tuple-element.24), channel_id=1, source_target_pairs={{0,1},{1,0},{2,3},{3,2},{4,5},{5,4},{6,7},{7,6},{8,9},{9,8},{10,11... | collective-permute-start | bytes 442376 | tf_op jit(solution)/shard_map/ppermute | solution.py:39
  38.7 12.8 %collective-permute-start.9 = (bf16[96,768]{1,0:T(8,128)(2,1)S(1)}, bf16[96,768]{1,0:T(8,128)(2,1)S(1)}, u32[]{:S(2)}, u32[]{:S(2)}) collective-permute-start(bf16[96,768]{1,0:T(8,128)(2,1)S(1)} %get-tuple-element.25), channel_id=1, source_target_pairs={{0,2},{1,3},{2,0},{3,1},{4,6},{5,7},{6,4},{7,5},{8,10},{9,11},{10,... | collective-permute-start | bytes 442376 | tf_op jit(solution)/shard_map/ppermute | solution.py:39
  67.9 14.6 %collective-permute-start.16 = (bf16[384,768]{1,0:T(8,128)(2,1)S(1)}, bf16[384,768]{1,0:T(8,128)(2,1)S(1)}, u32[]{:S(2)}, u32[]{:S(2)}) collective-permute-start(bf16[384,768]{1,0:T(8,128)(2,1)S(1)} %all_gather.3), channel_id=1, source_target_pairs={{0,8},{4,12},{8,0},{12,4},{16,24},{20,28},{24,16},{28,20},{1,9},{5... | collective-permute-start | bytes 1769480 | tf_op jit(solution)/shard_map/ppermute | solution.py:34
  68.5 14.7 %collective-permute-start.18 = (bf16[384,768]{1,0:T(8,128)(2,1)S(1)}, bf16[384,768]{1,0:T(8,128)(2,1)S(1)}, u32[]{:S(2)}, u32[]{:S(2)}) collective-permute-start(bf16[384,768]{1,0:T(8,128)(2,1)S(1)} %all_gather.3), channel_id=1, source_target_pairs={{0,16},{4,20},{8,24},{12,28},{16,0},{20,4},{24,8},{28,12},{1,17},{... | collective-permute-start | bytes 1769480 | tf_op jit(solution)/shard_map/ppermute | solution.py:34
  70.0 14.8 %collective-permute-start.15 = (bf16[384,768]{1,0:T(8,128)(2,1)S(1)}, bf16[384,768]{1,0:T(8,128)(2,1)}, u32[]{:S(2)}, u32[]{:S(2)}) collective-permute-start(bf16[384,768]{1,0:T(8,128)(2,1)S(1)} %all_gather.3), channel_id=1, source_target_pairs={{0,4},{4,0},{8,12},{12,8},{16,20},{20,16},{24,28},{28,24},{1,5},{5... | collective-permute-start | bytes 1769480 | tf_op jit(solution)/shard_map/ppermute | solution.py:34
  70.0 1.8 %collective-permute-start.11 = (f32[768]{0:T(1024)S(1)}, f32[768]{0:T(1024)S(1)}, u32[]{:S(2)}, u32[]{:S(2)}) collective-permute-start(f32[768]{0:T(1024)S(1)} %add_add_fusion.1), channel_id=1, source_target_pairs={{0,4},{4,0},{8,12},{12,8},{16,20},{20,16},{24,28},{28,24},{1,5},{5... | collective-permute-start | bytes 9224 | tf_op jit(solution)/shard_map/ppermute | solution.py:34
  71.8 3.8 %collective-permute-start.12 = (f32[768]{0:T(1024)S(1)}, f32[768]{0:T(1024)S(1)}, u32[]{:S(2)}, u32[]{:S(2)}) collective-permute-start(f32[768]{0:T(1024)S(1)} %add.121), channel_id=1, source_target_pairs={{0,1},{1,0},{2,3},{3,2},{4,5},{5,4},{6,7},{7,6},{8,9},{9,8},{10,11... | collective-permute-start | bytes 9224 | tf_op jit(solution)/shard_map/ppermute | solution.py:39
  73.1 5.6 %collective-permute-start.13 = (f32[768]{0:T(1024)S(1)}, f32[768]{0:T(1024)S(1)}, u32[]{:S(2)}, u32[]{:S(2)}) collective-permute-start(f32[768]{0:T(1024)S(1)} %add.121), channel_id=1, source_target_pairs={{0,2},{1,3},{2,0},{3,1},{4,6},{5,7},{6,4},{7,5},{8,10},{9,11},{10,... | collective-permute-start | bytes 9224 | tf_op jit(solution)/shard_map/ppermute | solution.py:39
  75.7 5.4 %collective-permute-start.14 = (f32[768]{0:T(1024)S(1)}, f32[768]{0:T(1024)S(1)}, u32[]{:S(2)}, u32[]{:S(2)}) collective-permute-start(f32[768]{0:T(1024)S(1)} %add.121), channel_id=1, source_target_pairs={{0,3},{1,2},{2,1},{3,0},{4,7},{5,6},{6,5},{7,4},{8,11},{9,10},{10,... | collective-permute-start | bytes 9224 | tf_op jit(solution)/shard_map/ppermute | solution.py:39
  81.7 11.2 %copy-start.11 = (f32[768]{0:T(1024)}, f32[768]{0:T(1024)S(1)}, u32[]{:S(2)}) copy-start(f32[768]{0:T(1024)S(1)} %get-tuple-element.33) | copy-start | bytes 9220
  82.6 7.4 %collective-permute-start.20 = (bf16[192,768]{1,0:T(8,128)(2,1)S(1)}, bf16[192,768]{1,0:T(8,128)(2,1)S(1)}, u32[]{:S(2)}, u32[]{:S(2)}) collective-permute-start(bf16[192,768]{1,0:T(8,128)(2,1)S(1)} %slice.62), channel_id=1, source_target_pairs={{0,16},{4,20},{8,24},{12,28},{16,0},{20,4},{24,8},{28,12},{1,17},{... | collective-permute-start | bytes 884744 | tf_op jit(solution)/shard_map/ppermute | solution.py:34
  83.2 7.2 %collective-permute-start.22 = (bf16[192,768]{1,0:T(8,128)(2,1)S(1)}, bf16[192,768]{1,0:T(8,128)(2,1)S(1)}, u32[]{:S(2)}, u32[]{:S(2)}) collective-permute-start(bf16[192,768]{1,0:T(8,128)(2,1)S(1)} %slice.63), channel_id=1, source_target_pairs={{0,8},{4,12},{8,0},{12,4},{16,24},{20,28},{24,16},{28,20},{1,9},{5... | collective-permute-start | bytes 884744 | tf_op jit(solution)/shard_map/ppermute | solution.py:34
  86.9 5.6 %collective-permute-start.19 = (bf16[384,768]{1,0:T(8,128)(2,1)S(1)}, bf16[384,768]{1,0:T(8,128)(2,1)S(1)}, u32[]{:S(2)}, u32[]{:S(2)}) collective-permute-start(bf16[384,768]{1,0:T(8,128)(2,1)S(1)} %collective-permute-done.18), channel_id=1, source_target_pairs={{0,4},{4,0},{8,12},{12,8},{16,20},{20,16},{24,28},{28,24},{1,5},{5... | collective-permute-start | bytes 1769480 | tf_op jit(solution)/shard_map/ppermute | solution.py:34
  87.3 5.5 %collective-permute-start.17 = (bf16[384,768]{1,0:T(8,128)(2,1)S(1)}, bf16[384,768]{1,0:T(8,128)(2,1)S(1)}, u32[]{:S(2)}, u32[]{:S(2)}) collective-permute-start(bf16[384,768]{1,0:T(8,128)(2,1)S(1)} %collective-permute-done.16), channel_id=1, source_target_pairs={{0,4},{4,0},{8,12},{12,8},{16,20},{20,16},{24,28},{28,24},{1,5},{5... | collective-permute-start | bytes 1769480 | tf_op jit(solution)/shard_map/ppermute | solution.py:34
  90.0 1.6 %collective-permute-start.21 = (bf16[192,768]{1,0:T(8,128)(2,1)S(1)}, bf16[192,768]{1,0:T(8,128)(2,1)S(1)}, u32[]{:S(2)}, u32[]{:S(2)}) collective-permute-start(bf16[192,768]{1,0:T(8,128)(2,1)S(1)} %collective-permute-done.20), channel_id=1, source_target_pairs={{0,4},{4,0},{8,12},{12,8},{16,20},{20,16},{24,28},{28,24},{1,5},{5... | collective-permute-start | bytes 884744 | tf_op jit(solution)/shard_map/ppermute | solution.py:34
  90.3 1.8 %collective-permute-start.23 = (bf16[192,768]{1,0:T(8,128)(2,1)S(1)}, bf16[192,768]{1,0:T(8,128)(2,1)S(1)}, u32[]{:S(2)}, u32[]{:S(2)}) collective-permute-start(bf16[192,768]{1,0:T(8,128)(2,1)S(1)} %collective-permute-done.22), channel_id=1, source_target_pairs={{0,4},{4,0},{8,12},{12,8},{16,20},{20,16},{24,28},{28,24},{1,5},{5... | collective-permute-start | bytes 884744 | tf_op jit(solution)/shard_map/ppermute | solution.py:34
  92.5 1.0 %copy-start.8 = (bf16[256,768]{1,0:T(8,128)(2,1)S(1)}, bf16[256,768]{1,0:T(8,128)(2,1)}, u32[]{:S(2)}) copy-start(bf16[256,768]{1,0:T(8,128)(2,1)} %param.25) | copy-start | bytes 1179652

commit v4 on v3

--- a/solution.py
+++ b/solution.py
@@ -202,7 +202,7 @@
     rows = own.shape[0]
     for j in range(len(outgoing) + 1):
         at = pl.ds(pl.multiple_of((place[0] ^ j) * rows, 32), rows)
-        total = keep[at, :] + arrived[at, :]
+        total = keep[at, :] + arrived[at, :].astype(jnp.float32)
         if j:
             outgoing[j - 1][...] = total.astype(jnp.bfloat16)
         else:
@@ -305,7 +305,7 @@
     keep, send = fold_tokens(layer_scale, hidden_of[:3], [out_cotangent, cot_x, cot_y], width)
     scaled = scale_it(jnp.concatenate(corner, 0))
     far = hidden_of[3][:tokens]
-    send = send + token_fold(far[:, width:], scaled)
+    send = (send + token_fold(far[:, width:], scaled)).astype(jnp.bfloat16)
     keep = keep + token_fold(far[:, :width], scaled)
     share = share + swap_fsdp(share, 1)
     own, *outgoing = split_rows(place, keep, swap_fsdp(send, 1), own_rows, rep_count)
@@ -320,6 +320,7 @@
         teacher_weight,
     )
 
+    sent_rows, share = lax.optimization_barrier((sent_rows, share))
     teacher_shard = lax.all_gather(sent_rows, "rep", axis=0, tiled=True)
     share = sum([swap_rep(share, j) for j in range(1, rep_count)], share)
     scale_new, scale_first_new, scale_second_new = adam_step(
@@ -339,11 +340,25 @@
             total = term if total is None else total + term
         return total
 
-    near = terms(teacher_shard, 0, 0) + terms(along_x, 2, 0) + terms(along_y, 4, 0)
-    near = teacher_input.astype(jnp.float32) + teacher_scale_new * near
-    stored_shard = jnp.where(me >= 0, teacher_shard, jnp.zeros_like(teacher_shard))
-    near, stored_shard = lax.optimization_barrier((near, stored_shard))
-    far = terms(corner_x, 6, 0) + terms(corner_y, 6, pair_rows)
+    near = teacher_input.astype(jnp.float32) + teacher_scale_new * terms(teacher_shard, 0, 0)
+    near = lax.optimization_barrier(near)
+    near = near + teacher_scale_new * (terms(along_x, 2, 0) + terms(along_y, 4, 0))
+    held_shard = after(teacher_shard, along_x, along_y)
+    stored_shard = jnp.where(me >= 0, held_shard, jnp.zeros_like(held_shard))
+    swapped_x, swapped_y = swap_fsdp(corner_x, 1), swap_fsdp(corner_y, 1)
+    near, stored_shard, swapped_x, swapped_y = lax.optimization_barrier(
+        (near, stored_shard, swapped_x, swapped_y)
+    )
+    far = None
+    for block, f, start in (
+        (corner_x, 6, 0),
+        (corner_y, 6, pair_rows),
+        (swapped_x, 7, 0),
+        (swapped_y, 7, pair_rows),
+    ):
+        units = columns(teacher_hidden, f)[:, start : start + pair_rows]
+        term = jnp.dot(units, block, preferred_element_type=jnp.float32)
+        far = term if far is None else far + term
     teacher_out = (near + teacher_scale_new * far).astype(jnp.bfloat16)
     return (
         new_weight,

time: 95.1 us -> 91.3 us (0.960)
  starting transfers between devices: 29 us -> 20.2 us
  waiting for transfers between devices: 30.1 us -> 34.7 us
  blocking collectives: 15.5 us -> 18 us
  Pallas kernels: 3.51 us -> 2.24 us
    ppermute x6, starting transfers between devices: 11.3 us -> 5.22 us  [swap_rep(): return lax.ppermute(value, 'rep', [(i, i ^ flip) for i in range(count)])]
    ppermute x6, waiting for transfers between devices: 12.9 us -> 17.8 us  [swap_rep(): return lax.ppermute(value, 'rep', [(i, i ^ flip) for i in range(count)])]
    ppermute x18, starting transfers between devices: 17.7 us -> 15 us  [swap_fsdp(): return lax.ppermute(value, 'fsdp', [(i, i ^ flip) for i in range(count)])]
    all_gather x1, blocking collectives: 15.5 us -> 18 us  [block_shards(): teacher_shard = lax.all_gather(sent_rows, 'rep', axis=0, tiled=True)]
    dot_general x10 -> x6, matrix products: 4.53 us -> 2.17 us  [terms(): term = jnp.dot(units, weights, preferred_element_type=jnp.float32)]
    reduce_sum x3, other arithmetic: 2.16 us -> 0.75 us  [block_shards(): jnp.sum(hidden[tokens:tokens + 3].astype(jnp.float32), axis=0)]
    pallas_call x1, Pallas kernels: 1.38 us -> 0.11 us  [split_rows(): pl.pallas_call(split_kernel, out_shape=[jax.ShapeDtypeStruct((rows, width...]
    dot_general x0 -> x4, matrix products: none -> 1.27 us  [block_shards(): term = jnp.dot(units, block, preferred_element_type=jnp.float32)]
  transfers between devices with their start and end apart: 24 -> 24, of which waited for: 13 -> 12; matrix products, arithmetic and copies ran while one was open for 13% -> 13% of each run, Pallas kernels for 1% -> 1%
where the time goes in v4:
time: 91.3 us; the launch traced here: 90.9 us
  waiting for transfers between devices  34.7 us (38%)
  starting transfers between devices  20.2 us (22%)
  blocking collectives  18 us (20%)
  other arithmetic  6.55 us (7%)
  matrix products  5.98 us (7%)
  local copies, waits for them, and re-layouts  2.28 us (2%)
  Pallas kernels  2.24 us (2%)
  between operations  1.05 us (1%)
    all_gather x1, blocking collectives, block_shards(): teacher_shard = lax.all_gather(sent_rows, 'rep', axis=0, tiled=True)  18 us
    ppermute x6, waiting for transfers between devices, swap_rep(): return lax.ppermute(value, 'rep', [(i, i ^ flip) for i in range(count)])  17.8 us
    ppermute x18, waiting for transfers between devices, swap_fsdp(): return lax.ppermute(value, 'fsdp', [(i, i ^ flip) for i in range(count)])  16.9 us
    ppermute x18, starting transfers between devices, swap_fsdp(): return lax.ppermute(value, 'fsdp', [(i, i ^ flip) for i in range(count)])  15 us
    ppermute x6, starting transfers between devices, swap_rep(): return lax.ppermute(value, 'rep', [(i, i ^ flip) for i in range(count)])  5.22 us
    dot_general x2, matrix products, token_fold(): lax.dot_general(arrived, portion, (((0,), (0,)), ((), ())), preferred_ele...  2.54 us
    dot_general x6, matrix products, terms(): term = jnp.dot(units, weights, preferred_element_type=jnp.float32)  2.17 us
  transfers between devices with their start and end apart: 24, of which 12 were waited for; matrix products, arithmetic and copies ran while one was open for 13% of the time, Pallas kernels for 1%

profile of v4, /device:TPU:0, one launch (start us, length us, event | category | flops | bytes accessed | tf_op | source)
XLA Modules:
  0.0 90.9 jit_solution(2274978191760469364)
XLA Ops:
  0.6 0.0 copy-start
  0.7 3.0 %collective-permute-start.2 = (bf16[192,768]{1,0:T(8,128)(2,1)}, bf16[192,768]{1,0:T(8,128)(2,1)S(1)}, u32[]{:S(2)}, u32[]{:S(2)}) collective-permute-start(bf16[192,768]{1,0:T(8,128)(2,1)} %refs_3_.1), channel_id=1, source_target_pairs={{0,8},{4,12},{8,0},{12,4},{16,24},{20,28},{24,16},{28,20},{1,9},{5... | collective-permute-start | bytes 884744 | tf_op jit(solution)/shard_map/ppermute | solution.py:34
  3.7 1.5 %collective-permute-start.3 = (bf16[192,768]{1,0:T(8,128)(2,1)}, bf16[192,768]{1,0:T(8,128)(2,1)S(1)}, u32[]{:S(2)}, u32[]{:S(2)}) collective-permute-start(bf16[192,768]{1,0:T(8,128)(2,1)} %refs_3_.1), channel_id=1, source_target_pairs={{0,16},{4,20},{8,24},{12,28},{16,0},{20,4},{24,8},{28,12},{1,17},{... | collective-permute-start | bytes 884744 | tf_op jit(solution)/shard_map/ppermute | solution.py:34
  5.2 1.1 %multiply_reduce_fusion = f32[768]{0:T(1024)S(1)} fusion(bf16[192,768]{1,0:T(8,128)(2,1)} %param.15, bf16[192,768]{1,0:T(8,128)(2,1)} %refs_3_.1), kind=kLoop, calls=%fused_computation.15 | loop fusion | flops 589056 | bytes 592896 | tf_op jit(solution)/shard_map/reduce_sum | solution.py:287
  6.4 1.5 %constant_dynamic-slice_fusion.1 = (bf16[192,384]{1,0:T(8,128)(2,1)S(1)}, bf16[192,384]{1,0:T(8,128)(2,1)S(1)}, bf16[192,384]{1,0:T(8,128)(2,1)S(1)}, bf16[192,3...) fusion(bf16[192,3072]{1,0:T(8,128)(2,1)} %param.13, ...), kind=kLoop, calls=%fused_computation.61 | loop fusion | bytes 2359328 | tf_op jit(solution)/shard_map/dynamic_slice | solution.py:284
  7.9 0.0 copy-start.8
  7.9 0.0 copy-start.2
  7.9 0.9 %pad_maximum_fusion = (bf16[200,768]{1,0:T(8,128)(2,1)}, bf16[200,768]{1,0:T(8,128)(2,1)}, bf16[200,768]{1,0:T(8,128)(2,1)}) fusion(bf16[8,768]{1,0:T(8,128)(2,1)S(1)} %fusion.30, bf16[192,384]{1,0:T(8,128)(2,1)S(1)} %get-tuple-element.54, bf16[192,384]{1,0:T(8,128)(2,1)S(1)} %get-tuple-element.47, bf16[192,384]{1,0:T(8,128)(2,1)S(1)} %get-tuple-element.48, ...), kind=kLoop, calls=%fused_computation.17 | loop fusion | flops 2457600 | bytes 1818624 | tf_op jit(solution)/shard_map/concatenate | solution.py:295
  8.9 0.5 collective-permute-start
  9.4 0.1 collective-permute-start.1
  9.5 2.9 %collective-permute-start.4 = (bf16[200,768]{1,0:T(8,128)(2,1)}, bf16[200,768]{1,0:T(8,128)(2,1)}, u32[]{:S(2)}, u32[]{:S(2)}) collective-permute-start(bf16[200,768]{1,0:T(8,128)(2,1)} %get-tuple-element.55), channel_id=1, source_target_pairs={{0,24},{4,28},{8,16},{12,20},{16,8},{20,12},{24,0},{28,4},{1,25},{... | collective-permute-start | bytes 921608 | tf_op jit(solution)/shard_map/ppermute | solution.py:34
  12.4 1.0 %collective-permute-done.3.refs_5_ = bf16[192,768]{1,0:T(8,128)(2,1)S(1)} collective-permute-done((bf16[192,768]{1,0:T(8,128)(2,1)}, bf16[192,768]{1,0:T(8,128)(2,1)S(1)}, u32[]{:S(2)}, u32[]{:S(2)}) %collective-permute-start.3) | collective-permute-done | bytes 294944 | tf_op jit(solution)/shard_map/ppermute | solution.py:34
  13.4 0.1 collective-permute-start.6
  13.5 0.7 slice.56
  14.2 2.1 %collective-permute-start.5 = (bf16[96,768]{1,0:T(8,128)(2,1)}, bf16[96,768]{1,0:T(8,128)(2,1)}, u32[]{:S(2)}, u32[]{:S(2)}) collective-permute-start(bf16[96,768]{1,0:T(8,128)(2,1)} %slice.56), channel_id=1, source_target_pairs={{0,16},{4,20},{8,24},{12,28},{16,0},{20,4},{24,8},{28,12},{1,17},{... | collective-permute-start | bytes 442376 | tf_op jit(solution)/shard_map/ppermute | solution.py:34
  16.3 3.0 %collective-permute-done.refs_1_ = bf16[200,768]{1,0:T(8,128)(2,1)S(1)} collective-permute-done((bf16[200,768]{1,0:T(8,128)(2,1)}, bf16[200,768]{1,0:T(8,128)(2,1)S(1)}, u32[]{:S(2)}, u32[]{:S(2)}) %collective-permute-start) | collective-permute-done | bytes 307232 | tf_op jit(solution)/shard_map/ppermute | solution.py:34
  19.3 7.3 %collective-permute-done.1.refs_2_ = bf16[200,768]{1,0:T(8,128)(2,1)S(1)} collective-permute-done((bf16[200,768]{1,0:T(8,128)(2,1)}, bf16[200,768]{1,0:T(8,128)(2,1)S(1)}, u32[]{:S(2)}, u32[]{:S(2)}) %collective-permute-start.1) | collective-permute-done | bytes 307232 | tf_op jit(solution)/shard_map/ppermute | solution.py:34
  26.6 1.1 %fold_tokens.1 = (f32[384,768]{1,0:T(8,128)S(1)}, f32[384,768]{1,0:T(8,128)S(1)}) custom-call(f32[1,768]{1,0:T(1,128)S(1)} %reshape.51.scale, bf16[192,768]{1,0:T(8,128)(2,1)S(1)} %pad_maximum_fusion.3.refs_0_, bf16[200,768]{1,0:T(8,128)(2,1)S(1)} %collective-permute-done.refs_1_, bf16[200,768]{1,0:T(8,128)(2,1)S(1)} %collective-permute-done.1.refs_2_, ...), custom_call_target="tpu_custom_call" | custom-call | flops 679477248 | bytes 2949120 | tf_op jit(solution)/shard_map/fold_tokens/pallas_call | solution.py:186
  27.7 1.1 %collective-permute-done.5 = bf16[96,768]{1,0:T(8,128)(2,1)} collective-permute-done((bf16[96,768]{1,0:T(8,128)(2,1)}, bf16[96,768]{1,0:T(8,128)(2,1)}, u32[]{:S(2)}, u32[]{:S(2)}) %collective-permute-start.5) | collective-permute-done | bytes 147488 | tf_op jit(solution)/shard_map/ppermute | solution.py:34
  28.8 1.0 %multiply_convert_fusion = bf16[192,768]{1,0:T(8,128)(2,1)S(1)} fusion(bf16[96,768]{1,0:T(8,128)(2,1)} %collective-permute-done.6, bf16[96,768]{1,0:T(8,128)(2,1)} %collective-permute-done.5, f32[768]{0:T(1024)S(1)} %copy-done.8), kind=kLoop, calls=%fused_computation.14 | loop fusion | flops 884736 | bytes 592896 | tf_op jit(solution)/shard_map/convert_element_type | solution.py:302
  29.8 1.3 %fusion.16 = f32[384,768]{1,0:T(8,128)S(1)} fusion(bf16[192,768]{1,0:T(8,128)(2,1)S(1)} %multiply_convert_fusion, bf16[200,768]{1,0:T(8,128)(2,1)} %collective-permute-done.4), kind=kOutput, calls=%fused_computation.30 | convolution fusion | flops 113246208 | bytes 1622016 | tf_op jit(solution)/shard_map/dot_general | solution.py:27
  31.1 0.1 add_convert_fusion
  31.2 0.1 collective-permute-start.7
  31.3 0.7 convert_reduce_fusion
  32.1 1.3 %fusion.18 = f32[384,768]{1,0:T(8,128)S(1)} fusion(bf16[192,768]{1,0:T(8,128)(2,1)S(1)} %multiply_convert_fusion, bf16[200,768]{1,0:T(8,128)(2,1)} %collective-permute-done.4), kind=kOutput, calls=%fused_computation.32 | convolution fusion | flops 113246208 | bytes 1622016 | tf_op jit(solution)/shard_map/dot_general | solution.py:27
  33.4 0.2 add.116.keep
  33.5 0.0 copy-start.1
  33.5 0.0 copy-start.3
  33.5 0.0 copy-start.4
  33.6 0.0 copy-start.5
  33.6 0.1 split_rows.1
  33.7 1.6 %collective-permute-start.8 = (bf16[96,768]{1,0:T(8,128)(2,1)S(1)}, bf16[96,768]{1,0:T(8,128)(2,1)S(1)}, u32[]{:S(2)}, u32[]{:S(2)}) collective-permute-start(bf16[96,768]{1,0:T(8,128)(2,1)S(1)} %get-tuple-element.29), channel_id=1, source_target_pairs={{0,1},{1,0},{2,3},{3,2},{4,5},{5,4},{6,7},{7,6},{8,9},{9,8},{10,11... | collective-permute-start | bytes 442376 | tf_op jit(solution)/shard_map/ppermute | solution.py:39
  35.3 2.6 %collective-permute-start.9 = (bf16[96,768]{1,0:T(8,128)(2,1)S(1)}, bf16[96,768]{1,0:T(8,128)(2,1)S(1)}, u32[]{:S(2)}, u32[]{:S(2)}) collective-permute-start(bf16[96,768]{1,0:T(8,128)(2,1)S(1)} %get-tuple-element.30), channel_id=1, source_target_pairs={{0,2},{1,3},{2,0},{3,1},{4,6},{5,7},{6,4},{7,5},{8,10},{9,11},{10,... | collective-permute-start | bytes 442376 | tf_op jit(solution)/shard_map/ppermute | solution.py:39
  37.9 0.2 collective-permute-start.10
  38.2 1.2 %collective-permute-done.11 = f32[768]{0:T(1024)S(1)} collective-permute-done((f32[768]{0:T(1024)S(1)}, f32[768]{0:T(1024)S(1)}, u32[]{:S(2)}, u32[]{:S(2)}) %collective-permute-start.11) | collective-permute-done | bytes 3104 | tf_op jit(solution)/shard_map/ppermute | solution.py:34
  39.3 3.4 %collective-permute-done.8.one = bf16[96,768]{1,0:T(8,128)(2,1)S(1)} collective-permute-done((bf16[96,768]{1,0:T(8,128)(2,1)S(1)}, bf16[96,768]{1,0:T(8,128)(2,1)S(1)}, u32[]{:S(2)}, u32[]{:S(2)}) %collective-permute-start.8) | collective-permute-done | bytes 147488 | tf_op jit(solution)/shard_map/ppermute | solution.py:39
  42.8 6.5 %collective-permute-done.9.two = bf16[96,768]{1,0:T(8,128)(2,1)S(1)} collective-permute-done((bf16[96,768]{1,0:T(8,128)(2,1)S(1)}, bf16[96,768]{1,0:T(8,128)(2,1)S(1)}, u32[]{:S(2)}, u32[]{:S(2)}) %collective-permute-start.9) | collective-permute-done | bytes 147488 | tf_op jit(solution)/shard_map/ppermute | solution.py:39
  49.3 1.0 %update_rows.1 = (bf16[96,768]{1,0:T(8,128)(2,1)}, bf16[96,768]{1,0:T(8,128)(2,1)}, bf16[96,768]{1,0:T(8,128)(2,1)}, bf16[96,768]{1,0:T(8,128)(2,1)S(1)}) custom-call(s32[1]{0:T(128)} %bitcast.place, f32[96,768]{1,0:T(8,128)S(1)} %get-tuple-element.28.own, bf16[96,768]{1,0:T(8,128)(2,1)S(1)} %collective-permute-done.8.one, ...), custom_call_target="tpu_custom_call" | custom-call | flops 1474560 | bytes 2211840 | tf_op jit(solution)/shard_map/update_rows/pallas_call | solution.py:246
  50.3 18.0 %all_gather.3 = bf16[384,768]{1,0:T(8,128)(2,1)S(1)} all-gather(bf16[96,768]{1,0:T(8,128)(2,1)S(1)} %get-tuple-element.37), channel_id=1, replica_groups=mesh['fsdp'=8,'rep'=4] {'rep'}, dimensions={0}, use_global_device_ids=true | all-gather | bytes 737280 | tf_op jit(solution)/shard_map/all_gather | solution.py:324
  68.3 0.5 collective-permute-start.16
  68.9 1.5 %collective-permute-start.18 = (bf16[384,768]{1,0:T(8,128)(2,1)S(1)}, bf16[384,768]{1,0:T(8,128)(2,1)S(1)}, u32[]{:S(2)}, u32[]{:S(2)}) collective-permute-start(bf16[384,768]{1,0:T(8,128)(2,1)S(1)} %all_gather.3), channel_id=1, source_target_pairs={{0,16},{4,20},{8,24},{12,28},{16,0},{20,4},{24,8},{28,12},{1,17},{... | collective-permute-start | bytes 1769480 | tf_op jit(solution)/shard_map/ppermute | solution.py:34
  70.4 0.8 collective-permute-start.14
  71.1 4.6 %collective-permute-done.14 = f32[768]{0:T(1024)S(1)} collective-permute-done((f32[768]{0:T(1024)S(1)}, f32[768]{0:T(1024)S(1)}, u32[]{:S(2)}, u32[]{:S(2)}) %collective-permute-start.14) | collective-permute-done | bytes 3104 | tf_op jit(solution)/shard_map/ppermute | solution.py:39
  75.8 0.4 fusion.14
  76.1 0.0 copy-start.6
  76.2 3.2 %collective-permute-done.12 = f32[768]{0:T(1024)S(1)} collective-permute-done((f32[768]{0:T(1024)S(1)}, f32[768]{0:T(1024)S(1)}, u32[]{:S(2)}, u32[]{:S(2)}) %collective-permute-start.12) | collective-permute-done | bytes 3104 | tf_op jit(solution)/shard_map/ppermute | solution.py:39
  79.4 0.6 multiply_add_fusion
  80.1 1.0 %collective-permute-start.20 = (bf16[192,768]{1,0:T(8,128)(2,1)S(1)}, bf16[192,768]{1,0:T(8,128)(2,1)S(1)}, u32[]{:S(2)}, u32[]{:S(2)}) collective-permute-start(bf16[192,768]{1,0:T(8,128)(2,1)S(1)} %slice.62), channel_id=1, source_target_pairs={{0,16},{4,20},{8,24},{12,28},{16,0},{20,4},{24,8},{28,12},{1,17},{... | collective-permute-start | bytes 884744 | tf_op jit(solution)/shard_map/ppermute | solution.py:34
  81.1 1.1 %collective-permute-start.22 = (bf16[192,768]{1,0:T(8,128)(2,1)S(1)}, bf16[192,768]{1,0:T(8,128)(2,1)S(1)}, u32[]{:S(2)}, u32[]{:S(2)}) collective-permute-start(bf16[192,768]{1,0:T(8,128)(2,1)S(1)} %slice.63), channel_id=1, source_target_pairs={{0,8},{4,12},{8,0},{12,4},{16,24},{20,28},{24,16},{28,20},{1,9},{5... | collective-permute-start | bytes 884744 | tf_op jit(solution)/shard_map/ppermute | solution.py:34
  82.2 0.4 fusion.8
  82.6 0.4 fusion.1
  83.0 0.4 fusion.11
  83.3 0.9 broadcast_select_fusion
  84.2 0.5 collective-permute-start.17
  84.7 2.1 %collective-permute-done.20 = bf16[192,768]{1,0:T(8,128)(2,1)S(1)} collective-permute-done((bf16[192,768]{1,0:T(8,128)(2,1)S(1)}, bf16[192,768]{1,0:T(8,128)(2,1)S(1)}, u32[]{:S(2)}, u32[]{:S(2)}) %collective-permute-start.20) | collective-permute-done | bytes 294944 | tf_op jit(solution)/shard_map/ppermute | solution.py:34
  86.8 1.0 %collective-permute-done.22 = bf16[192,768]{1,0:T(8,128)(2,1)S(1)} collective-permute-done((bf16[192,768]{1,0:T(8,128)(2,1)S(1)}, bf16[192,768]{1,0:T(8,128)(2,1)S(1)}, u32[]{:S(2)}, u32[]{:S(2)}) %collective-permute-start.22) | collective-permute-done | bytes 294944 | tf_op jit(solution)/shard_map/ppermute | solution.py:34
  87.9 0.3 fusion.23
  88.2 0.3 convolution_add_fusion.4
  88.5 0.4 convolution_add_fusion
  88.9 0.4 fusion.4
  89.3 0.2 collective-permute-done.23
  89.5 0.3 fusion.20
  89.8 0.3 fusion.6
  90.1 0.8 add_convert_fusion.1
  (46 shorter events, 0.2 us)
Async XLA Ops:
  0.6 75.1 %copy-start = (bf16[256,3072]{1,0:T(8,128)(2,1)S(1)}, bf16[256,3072]{1,0:T(8,128)(2,1)}, u32[]{:S(2)}) copy-start(bf16[256,3072]{1,0:T(8,128)(2,1)} %param.24) | copy-start | bytes 4718596
  0.7 12.8 %collective-permute-start.2 = (bf16[192,768]{1,0:T(8,128)(2,1)}, bf16[192,768]{1,0:T(8,128)(2,1)S(1)}, u32[]{:S(2)}, u32[]{:S(2)}) collective-permute-start(bf16[192,768]{1,0:T(8,128)(2,1)} %refs_3_.1), channel_id=1, source_target_pairs={{0,8},{4,12},{8,0},{12,4},{16,24},{20,28},{24,16},{28,20},{1,9},{5... | collective-permute-start | bytes 884744 | tf_op jit(solution)/shard_map/ppermute | solution.py:34
  3.7 9.7 %collective-permute-start.3 = (bf16[192,768]{1,0:T(8,128)(2,1)}, bf16[192,768]{1,0:T(8,128)(2,1)S(1)}, u32[]{:S(2)}, u32[]{:S(2)}) collective-permute-start(bf16[192,768]{1,0:T(8,128)(2,1)} %refs_3_.1), channel_id=1, source_target_pairs={{0,16},{4,20},{8,24},{12,28},{16,0},{20,4},{24,8},{28,12},{1,17},{... | collective-permute-start | bytes 884744 | tf_op jit(solution)/shard_map/ppermute | solution.py:34
  7.9 8.4 %copy-start.8 = (f32[768]{0:T(1024)S(1)}, f32[768]{0:T(1024)}, u32[]{:S(2)}) copy-start(f32[768]{0:T(1024)} %param.16) | copy-start | bytes 9220
  7.9 18.7 %copy-start.2 = (bf16[192,768]{1,0:T(8,128)(2,1)S(1)}, bf16[192,768]{1,0:T(8,128)(2,1)}, u32[]{:S(2)}) copy-start(bf16[192,768]{1,0:T(8,128)(2,1)} %refs_3_.1) | copy-start | bytes 884740
  8.9 10.4 %collective-permute-start = (bf16[200,768]{1,0:T(8,128)(2,1)}, bf16[200,768]{1,0:T(8,128)(2,1)S(1)}, u32[]{:S(2)}, u32[]{:S(2)}) collective-permute-start(bf16[200,768]{1,0:T(8,128)(2,1)} %get-tuple-element.57), channel_id=1, source_target_pairs={{0,8},{4,12},{8,0},{12,4},{16,24},{20,28},{24,16},{28,20},{1,9},{5... | collective-permute-start | bytes 921608 | tf_op jit(solution)/shard_map/ppermute | solution.py:34
  9.4 17.2 %collective-permute-start.1 = (bf16[200,768]{1,0:T(8,128)(2,1)}, bf16[200,768]{1,0:T(8,128)(2,1)S(1)}, u32[]{:S(2)}, u32[]{:S(2)}) collective-permute-start(bf16[200,768]{1,0:T(8,128)(2,1)} %get-tuple-element.56), channel_id=1, source_target_pairs={{0,16},{4,20},{8,24},{12,28},{16,0},{20,4},{24,8},{28,12},{1,17},{... | collective-permute-start | bytes 921608 | tf_op jit(solution)/shard_map/ppermute | solution.py:34
  9.5 20.3 %collective-permute-start.4 = (bf16[200,768]{1,0:T(8,128)(2,1)}, bf16[200,768]{1,0:T(8,128)(2,1)}, u32[]{:S(2)}, u32[]{:S(2)}) collective-permute-start(bf16[200,768]{1,0:T(8,128)(2,1)} %get-tuple-element.55), channel_id=1, source_target_pairs={{0,24},{4,28},{8,16},{12,20},{16,8},{20,12},{24,0},{28,4},{1,25},{... | collective-permute-start | bytes 921608 | tf_op jit(solution)/shard_map/ppermute | solution.py:34
  13.4 14.3 %collective-permute-start.6 = (bf16[96,768]{1,0:T(8,128)(2,1)S(1)}, bf16[96,768]{1,0:T(8,128)(2,1)}, u32[]{:S(2)}, u32[]{:S(2)}) collective-permute-start(bf16[96,768]{1,0:T(8,128)(2,1)S(1)} %slice.57), channel_id=1, source_target_pairs={{0,8},{4,12},{8,0},{12,4},{16,24},{20,28},{24,16},{28,20},{1,9},{5... | collective-permute-start | bytes 442376 | tf_op jit(solution)/shard_map/ppermute | solution.py:34
  14.2 14.6 %collective-permute-start.5 = (bf16[96,768]{1,0:T(8,128)(2,1)}, bf16[96,768]{1,0:T(8,128)(2,1)}, u32[]{:S(2)}, u32[]{:S(2)}) collective-permute-start(bf16[96,768]{1,0:T(8,128)(2,1)} %slice.56), channel_id=1, source_target_pairs={{0,16},{4,20},{8,24},{12,28},{16,0},{20,4},{24,8},{28,12},{1,17},{... | collective-permute-start | bytes 442376 | tf_op jit(solution)/shard_map/ppermute | solution.py:34
  31.2 2.3 %collective-permute-start.7 = (bf16[384,768]{1,0:T(8,128)(2,1)S(1)}, bf16[384,768]{1,0:T(8,128)(2,1)S(1)}, u32[]{:S(2)}, u32[]{:S(2)}) collective-permute-start(bf16[384,768]{1,0:T(8,128)(2,1)S(1)} %add_convert_fusion), channel_id=1, source_target_pairs={{0,4},{4,0},{8,12},{12,8},{16,20},{20,16},{24,28},{28,24},{1,5},{5... | collective-permute-start | bytes 1769480 | tf_op jit(solution)/shard_map/ppermute | solution.py:34
  33.5 15.8 %copy-start.1 = (bf16[384,768]{1,0:T(8,128)(2,1)S(1)}, bf16[384,768]{1,0:T(8,128)(2,1)}, u32[]{:S(2)}) copy-start(bf16[384,768]{1,0:T(8,128)(2,1)} %teacher.1) | copy-start | bytes 1769476
  33.5 15.8 %copy-start.3 = (bf16[96,768]{1,0:T(8,128)(2,1)S(1)}, bf16[96,768]{1,0:T(8,128)(2,1)}, u32[]{:S(2)}) copy-start(bf16[96,768]{1,0:T(8,128)(2,1)} %weight.1) | copy-start | bytes 442372
  33.5 15.8 %copy-start.4 = (bf16[96,768]{1,0:T(8,128)(2,1)S(1)}, bf16[96,768]{1,0:T(8,128)(2,1)}, u32[]{:S(2)}) copy-start(bf16[96,768]{1,0:T(8,128)(2,1)} %first.1) | copy-start | bytes 442372
  33.6 15.8 %copy-start.5 = (bf16[96,768]{1,0:T(8,128)(2,1)S(1)}, bf16[96,768]{1,0:T(8,128)(2,1)}, u32[]{:S(2)}) copy-start(bf16[96,768]{1,0:T(8,128)(2,1)} %second.1) | copy-start | bytes 442372
  33.7 9.1 %collective-permute-start.8 = (bf16[96,768]{1,0:T(8,128)(2,1)S(1)}, bf16[96,768]{1,0:T(8,128)(2,1)S(1)}, u32[]{:S(2)}, u32[]{:S(2)}) collective-permute-start(bf16[96,768]{1,0:T(8,128)(2,1)S(1)} %get-tuple-element.29), channel_id=1, source_target_pairs={{0,1},{1,0},{2,3},{3,2},{4,5},{5,4},{6,7},{7,6},{8,9},{9,8},{10,11... | collective-permute-start | bytes 442376 | tf_op jit(solution)/shard_map/ppermute | solution.py:39
  35.3 13.9 %collective-permute-start.9 = (bf16[96,768]{1,0:T(8,128)(2,1)S(1)}, bf16[96,768]{1,0:T(8,128)(2,1)S(1)}, u32[]{:S(2)}, u32[]{:S(2)}) collective-permute-start(bf16[96,768]{1,0:T(8,128)(2,1)S(1)} %get-tuple-element.30), channel_id=1, source_target_pairs={{0,2},{1,3},{2,0},{3,1},{4,6},{5,7},{6,4},{7,5},{8,10},{9,11},{10,... | collective-permute-start | bytes 442376 | tf_op jit(solution)/shard_map/ppermute | solution.py:39
  37.9 11.4 %collective-permute-start.10 = (bf16[96,768]{1,0:T(8,128)(2,1)S(1)}, bf16[96,768]{1,0:T(8,128)(2,1)S(1)}, u32[]{:S(2)}, u32[]{:S(2)}) collective-permute-start(bf16[96,768]{1,0:T(8,128)(2,1)S(1)} %get-tuple-element.31), channel_id=1, source_target_pairs={{0,3},{1,2},{2,1},{3,0},{4,7},{5,6},{6,5},{7,4},{8,11},{9,10},{10,... | collective-permute-start | bytes 442376 | tf_op jit(solution)/shard_map/ppermute | solution.py:39
  38.2 1.2 %collective-permute-start.11 = (f32[768]{0:T(1024)S(1)}, f32[768]{0:T(1024)S(1)}, u32[]{:S(2)}, u32[]{:S(2)}) collective-permute-start(f32[768]{0:T(1024)S(1)} %add_add_fusion.1), channel_id=1, source_target_pairs={{0,4},{4,0},{8,12},{12,8},{16,20},{20,16},{24,28},{28,24},{1,5},{5... | collective-permute-start | bytes 9224 | tf_op jit(solution)/shard_map/ppermute | solution.py:34
  50.3 29.1 %copy-start.9 = (f32[768]{0:T(1024)S(1)}, f32[768]{0:T(1024)}, u32[]{:S(2)}) copy-start(f32[768]{0:T(1024)} %param.23) | copy-start | bytes 9220
  50.3 29.1 %copy-start.10 = (f32[768]{0:T(1024)S(1)}, f32[768]{0:T(1024)}, u32[]{:S(2)}) copy-start(f32[768]{0:T(1024)} %param.17) | copy-start | bytes 9220
  50.3 29.1 %copy-start.11 = (f32[768]{0:T(1024)S(1)}, f32[768]{0:T(1024)}, u32[]{:S(2)}) copy-start(f32[768]{0:T(1024)} %param.18) | copy-start | bytes 9220
  68.3 11.7 %collective-permute-start.16 = (bf16[384,768]{1,0:T(8,128)(2,1)S(1)}, bf16[384,768]{1,0:T(8,128)(2,1)S(1)}, u32[]{:S(2)}, u32[]{:S(2)}) collective-permute-start(bf16[384,768]{1,0:T(8,128)(2,1)S(1)} %all_gather.3), channel_id=1, source_target_pairs={{0,8},{4,12},{8,0},{12,4},{16,24},{20,28},{24,16},{28,20},{1,9},{5... | collective-permute-start | bytes 1769480 | tf_op jit(solution)/shard_map/ppermute | solution.py:34
  68.9 12.2 %collective-permute-start.18 = (bf16[384,768]{1,0:T(8,128)(2,1)S(1)}, bf16[384,768]{1,0:T(8,128)(2,1)S(1)}, u32[]{:S(2)}, u32[]{:S(2)}) collective-permute-start(bf16[384,768]{1,0:T(8,128)(2,1)S(1)} %all_gather.3), channel_id=1, source_target_pairs={{0,16},{4,20},{8,24},{12,28},{16,0},{20,4},{24,8},{28,12},{1,17},{... | collective-permute-start | bytes 1769480 | tf_op jit(solution)/shard_map/ppermute | solution.py:34
  70.4 5.4 %collective-permute-start.14 = (f32[768]{0:T(1024)S(1)}, f32[768]{0:T(1024)S(1)}, u32[]{:S(2)}, u32[]{:S(2)}) collective-permute-start(f32[768]{0:T(1024)S(1)} %add.121), channel_id=1, source_target_pairs={{0,3},{1,2},{2,1},{3,0},{4,7},{5,6},{6,5},{7,4},{8,11},{9,10},{10,... | collective-permute-start | bytes 9224 | tf_op jit(solution)/shard_map/ppermute | solution.py:39
  71.1 11.4 %collective-permute-start.15 = (bf16[384,768]{1,0:T(8,128)(2,1)S(1)}, bf16[384,768]{1,0:T(8,128)(2,1)S(1)}, u32[]{:S(2)}, u32[]{:S(2)}) collective-permute-start(bf16[384,768]{1,0:T(8,128)(2,1)S(1)} %all_gather.3), channel_id=1, source_target_pairs={{0,4},{4,0},{8,12},{12,8},{16,20},{20,16},{24,28},{28,24},{1,5},{5... | collective-permute-start | bytes 1769480 | tf_op jit(solution)/shard_map/ppermute | solution.py:34
  71.1 5.0 %collective-permute-start.13 = (f32[768]{0:T(1024)S(1)}, f32[768]{0:T(1024)S(1)}, u32[]{:S(2)}, u32[]{:S(2)}) collective-permute-start(f32[768]{0:T(1024)S(1)} %add.121), channel_id=1, source_target_pairs={{0,2},{1,3},{2,0},{3,1},{4,6},{5,7},{6,4},{7,5},{8,10},{9,11},{10,... | collective-permute-start | bytes 9224 | tf_op jit(solution)/shard_map/ppermute | solution.py:39
  75.8 3.6 %collective-permute-start.12 = (f32[768]{0:T(1024)S(1)}, f32[768]{0:T(1024)S(1)}, u32[]{:S(2)}, u32[]{:S(2)}) collective-permute-start(f32[768]{0:T(1024)S(1)} %add.121), channel_id=1, source_target_pairs={{0,1},{1,0},{2,3},{3,2},{4,5},{5,4},{6,7},{7,6},{8,9},{9,8},{10,11... | collective-permute-start | bytes 9224 | tf_op jit(solution)/shard_map/ppermute | solution.py:39
  76.1 6.4 %copy-start.6 = (bf16[256,768]{1,0:T(8,128)(2,1)S(1)}, bf16[256,768]{1,0:T(8,128)(2,1)}, u32[]{:S(2)}) copy-start(bf16[256,768]{1,0:T(8,128)(2,1)} %param.25) | copy-start | bytes 1179652
  80.0 9.8 %copy-start.7 = (f32[768]{0:T(1024)}, f32[768]{0:T(1024)S(1)}, u32[]{:S(2)}) copy-start(f32[768]{0:T(1024)S(1)} %get-tuple-element.43) | copy-start | bytes 9220
  80.1 6.8 %collective-permute-start.20 = (bf16[192,768]{1,0:T(8,128)(2,1)S(1)}, bf16[192,768]{1,0:T(8,128)(2,1)S(1)}, u32[]{:S(2)}, u32[]{:S(2)}) collective-permute-start(bf16[192,768]{1,0:T(8,128)(2,1)S(1)} %slice.62), channel_id=1, source_target_pairs={{0,16},{4,20},{8,24},{12,28},{16,0},{20,4},{24,8},{28,12},{1,17},{... | collective-permute-start | bytes 884744 | tf_op jit(solution)/shard_map/ppermute | solution.py:34
  81.1 6.8 %collective-permute-start.22 = (bf16[192,768]{1,0:T(8,128)(2,1)S(1)}, bf16[192,768]{1,0:T(8,128)(2,1)S(1)}, u32[]{:S(2)}, u32[]{:S(2)}) collective-permute-start(bf16[192,768]{1,0:T(8,128)(2,1)S(1)} %slice.63), channel_id=1, source_target_pairs={{0,8},{4,12},{8,0},{12,4},{16,24},{20,28},{24,16},{28,20},{1,9},{5... | collective-permute-start | bytes 884744 | tf_op jit(solution)/shard_map/ppermute | solution.py:34
  82.2 6.3 %collective-permute-start.19 = (bf16[384,768]{1,0:T(8,128)(2,1)S(1)}, bf16[384,768]{1,0:T(8,128)(2,1)S(1)}, u32[]{:S(2)}, u32[]{:S(2)}) collective-permute-start(bf16[384,768]{1,0:T(8,128)(2,1)S(1)} %collective-permute-done.18), channel_id=1, source_target_pairs={{0,4},{4,0},{8,12},{12,8},{16,20},{20,16},{24,28},{28,24},{1,5},{5... | collective-permute-start | bytes 1769480 | tf_op jit(solution)/shard_map/ppermute | solution.py:34
  84.2 4.7 %collective-permute-start.17 = (bf16[384,768]{1,0:T(8,128)(2,1)S(1)}, bf16[384,768]{1,0:T(8,128)(2,1)S(1)}, u32[]{:S(2)}, u32[]{:S(2)}) collective-permute-start(bf16[384,768]{1,0:T(8,128)(2,1)S(1)} %collective-permute-done.16), channel_id=1, source_target_pairs={{0,4},{4,0},{8,12},{12,8},{16,20},{20,16},{24,28},{28,24},{1,5},{5... | collective-permute-start | bytes 1769480 | tf_op jit(solution)/shard_map/ppermute | solution.py:34
  86.8 2.5 %collective-permute-start.21 = (bf16[192,768]{1,0:T(8,128)(2,1)S(1)}, bf16[192,768]{1,0:T(8,128)(2,1)S(1)}, u32[]{:S(2)}, u32[]{:S(2)}) collective-permute-start(bf16[192,768]{1,0:T(8,128)(2,1)S(1)} %collective-permute-done.20), channel_id=1, source_target_pairs={{0,4},{4,0},{8,12},{12,8},{16,20},{20,16},{24,28},{28,24},{1,5},{5... | collective-permute-start | bytes 884744 | tf_op jit(solution)/shard_map/ppermute | solution.py:34
  87.9 1.6 %collective-permute-start.23 = (bf16[192,768]{1,0:T(8,128)(2,1)S(1)}, bf16[192,768]{1,0:T(8,128)(2,1)S(1)}, u32[]{:S(2)}, u32[]{:S(2)}) collective-permute-start(bf16[192,768]{1,0:T(8,128)(2,1)S(1)} %collective-permute-done.22), channel_id=1, source_target_pairs={{0,4},{4,0},{8,12},{12,8},{16,20},{20,16},{24,28},{28,24},{1,5},{5... | collective-permute-start | bytes 884744 | tf_op jit(solution)/shard_map/ppermute | solution.py:34

commit v5 on v4

--- a/solution.py
+++ b/solution.py
@@ -198,6 +198,38 @@
     )(scale.reshape(1, -1), *hidden, *cotangent)
 
 
+def finish_kernel(scale, hidden, upper, lower, before, out, held):
+    width, half = out.shape[0], upper.shape[0]
+    for i, block in enumerate((upper, lower)):
+        held[i * half : (i + 1) * half, :] = (
+            block[...].astype(jnp.float32) * scale[...]
+        ).astype(jnp.bfloat16)
+    tokens = 2 * half
+    total = before[...] + token_fold(hidden[:tokens, width:], held[...])
+    out[...] = total.astype(jnp.bfloat16)
+
+
+def finish_send(scale, hidden, corner, before):
+    width, model_width = before.shape
+    tokens = 2 * corner[0].shape[0]
+    return pl.pallas_call(
+        finish_kernel,
+        out_shape=[
+            jax.ShapeDtypeStruct((width, model_width), jnp.bfloat16),
+            jax.ShapeDtypeStruct((tokens, model_width), jnp.bfloat16),
+        ],
+        in_specs=[VMEM] * 5,
+        out_specs=[VMEM] * 2,
+        compiler_params=pltpu.CompilerParams(vmem_limit_bytes=24 * MIB),
+        cost_estimate=pl.CostEstimate(
+            flops=2 * tokens * width * model_width,
+            bytes_accessed=6 * width * model_width + 8 * tokens * model_width,
+            transcendentals=0,
+        ),
+        name="finish_send",
+    )(scale.reshape(1, -1), hidden, *corner, before)
+
+
 def split_kernel(place, keep, arrived, own, *outgoing):
     rows = own.shape[0]
     for j in range(len(outgoing) + 1):
@@ -225,9 +257,8 @@
     )(place, keep, arrived)
 
 
-def update_kernel(place, own, one, two, three, weight, first, second, teacher, *outs):
+def update_kernel(own, one, two, three, weight, first, second, teacher, *outs):
     new_weight, new_first, new_second, sent = outs
-    rows = own.shape[0]
     gradient = own[...] + one[...].astype(jnp.float32)
     gradient = gradient + two[...].astype(jnp.float32) + three[...].astype(jnp.float32)
     weight_new, first_new, second_new = adam_step(
@@ -236,24 +267,24 @@
     new_weight[...] = weight_new.astype(jnp.bfloat16)
     new_first[...] = first_new.astype(jnp.bfloat16)
     new_second[...] = second_new.astype(jnp.bfloat16)
-    held = teacher[pl.ds(pl.multiple_of(place[0] * rows, 32), rows), :].astype(jnp.float32)
+    held = teacher[...].astype(jnp.float32)
     sent[...] = (teacher_keep * held + (1.0 - teacher_keep) * weight_new).astype(jnp.bfloat16)
 
 
-def update_rows(place, own, arrived, weight, first, second, teacher):
+def update_rows(own, arrived, weight, first, second, teacher):
     rows, width = own.shape
     stored = jax.ShapeDtypeStruct((rows, width), jnp.bfloat16)
     return pl.pallas_call(
         update_kernel,
         out_shape=[stored] * 4,
-        in_specs=[SMEM] + [VMEM] * 8,
+        in_specs=[VMEM] * 8,
         out_specs=[VMEM] * 4,
         compiler_params=pltpu.CompilerParams(vmem_limit_bytes=24 * MIB),
         cost_estimate=pl.CostEstimate(
             flops=20 * own.size, bytes_accessed=30 * own.size, transcendentals=2 * own.size
         ),
         name="update_rows",
-    )(place, own, *arrived, weight, first, second, teacher)
+    )(own, *arrived, weight, first, second, teacher)
 
 
 def block_shards(
@@ -298,26 +329,20 @@
     for hidden in hidden_of[1:]:
         share = share + jnp.sum(hidden[tokens : tokens + 3].astype(jnp.float32), axis=0)
 
-    def scale_it(block):
-        scaled = (block.astype(jnp.float32) * layer_scale).astype(jnp.bfloat16)
-        return lax.optimization_barrier(scaled)
-
     keep, send = fold_tokens(layer_scale, hidden_of[:3], [out_cotangent, cot_x, cot_y], width)
-    scaled = scale_it(jnp.concatenate(corner, 0))
+    send, scaled = finish_send(layer_scale, hidden_of[3], corner, send)
     far = hidden_of[3][:tokens]
-    send = (send + token_fold(far[:, width:], scaled)).astype(jnp.bfloat16)
     keep = keep + token_fold(far[:, :width], scaled)
     share = share + swap_fsdp(share, 1)
     own, *outgoing = split_rows(place, keep, swap_fsdp(send, 1), own_rows, rep_count)
     arrived = [swap_rep(piece, j + 1) for j, piece in enumerate(outgoing)]
     new_weight, new_first, new_second, sent_rows = update_rows(
-        place,
         own,
         arrived,
         student_weight,
         first_moment,
         second_moment,
-        teacher_weight,
+        lax.dynamic_slice_in_dim(teacher_weight, my_rep * own_rows, own_rows, 0),
     )
 
     sent_rows, share = lax.optimization_barrier((sent_rows, share))

time: 91.3 us -> 88.4 us (0.968)
  matrix products: 5.98 us -> 3.83 us
  waiting for transfers between devices: 34.7 us -> 33.7 us
  other arithmetic: 6.55 us -> 5.58 us
  local copies, waits for them, and re-layouts: 2.28 us -> 3.2 us
    dot_general x2 -> x1, matrix products: 2.54 us -> 0.36 us  [token_fold(): lax.dot_general(arrived, portion, (((0,), (0,)), ((), ())), preferred_ele...]
    convert_element_type x2 -> x0, other arithmetic: 1.18 us -> none  [the longest x1 1.03 us: scale_it(): scaled = (block.astype(jnp.float32) * layer_scale).astype(jnp.bfloat16)]
    dynamic_slice x0 -> x1, local copies, waits for them, and re-layouts: none -> 0.92 us  [block_shards(): lax.dynamic_slice_in_dim(teacher_weight, my_rep * own_rows, own_rows, 0)]
where the time goes in v5:
time: 88.4 us; the launch traced here: 88.1 us
  waiting for transfers between devices  33.7 us (38%)
  starting transfers between devices  20.7 us (23%)
  blocking collectives  17.6 us (20%)
  other arithmetic  5.58 us (6%)
  matrix products  3.83 us (4%)
  local copies, waits for them, and re-layouts  3.2 us (4%)
  Pallas kernels  2.59 us (3%)
  between operations  1.01 us (1%)
    all_gather x1, blocking collectives, block_shards(): teacher_shard = lax.all_gather(sent_rows, 'rep', axis=0, tiled=True)  17.6 us
    ppermute x6, waiting for transfers between devices, swap_rep(): return lax.ppermute(value, 'rep', [(i, i ^ flip) for i in range(count)])  17.6 us
    ppermute x18, waiting for transfers between devices, swap_fsdp(): return lax.ppermute(value, 'fsdp', [(i, i ^ flip) for i in range(count)])  16.1 us
    ppermute x18, starting transfers between devices, swap_fsdp(): return lax.ppermute(value, 'fsdp', [(i, i ^ flip) for i in range(count)])  15.2 us
    ppermute x6, starting transfers between devices, swap_rep(): return lax.ppermute(value, 'rep', [(i, i ^ flip) for i in range(count)])  5.48 us
    dot_general x6, matrix products, terms(): term = jnp.dot(units, weights, preferred_element_type=jnp.float32)  2.17 us
    dynamic_slice x1, local copies, waits for them, and re-layouts, columns(): return lax.dynamic_slice_in_dim(array, (me ^ flip) * width, width, 1)  2.15 us
  transfers between devices with their start and end apart: 24, of which 12 were waited for; matrix products, arithmetic and copies ran while one was open for 13% of the time, Pallas kernels for 1%

profile of v5, /device:TPU:0, one launch (start us, length us, event | category | flops | bytes accessed | tf_op | source)
XLA Modules:
  0.0 88.1 jit_solution(5401530683773282558)
XLA Ops:
  0.6 0.0 copy-start
  0.7 3.0 %collective-permute-start.2 = (bf16[192,768]{1,0:T(8,128)(2,1)}, bf16[192,768]{1,0:T(8,128)(2,1)S(1)}, u32[]{:S(2)}, u32[]{:S(2)}) collective-permute-start(bf16[192,768]{1,0:T(8,128)(2,1)} %refs_3_.1), channel_id=1, source_target_pairs={{0,8},{4,12},{8,0},{12,4},{16,24},{20,28},{24,16},{28,20},{1,9},{5... | collective-permute-start | bytes 884744 | tf_op jit(solution)/shard_map/ppermute | solution.py:34
  3.7 1.5 %collective-permute-start.3 = (bf16[192,768]{1,0:T(8,128)(2,1)}, bf16[192,768]{1,0:T(8,128)(2,1)S(1)}, u32[]{:S(2)}, u32[]{:S(2)}) collective-permute-start(bf16[192,768]{1,0:T(8,128)(2,1)} %refs_3_.1), channel_id=1, source_target_pairs={{0,16},{4,20},{8,24},{12,28},{16,0},{20,4},{24,8},{28,12},{1,17},{... | collective-permute-start | bytes 884744 | tf_op jit(solution)/shard_map/ppermute | solution.py:34
  5.2 1.1 %multiply_reduce_fusion = f32[768]{0:T(1024)S(1)} fusion(bf16[192,768]{1,0:T(8,128)(2,1)} %param.15, bf16[192,768]{1,0:T(8,128)(2,1)} %refs_3_.1), kind=kLoop, calls=%fused_computation.13 | loop fusion | flops 589056 | bytes 592896 | tf_op jit(solution)/shard_map/reduce_sum | solution.py:318
  6.4 0.0 copy-start.7
  6.4 2.1 %constant_dynamic-slice_fusion.2 = (bf16[192,384]{1,0:T(8,128)(2,1)S(1)}, bf16[192,384]{1,0:T(8,128)(2,1)S(1)}, bf16[192,384]{1,0:T(8,128)(2,1)S(1)}, bf16[192,3...) fusion(bf16[192,3072]{1,0:T(8,128)(2,1)} %param.13, ...), kind=kLoop, calls=%fused_computation.58 | loop fusion | bytes 2359328 | tf_op jit(solution)/shard_map/dynamic_slice | solution.py:315
  8.6 1.0 %pad_maximum_fusion = (bf16[200,768]{1,0:T(8,128)(2,1)}, bf16[200,768]{1,0:T(8,128)(2,1)}, bf16[200,768]{1,0:T(8,128)(2,1)}) fusion(bf16[8,768]{1,0:T(8,128)(2,1)S(1)} %fusion.28, bf16[192,384]{1,0:T(8,128)(2,1)S(1)} %get-tuple-element.58, bf16[192,384]{1,0:T(8,128)(2,1)S(1)} %get-tuple-element.51, bf16[192,384]{1,0:T(8,128)(2,1)S(1)} %get-tuple-element.52, ...), kind=kLoop, calls=%fused_computation.15 | loop fusion | flops 2457600 | bytes 1818624 | tf_op jit(solution)/shard_map/concatenate | solution.py:326
  9.5 0.5 collective-permute-start
  10.1 0.1 collective-permute-start.1
  10.1 2.9 %collective-permute-start.4 = (bf16[200,768]{1,0:T(8,128)(2,1)}, bf16[200,768]{1,0:T(8,128)(2,1)S(1)}, u32[]{:S(2)}, u32[]{:S(2)}) collective-permute-start(bf16[200,768]{1,0:T(8,128)(2,1)} %get-tuple-element.59), channel_id=1, source_target_pairs={{0,24},{4,28},{8,16},{12,20},{16,8},{20,12},{24,0},{28,4},{1,25},{... | collective-permute-start | bytes 921608 | tf_op jit(solution)/shard_map/ppermute | solution.py:34
  13.0 0.0 collective-permute-done.2.refs_4_
  13.0 0.6 collective-permute-start.5
  13.6 1.8 %collective-permute-start.6 = (bf16[96,768]{1,0:T(8,128)(2,1)S(1)}, bf16[96,768]{1,0:T(8,128)(2,1)S(1)}, u32[]{:S(2)}, u32[]{:S(2)}) collective-permute-start(bf16[96,768]{1,0:T(8,128)(2,1)S(1)} %slice.52), channel_id=1, source_target_pairs={{0,8},{4,12},{8,0},{12,4},{16,24},{20,28},{24,16},{28,20},{1,9},{5... | collective-permute-start | bytes 442376 | tf_op jit(solution)/shard_map/ppermute | solution.py:34
  15.4 0.9 %pad_maximum_fusion.3.refs_0_ = bf16[192,768]{1,0:T(8,128)(2,1)S(1)} fusion(bf16[192,384]{1,0:T(8,128)(2,1)S(1)} %get-tuple-element.56, bf16[192,384]{1,0:T(8,128)(2,1)} %get-tuple-element.57), kind=kLoop, calls=%fused_computation.18 | loop fusion | flops 589824 | bytes 589824 | tf_op jit(solution)/shard_map/concatenate | solution.py:323
  16.4 3.6 %collective-permute-done.refs_1_ = bf16[200,768]{1,0:T(8,128)(2,1)S(1)} collective-permute-done((bf16[200,768]{1,0:T(8,128)(2,1)}, bf16[200,768]{1,0:T(8,128)(2,1)S(1)}, u32[]{:S(2)}, u32[]{:S(2)}) %collective-permute-start) | collective-permute-done | bytes 307232 | tf_op jit(solution)/shard_map/ppermute | solution.py:34
  20.0 7.1 %collective-permute-done.1.refs_2_ = bf16[200,768]{1,0:T(8,128)(2,1)S(1)} collective-permute-done((bf16[200,768]{1,0:T(8,128)(2,1)}, bf16[200,768]{1,0:T(8,128)(2,1)S(1)}, u32[]{:S(2)}, u32[]{:S(2)}) %collective-permute-start.1) | collective-permute-done | bytes 307232 | tf_op jit(solution)/shard_map/ppermute | solution.py:34
  27.1 1.1 %fold_tokens.1 = (f32[384,768]{1,0:T(8,128)S(1)}, f32[384,768]{1,0:T(8,128)S(1)}) custom-call(f32[1,768]{1,0:T(1,128)S(1)} %reshape.51.scale, bf16[192,768]{1,0:T(8,128)(2,1)S(1)} %pad_maximum_fusion.3.refs_0_, bf16[200,768]{1,0:T(8,128)(2,1)S(1)} %collective-permute-done.refs_1_, bf16[200,768]{1,0:T(8,128)(2,1)S(1)} %collective-permute-done.1.refs_2_, ...), custom_call_target="tpu_custom_call" | custom-call | flops 679477248 | bytes 2949120 | tf_op jit(solution)/shard_map/fold_tokens/pallas_call | solution.py:186
  28.2 0.4 collective-permute-done.5.upper
  28.7 0.4 finish_send.1
  29.0 0.1 collective-permute-start.7
  29.2 0.4 fusion.16
  29.6 0.2 add.116.keep
  29.7 0.0 copy-start.2
  29.7 0.0 copy-start.3
  29.7 0.0 copy-start.4
  29.7 1.4 %collective-permute-done.7.arrived = bf16[384,768]{1,0:T(8,128)(2,1)S(1)} collective-permute-done((bf16[384,768]{1,0:T(8,128)(2,1)S(1)}, bf16[384,768]{1,0:T(8,128)(2,1)S(1)}, u32[]{:S(2)}, u32[]{:S(2)}) %collective-permute-start.7) | collective-permute-done | bytes 589856 | tf_op jit(solution)/shard_map/ppermute | solution.py:34
  31.1 0.1 split_rows.1
  31.2 1.6 %collective-permute-start.8 = (bf16[96,768]{1,0:T(8,128)(2,1)S(1)}, bf16[96,768]{1,0:T(8,128)(2,1)S(1)}, u32[]{:S(2)}, u32[]{:S(2)}) collective-permute-start(bf16[96,768]{1,0:T(8,128)(2,1)S(1)} %get-tuple-element.33), channel_id=1, source_target_pairs={{0,1},{1,0},{2,3},{3,2},{4,5},{5,4},{6,7},{7,6},{8,9},{9,8},{10,11... | collective-permute-start | bytes 442376 | tf_op jit(solution)/shard_map/ppermute | solution.py:39
  32.9 2.6 %collective-permute-start.9 = (bf16[96,768]{1,0:T(8,128)(2,1)S(1)}, bf16[96,768]{1,0:T(8,128)(2,1)S(1)}, u32[]{:S(2)}, u32[]{:S(2)}) collective-permute-start(bf16[96,768]{1,0:T(8,128)(2,1)S(1)} %get-tuple-element.34), channel_id=1, source_target_pairs={{0,2},{1,3},{2,0},{3,1},{4,6},{5,7},{6,4},{7,5},{8,10},{9,11},{10,... | collective-permute-start | bytes 442376 | tf_op jit(solution)/shard_map/ppermute | solution.py:39
  35.5 0.2 collective-permute-start.10
  35.7 0.9 %constant_dynamic-slice_fusion.teacher = bf16[96,768]{1,0:T(8,128)(2,1)S(1)} fusion(bf16[384,768]{1,0:T(8,128)(2,1)} %param.22, s32[]{:T(128)S(6)} %select_n.53), kind=kLoop, calls=%fused_computation.56 | loop fusion | bytes 294916 | tf_op jit(solution)/shard_map/dynamic_slice | solution.py:345
  36.6 0.2 collective-permute-done.11
  36.8 2.7 %collective-permute-done.8.one = bf16[96,768]{1,0:T(8,128)(2,1)S(1)} collective-permute-done((bf16[96,768]{1,0:T(8,128)(2,1)S(1)}, bf16[96,768]{1,0:T(8,128)(2,1)S(1)}, u32[]{:S(2)}, u32[]{:S(2)}) %collective-permute-start.8) | collective-permute-done | bytes 147488 | tf_op jit(solution)/shard_map/ppermute | solution.py:39
  39.6 7.2 %collective-permute-done.9.two = bf16[96,768]{1,0:T(8,128)(2,1)S(1)} collective-permute-done((bf16[96,768]{1,0:T(8,128)(2,1)S(1)}, bf16[96,768]{1,0:T(8,128)(2,1)S(1)}, u32[]{:S(2)}, u32[]{:S(2)}) %collective-permute-start.9) | collective-permute-done | bytes 147488 | tf_op jit(solution)/shard_map/ppermute | solution.py:39
  46.8 0.0 copy-start.8
  46.8 0.0 copy-start.9
  46.9 0.0 copy-start.10
  46.9 1.0 %update_rows.1 = (bf16[96,768]{1,0:T(8,128)(2,1)}, bf16[96,768]{1,0:T(8,128)(2,1)}, bf16[96,768]{1,0:T(8,128)(2,1)}, bf16[96,768]{1,0:T(8,128)(2,1)S(1)}) custom-call(f32[96,768]{1,0:T(8,128)S(1)} %get-tuple-element.32.own, bf16[96,768]{1,0:T(8,128)(2,1)S(1)} %collective-permute-done.8.one, bf16[96,768]{1,0:T(8,128)(2,1)S(1)} %collective-permute-done.9.two, ...), custom_call_target="tpu_custom_call" | custom-call | flops 1474560 | bytes 2211840 | tf_op jit(solution)/shard_map/update_rows/pallas_call | solution.py:277
  47.9 17.6 %all_gather.3 = bf16[384,768]{1,0:T(8,128)(2,1)S(1)} all-gather(bf16[96,768]{1,0:T(8,128)(2,1)S(1)} %get-tuple-element.41), channel_id=1, replica_groups=mesh['fsdp'=8,'rep'=4] {'rep'}, dimensions={0}, use_global_device_ids=true | all-gather | bytes 737280 | tf_op jit(solution)/shard_map/all_gather | solution.py:349
  65.5 1.0 %collective-permute-start.16 = (bf16[384,768]{1,0:T(8,128)(2,1)S(1)}, bf16[384,768]{1,0:T(8,128)(2,1)S(1)}, u32[]{:S(2)}, u32[]{:S(2)}) collective-permute-start(bf16[384,768]{1,0:T(8,128)(2,1)S(1)} %all_gather.3), channel_id=1, source_target_pairs={{0,8},{4,12},{8,0},{12,4},{16,24},{20,28},{24,16},{28,20},{1,9},{5... | collective-permute-start | bytes 1769480 | tf_op jit(solution)/shard_map/ppermute | solution.py:34
  66.5 1.1 %collective-permute-start.18 = (bf16[384,768]{1,0:T(8,128)(2,1)S(1)}, bf16[384,768]{1,0:T(8,128)(2,1)S(1)}, u32[]{:S(2)}, u32[]{:S(2)}) collective-permute-start(bf16[384,768]{1,0:T(8,128)(2,1)S(1)} %all_gather.3), channel_id=1, source_target_pairs={{0,16},{4,20},{8,24},{12,28},{16,0},{20,4},{24,8},{28,12},{1,17},{... | collective-permute-start | bytes 1769480 | tf_op jit(solution)/shard_map/ppermute | solution.py:34
  67.5 1.0 %collective-permute-start.14 = (f32[768]{0:T(1024)S(1)}, f32[768]{0:T(1024)S(1)}, u32[]{:S(2)}, u32[]{:S(2)}) collective-permute-start(f32[768]{0:T(1024)S(1)} %add.121), channel_id=1, source_target_pairs={{0,3},{1,2},{2,1},{3,0},{4,7},{5,6},{6,5},{7,4},{8,11},{9,10},{10,... | collective-permute-start | bytes 9224 | tf_op jit(solution)/shard_map/ppermute | solution.py:39
  68.6 4.4 %collective-permute-done.14 = f32[768]{0:T(1024)S(1)} collective-permute-done((f32[768]{0:T(1024)S(1)}, f32[768]{0:T(1024)S(1)}, u32[]{:S(2)}, u32[]{:S(2)}) %collective-permute-start.14) | collective-permute-done | bytes 3104 | tf_op jit(solution)/shard_map/ppermute | solution.py:39
  73.0 0.4 fusion.14
  73.3 0.0 copy-start.5
  73.3 3.2 %collective-permute-done.12 = f32[768]{0:T(1024)S(1)} collective-permute-done((f32[768]{0:T(1024)S(1)}, f32[768]{0:T(1024)S(1)}, u32[]{:S(2)}, u32[]{:S(2)}) %collective-permute-start.12) | collective-permute-done | bytes 3104 | tf_op jit(solution)/shard_map/ppermute | solution.py:39
  76.6 0.6 multiply_add_fusion
  77.2 1.0 %collective-permute-start.20 = (bf16[192,768]{1,0:T(8,128)(2,1)S(1)}, bf16[192,768]{1,0:T(8,128)(2,1)S(1)}, u32[]{:S(2)}, u32[]{:S(2)}) collective-permute-start(bf16[192,768]{1,0:T(8,128)(2,1)S(1)} %slice.56), channel_id=1, source_target_pairs={{0,16},{4,20},{8,24},{12,28},{16,0},{20,4},{24,8},{28,12},{1,17},{... | collective-permute-start | bytes 884744 | tf_op jit(solution)/shard_map/ppermute | solution.py:34
  78.3 1.1 %collective-permute-start.22 = (bf16[192,768]{1,0:T(8,128)(2,1)S(1)}, bf16[192,768]{1,0:T(8,128)(2,1)S(1)}, u32[]{:S(2)}, u32[]{:S(2)}) collective-permute-start(bf16[192,768]{1,0:T(8,128)(2,1)S(1)} %slice.57), channel_id=1, source_target_pairs={{0,8},{4,12},{8,0},{12,4},{16,24},{20,28},{24,16},{28,20},{1,9},{5... | collective-permute-start | bytes 884744 | tf_op jit(solution)/shard_map/ppermute | solution.py:34
  79.4 0.4 fusion.8
  79.7 0.4 fusion.1
  80.1 0.4 fusion.11
  80.5 0.9 broadcast_select_fusion
  81.3 0.5 collective-permute-start.17
  81.9 2.2 %collective-permute-done.20 = bf16[192,768]{1,0:T(8,128)(2,1)S(1)} collective-permute-done((bf16[192,768]{1,0:T(8,128)(2,1)S(1)}, bf16[192,768]{1,0:T(8,128)(2,1)S(1)}, u32[]{:S(2)}, u32[]{:S(2)}) %collective-permute-start.20) | collective-permute-done | bytes 294944 | tf_op jit(solution)/shard_map/ppermute | solution.py:34
  84.0 1.0 %collective-permute-done.22 = bf16[192,768]{1,0:T(8,128)(2,1)S(1)} collective-permute-done((bf16[192,768]{1,0:T(8,128)(2,1)S(1)}, bf16[192,768]{1,0:T(8,128)(2,1)S(1)}, u32[]{:S(2)}, u32[]{:S(2)}) %collective-permute-start.22) | collective-permute-done | bytes 294944 | tf_op jit(solution)/shard_map/ppermute | solution.py:34
  85.1 0.3 fusion.21
  85.4 0.3 convolution_add_fusion.4
  85.7 0.4 convolution_add_fusion
  86.1 0.4 fusion.4
  86.5 0.2 collective-permute-done.23
  86.6 0.3 fusion.18
  87.0 0.3 fusion.6
  87.3 0.8 add_convert_fusion
  (43 shorter events, 0.2 us)
Async XLA Ops:
  0.6 72.3 %copy-start = (bf16[256,3072]{1,0:T(8,128)(2,1)S(1)}, bf16[256,3072]{1,0:T(8,128)(2,1)}, u32[]{:S(2)}) copy-start(bf16[256,3072]{1,0:T(8,128)(2,1)} %param.24) | copy-start | bytes 4718596
  0.7 12.4 %collective-permute-start.2 = (bf16[192,768]{1,0:T(8,128)(2,1)}, bf16[192,768]{1,0:T(8,128)(2,1)S(1)}, u32[]{:S(2)}, u32[]{:S(2)}) collective-permute-start(bf16[192,768]{1,0:T(8,128)(2,1)} %refs_3_.1), channel_id=1, source_target_pairs={{0,8},{4,12},{8,0},{12,4},{16,24},{20,28},{24,16},{28,20},{1,9},{5... | collective-permute-start | bytes 884744 | tf_op jit(solution)/shard_map/ppermute | solution.py:34
  3.7 10.0 %collective-permute-start.3 = (bf16[192,768]{1,0:T(8,128)(2,1)}, bf16[192,768]{1,0:T(8,128)(2,1)S(1)}, u32[]{:S(2)}, u32[]{:S(2)}) collective-permute-start(bf16[192,768]{1,0:T(8,128)(2,1)} %refs_3_.1), channel_id=1, source_target_pairs={{0,16},{4,20},{8,24},{12,28},{16,0},{20,4},{24,8},{28,12},{1,17},{... | collective-permute-start | bytes 884744 | tf_op jit(solution)/shard_map/ppermute | solution.py:34
  6.4 6.6 %copy-start.7 = (f32[768]{0:T(1024)S(1)}, f32[768]{0:T(1024)}, u32[]{:S(2)}) copy-start(f32[768]{0:T(1024)} %param.16) | copy-start | bytes 9220
  8.6 18.5 %copy-start.1 = (bf16[192,768]{1,0:T(8,128)(2,1)S(1)}, bf16[192,768]{1,0:T(8,128)(2,1)}, u32[]{:S(2)}) copy-start(bf16[192,768]{1,0:T(8,128)(2,1)} %refs_3_.1) | copy-start | bytes 884740
  9.5 10.4 %collective-permute-start = (bf16[200,768]{1,0:T(8,128)(2,1)}, bf16[200,768]{1,0:T(8,128)(2,1)S(1)}, u32[]{:S(2)}, u32[]{:S(2)}) collective-permute-start(bf16[200,768]{1,0:T(8,128)(2,1)} %get-tuple-element.61), channel_id=1, source_target_pairs={{0,8},{4,12},{8,0},{12,4},{16,24},{20,28},{24,16},{28,20},{1,9},{5... | collective-permute-start | bytes 921608 | tf_op jit(solution)/shard_map/ppermute | solution.py:34
  10.1 17.0 %collective-permute-start.1 = (bf16[200,768]{1,0:T(8,128)(2,1)}, bf16[200,768]{1,0:T(8,128)(2,1)S(1)}, u32[]{:S(2)}, u32[]{:S(2)}) collective-permute-start(bf16[200,768]{1,0:T(8,128)(2,1)} %get-tuple-element.60), channel_id=1, source_target_pairs={{0,16},{4,20},{8,24},{12,28},{16,0},{20,4},{24,8},{28,12},{1,17},{... | collective-permute-start | bytes 921608 | tf_op jit(solution)/shard_map/ppermute | solution.py:34
  10.1 18.1 %collective-permute-start.4 = (bf16[200,768]{1,0:T(8,128)(2,1)}, bf16[200,768]{1,0:T(8,128)(2,1)S(1)}, u32[]{:S(2)}, u32[]{:S(2)}) collective-permute-start(bf16[200,768]{1,0:T(8,128)(2,1)} %get-tuple-element.59), channel_id=1, source_target_pairs={{0,24},{4,28},{8,16},{12,20},{16,8},{20,12},{24,0},{28,4},{1,25},{... | collective-permute-start | bytes 921608 | tf_op jit(solution)/shard_map/ppermute | solution.py:34
  13.0 15.6 %collective-permute-start.5 = (bf16[96,768]{1,0:T(8,128)(2,1)S(1)}, bf16[96,768]{1,0:T(8,128)(2,1)S(1)}, u32[]{:S(2)}, u32[]{:S(2)}) collective-permute-start(bf16[96,768]{1,0:T(8,128)(2,1)S(1)} %slice.51), channel_id=1, source_target_pairs={{0,16},{4,20},{8,24},{12,28},{16,0},{20,4},{24,8},{28,12},{1,17},{... | collective-permute-start | bytes 442376 | tf_op jit(solution)/shard_map/ppermute | solution.py:34
  13.6 15.0 %collective-permute-start.6 = (bf16[96,768]{1,0:T(8,128)(2,1)S(1)}, bf16[96,768]{1,0:T(8,128)(2,1)S(1)}, u32[]{:S(2)}, u32[]{:S(2)}) collective-permute-start(bf16[96,768]{1,0:T(8,128)(2,1)S(1)} %slice.52), channel_id=1, source_target_pairs={{0,8},{4,12},{8,0},{12,4},{16,24},{20,28},{24,16},{28,20},{1,9},{5... | collective-permute-start | bytes 442376 | tf_op jit(solution)/shard_map/ppermute | solution.py:34
  29.0 2.1 %collective-permute-start.7 = (bf16[384,768]{1,0:T(8,128)(2,1)S(1)}, bf16[384,768]{1,0:T(8,128)(2,1)S(1)}, u32[]{:S(2)}, u32[]{:S(2)}) collective-permute-start(bf16[384,768]{1,0:T(8,128)(2,1)S(1)} %get-tuple-element.31), channel_id=1, source_target_pairs={{0,4},{4,0},{8,12},{12,8},{16,20},{20,16},{24,28},{28,24},{1,5},{5... | collective-permute-start | bytes 1769480 | tf_op jit(solution)/shard_map/ppermute | solution.py:34
  29.7 17.1 %copy-start.2 = (bf16[96,768]{1,0:T(8,128)(2,1)S(1)}, bf16[96,768]{1,0:T(8,128)(2,1)}, u32[]{:S(2)}) copy-start(bf16[96,768]{1,0:T(8,128)(2,1)} %weight.1) | copy-start | bytes 442372
  29.7 17.1 %copy-start.3 = (bf16[96,768]{1,0:T(8,128)(2,1)S(1)}, bf16[96,768]{1,0:T(8,128)(2,1)}, u32[]{:S(2)}) copy-start(bf16[96,768]{1,0:T(8,128)(2,1)} %first.1) | copy-start | bytes 442372
  29.7 17.1 %copy-start.4 = (bf16[96,768]{1,0:T(8,128)(2,1)S(1)}, bf16[96,768]{1,0:T(8,128)(2,1)}, u32[]{:S(2)}) copy-start(bf16[96,768]{1,0:T(8,128)(2,1)} %second.1) | copy-start | bytes 442372
  31.2 8.4 %collective-permute-start.8 = (bf16[96,768]{1,0:T(8,128)(2,1)S(1)}, bf16[96,768]{1,0:T(8,128)(2,1)S(1)}, u32[]{:S(2)}, u32[]{:S(2)}) collective-permute-start(bf16[96,768]{1,0:T(8,128)(2,1)S(1)} %get-tuple-element.33), channel_id=1, source_target_pairs={{0,1},{1,0},{2,3},{3,2},{4,5},{5,4},{6,7},{7,6},{8,9},{9,8},{10,11... | collective-permute-start | bytes 442376 | tf_op jit(solution)/shard_map/ppermute | solution.py:39
  32.9 13.9 %collective-permute-start.9 = (bf16[96,768]{1,0:T(8,128)(2,1)S(1)}, bf16[96,768]{1,0:T(8,128)(2,1)S(1)}, u32[]{:S(2)}, u32[]{:S(2)}) collective-permute-start(bf16[96,768]{1,0:T(8,128)(2,1)S(1)} %get-tuple-element.34), channel_id=1, source_target_pairs={{0,2},{1,3},{2,0},{3,1},{4,6},{5,7},{6,4},{7,5},{8,10},{9,11},{10,... | collective-permute-start | bytes 442376 | tf_op jit(solution)/shard_map/ppermute | solution.py:39
  35.5 11.4 %collective-permute-start.10 = (bf16[96,768]{1,0:T(8,128)(2,1)S(1)}, bf16[96,768]{1,0:T(8,128)(2,1)S(1)}, u32[]{:S(2)}, u32[]{:S(2)}) collective-permute-start(bf16[96,768]{1,0:T(8,128)(2,1)S(1)} %get-tuple-element.35), channel_id=1, source_target_pairs={{0,3},{1,2},{2,1},{3,0},{4,7},{5,6},{6,5},{7,4},{8,11},{9,10},{10,... | collective-permute-start | bytes 442376 | tf_op jit(solution)/shard_map/ppermute | solution.py:39
  35.7 1.2 %collective-permute-start.11 = (f32[768]{0:T(1024)S(1)}, f32[768]{0:T(1024)S(1)}, u32[]{:S(2)}, u32[]{:S(2)}) collective-permute-start(f32[768]{0:T(1024)S(1)} %add_add_fusion.1), channel_id=1, source_target_pairs={{0,4},{4,0},{8,12},{12,8},{16,20},{20,16},{24,28},{28,24},{1,5},{5... | collective-permute-start | bytes 9224 | tf_op jit(solution)/shard_map/ppermute | solution.py:34
  46.8 29.7 %copy-start.8 = (f32[768]{0:T(1024)S(1)}, f32[768]{0:T(1024)}, u32[]{:S(2)}) copy-start(f32[768]{0:T(1024)} %param.23) | copy-start | bytes 9220
  46.8 29.7 %copy-start.9 = (f32[768]{0:T(1024)S(1)}, f32[768]{0:T(1024)}, u32[]{:S(2)}) copy-start(f32[768]{0:T(1024)} %param.17) | copy-start | bytes 9220
  46.9 29.7 %copy-start.10 = (f32[768]{0:T(1024)S(1)}, f32[768]{0:T(1024)}, u32[]{:S(2)}) copy-start(f32[768]{0:T(1024)} %param.18) | copy-start | bytes 9220
  65.5 11.7 %collective-permute-start.16 = (bf16[384,768]{1,0:T(8,128)(2,1)S(1)}, bf16[384,768]{1,0:T(8,128)(2,1)S(1)}, u32[]{:S(2)}, u32[]{:S(2)}) collective-permute-start(bf16[384,768]{1,0:T(8,128)(2,1)S(1)} %all_gather.3), channel_id=1, source_target_pairs={{0,8},{4,12},{8,0},{12,4},{16,24},{20,28},{24,16},{28,20},{1,9},{5... | collective-permute-start | bytes 1769480 | tf_op jit(solution)/shard_map/ppermute | solution.py:34
  66.5 11.8 %collective-permute-start.18 = (bf16[384,768]{1,0:T(8,128)(2,1)S(1)}, bf16[384,768]{1,0:T(8,128)(2,1)S(1)}, u32[]{:S(2)}, u32[]{:S(2)}) collective-permute-start(bf16[384,768]{1,0:T(8,128)(2,1)S(1)} %all_gather.3), channel_id=1, source_target_pairs={{0,16},{4,20},{8,24},{12,28},{16,0},{20,4},{24,8},{28,12},{1,17},{... | collective-permute-start | bytes 1769480 | tf_op jit(solution)/shard_map/ppermute | solution.py:34
  67.5 5.4 %collective-permute-start.14 = (f32[768]{0:T(1024)S(1)}, f32[768]{0:T(1024)S(1)}, u32[]{:S(2)}, u32[]{:S(2)}) collective-permute-start(f32[768]{0:T(1024)S(1)} %add.121), channel_id=1, source_target_pairs={{0,3},{1,2},{2,1},{3,0},{4,7},{5,6},{6,5},{7,4},{8,11},{9,10},{10,... | collective-permute-start | bytes 9224 | tf_op jit(solution)/shard_map/ppermute | solution.py:39
  68.6 11.2 %collective-permute-start.15 = (bf16[384,768]{1,0:T(8,128)(2,1)S(1)}, bf16[384,768]{1,0:T(8,128)(2,1)S(1)}, u32[]{:S(2)}, u32[]{:S(2)}) collective-permute-start(bf16[384,768]{1,0:T(8,128)(2,1)S(1)} %all_gather.3), channel_id=1, source_target_pairs={{0,4},{4,0},{8,12},{12,8},{16,20},{20,16},{24,28},{28,24},{1,5},{5... | collective-permute-start | bytes 1769480 | tf_op jit(solution)/shard_map/ppermute | solution.py:34
  68.6 4.8 %collective-permute-start.13 = (f32[768]{0:T(1024)S(1)}, f32[768]{0:T(1024)S(1)}, u32[]{:S(2)}, u32[]{:S(2)}) collective-permute-start(f32[768]{0:T(1024)S(1)} %add.121), channel_id=1, source_target_pairs={{0,2},{1,3},{2,0},{3,1},{4,6},{5,7},{6,4},{7,5},{8,10},{9,11},{10,... | collective-permute-start | bytes 9224 | tf_op jit(solution)/shard_map/ppermute | solution.py:39
  73.0 3.6 %collective-permute-start.12 = (f32[768]{0:T(1024)S(1)}, f32[768]{0:T(1024)S(1)}, u32[]{:S(2)}, u32[]{:S(2)}) collective-permute-start(f32[768]{0:T(1024)S(1)} %add.121), channel_id=1, source_target_pairs={{0,1},{1,0},{2,3},{3,2},{4,5},{5,4},{6,7},{7,6},{8,9},{9,8},{10,11... | collective-permute-start | bytes 9224 | tf_op jit(solution)/shard_map/ppermute | solution.py:39
  73.3 6.4 %copy-start.5 = (bf16[256,768]{1,0:T(8,128)(2,1)S(1)}, bf16[256,768]{1,0:T(8,128)(2,1)}, u32[]{:S(2)}) copy-start(bf16[256,768]{1,0:T(8,128)(2,1)} %param.25) | copy-start | bytes 1179652
  77.2 9.8 %copy-start.6 = (f32[768]{0:T(1024)}, f32[768]{0:T(1024)S(1)}, u32[]{:S(2)}) copy-start(f32[768]{0:T(1024)S(1)} %get-tuple-element.47) | copy-start | bytes 9220
  77.2 6.8 %collective-permute-start.20 = (bf16[192,768]{1,0:T(8,128)(2,1)S(1)}, bf16[192,768]{1,0:T(8,128)(2,1)S(1)}, u32[]{:S(2)}, u32[]{:S(2)}) collective-permute-start(bf16[192,768]{1,0:T(8,128)(2,1)S(1)} %slice.56), channel_id=1, source_target_pairs={{0,16},{4,20},{8,24},{12,28},{16,0},{20,4},{24,8},{28,12},{1,17},{... | collective-permute-start | bytes 884744 | tf_op jit(solution)/shard_map/ppermute | solution.py:34
  78.3 6.8 %collective-permute-start.22 = (bf16[192,768]{1,0:T(8,128)(2,1)S(1)}, bf16[192,768]{1,0:T(8,128)(2,1)S(1)}, u32[]{:S(2)}, u32[]{:S(2)}) collective-permute-start(bf16[192,768]{1,0:T(8,128)(2,1)S(1)} %slice.57), channel_id=1, source_target_pairs={{0,8},{4,12},{8,0},{12,4},{16,24},{20,28},{24,16},{28,20},{1,9},{5... | collective-permute-start | bytes 884744 | tf_op jit(solution)/shard_map/ppermute | solution.py:34
  79.4 6.4 %collective-permute-start.19 = (bf16[384,768]{1,0:T(8,128)(2,1)S(1)}, bf16[384,768]{1,0:T(8,128)(2,1)S(1)}, u32[]{:S(2)}, u32[]{:S(2)}) collective-permute-start(bf16[384,768]{1,0:T(8,128)(2,1)S(1)} %collective-permute-done.18), channel_id=1, source_target_pairs={{0,4},{4,0},{8,12},{12,8},{16,20},{20,16},{24,28},{28,24},{1,5},{5... | collective-permute-start | bytes 1769480 | tf_op jit(solution)/shard_map/ppermute | solution.py:34
  81.3 4.8 %collective-permute-start.17 = (bf16[384,768]{1,0:T(8,128)(2,1)S(1)}, bf16[384,768]{1,0:T(8,128)(2,1)S(1)}, u32[]{:S(2)}, u32[]{:S(2)}) collective-permute-start(bf16[384,768]{1,0:T(8,128)(2,1)S(1)} %collective-permute-done.16), channel_id=1, source_target_pairs={{0,4},{4,0},{8,12},{12,8},{16,20},{20,16},{24,28},{28,24},{1,5},{5... | collective-permute-start | bytes 1769480 | tf_op jit(solution)/shard_map/ppermute | solution.py:34
  84.0 2.5 %collective-permute-start.21 = (bf16[192,768]{1,0:T(8,128)(2,1)S(1)}, bf16[192,768]{1,0:T(8,128)(2,1)S(1)}, u32[]{:S(2)}, u32[]{:S(2)}) collective-permute-start(bf16[192,768]{1,0:T(8,128)(2,1)S(1)} %collective-permute-done.20), channel_id=1, source_target_pairs={{0,4},{4,0},{8,12},{12,8},{16,20},{20,16},{24,28},{28,24},{1,5},{5... | collective-permute-start | bytes 884744 | tf_op jit(solution)/shard_map/ppermute | solution.py:34
  85.1 1.6 %collective-permute-start.23 = (bf16[192,768]{1,0:T(8,128)(2,1)S(1)}, bf16[192,768]{1,0:T(8,128)(2,1)S(1)}, u32[]{:S(2)}, u32[]{:S(2)}) collective-permute-start(bf16[192,768]{1,0:T(8,128)(2,1)S(1)} %collective-permute-done.22), channel_id=1, source_target_pairs={{0,4},{4,0},{8,12},{12,8},{16,20},{20,16},{24,28},{28,24},{1,5},{5... | collective-permute-start | bytes 884744 | tf_op jit(solution)/shard_map/ppermute | solution.py:34
